TPU v7x, 32 devices: a whole 2x2x4 slice. The times are simulated.
32 devices in a mesh: dp: 16 (over z, y, x), fsdp: 2 (over core).
Axes of the slice: x: 2, y: 2, z: 4, core: 2. Of those that a mesh axis runs over, the one named last changes fastest.
Arguments:
- teacher_feat: bfloat16 [1024, 256], P(('dp', 'fsdp')), may hold values from -1 to 1
- student_feat: bfloat16 [1024, 256], P(('dp', 'fsdp')), may hold values from -1 to 1
- crop_weight: bfloat16 [1024], P(('dp', 'fsdp')), may hold values from -96 to 96
- teacher_v: bfloat16 [256, 32768], P(None, 'fsdp'), may hold values from -2 to 2
- student_v: bfloat16 [256, 32768], P(None, 'fsdp'), may hold values from -2 to 2
Outputs:
- grad_v: float32 [256, 32768], P('dp', 'fsdp')
- grad_feat: float32 [1024, 256], P(('dp', 'fsdp'))
All inputs are finite; a program needn't handle non-finite values.
Results may differ from a plain program's by a relative error of at most 0.0073.
Values may be sent and summed in bfloat16 or wider, within the bound.
No kernel may reach another device: no remote copies, remote signals or barrier semaphores. Data moves between devices by JAX's collectives and lax.ppermute only.
A program may use at most 128 MiB of HBM per device.

v0:
```python
import functools
import math

import jax
import jax.numpy as jnp
from jax import lax
from jax.experimental import pallas as pl
from jax.experimental.pallas import tpu as pltpu
from jax.sharding import Mesh
from jax.sharding import PartitionSpec as P

ITERS = 3

teacher_temp = 0.04
student_temp = 0.1
epsilon = 1e-06

GROUPS = 2
TILE = 256
FETCH = 2
LANES = 128
VMEM_BYTES = 12 << 20
KEPT_BYTES = 18 << 20

EVERY = ("dp", "fsdp")
CHIPS = ("group", "block")
GROUP = ("block", "fsdp")


def unit_rows(values):
    floats = values.astype(jnp.float32)
    length = jnp.sqrt(jnp.sum(floats * floats, axis=1, keepdims=True) + epsilon)
    return (floats / length, length)


def unit_columns(values):
    floats = values.astype(jnp.float32)
    length = jnp.sqrt(jnp.sum(floats * floats, axis=0, keepdims=True) + epsilon)
    return (floats / length, length)


COPY_BYTES = 1 << 22


def share(values, axes):
    count = lax.axis_size(axes)
    if count * values.size * values.dtype.itemsize > COPY_BYTES:
        return lax.all_gather(values, axes)
    return lax.all_to_all(jnp.broadcast_to(values, (count, *values.shape)), axes, 0, 0)


def add_up(values):
    if lax.axis_size(EVERY) * values.size * values.dtype.itemsize > COPY_BYTES:
        return lax.psum(values, EVERY)
    return jnp.sum(share(values, EVERY), axis=0)


def plain_body(teacher_feat, student_feat, crop_weight, teacher_v, student_v):
    fsdp = lax.axis_size("fsdp")
    devices = lax.axis_size("dp") * fsdp
    own_rows, width = teacher_feat.shape
    crops = own_rows * devices
    block = teacher_v.shape[1] // lax.axis_size("dp")
    prototypes = block * devices
    first = lax.axis_index("dp") * block

    teacher_hat, _ = unit_rows(teacher_feat)
    student_hat, student_len = unit_rows(student_feat)
    units = jnp.concatenate(
        [teacher_hat.astype(jnp.bfloat16), student_hat.astype(jnp.bfloat16)], axis=1
    )
    units = share(share(units, "dp"), "fsdp").reshape(crops, 2 * width)
    teacher_unit, student_unit = units[:, :width], units[:, width:]

    teacher_w, _ = unit_columns(lax.dynamic_slice_in_dim(teacher_v, first, block, 1))
    student_w, student_wlen = unit_columns(lax.dynamic_slice_in_dim(student_v, first, block, 1))
    student_wunit = student_w.astype(jnp.bfloat16)

    mass = jnp.exp(
        jnp.dot(teacher_unit, teacher_w.astype(jnp.bfloat16), preferred_element_type=jnp.float32)
        / teacher_temp
    )
    student_mass = jnp.exp(
        jnp.dot(student_unit, student_wunit, preferred_element_type=jnp.float32) / student_temp
    )
    student_part = jnp.sum(student_mass, axis=1)

    crop_scale = None
    for sweep in range(ITERS):
        scaled = mass if sweep == 0 else mass * crop_scale[:, None]
        proto_scale = 1.0 / (prototypes * jnp.sum(scaled, axis=0))
        crop_part = jnp.sum(mass * proto_scale[None, :], axis=1)
        if sweep == 0:
            placed = jnp.zeros((fsdp, crops // (fsdp * own_rows), own_rows), jnp.float32)
            own = crop_weight.astype(jnp.float32)[None, None]
            spot = (lax.axis_index("fsdp"), lax.axis_index("dp"), 0)
            placed = lax.dynamic_update_slice(placed, own, spot).reshape(crops)
            sums = add_up(jnp.stack([crop_part, student_part, placed]))
            crop_mass, student_total, weights = sums[0], sums[1], sums[2]
        else:
            crop_mass = add_up(crop_part)
        crop_scale = 1.0 / (crops * crop_mass)

    target = crops * (mass * crop_scale[:, None] * proto_scale[None, :])
    student_prob = student_mass / student_total[:, None]
    gradient = ((student_prob - target) * weights[:, None] / student_temp).astype(jnp.bfloat16)
    feature_part = lax.dot_general(
        gradient, student_wunit, (((1,), (1,)), ((), ())), preferred_element_type=jnp.float32
    )
    weight_grad = lax.dot_general(
        student_unit, gradient, (((0,), (0,)), ((), ())), preferred_element_type=jnp.float32
    )
    weight_dot = jnp.sum(student_w * weight_grad, axis=0, keepdims=True)
    grad_block = (weight_grad - student_w * weight_dot) / student_wlen

    feature_sent = feature_part.astype(jnp.bfloat16).reshape(fsdp, -1, own_rows, width)
    feature_sent = jnp.swapaxes(feature_sent, 0, 1).reshape(devices, own_rows, width)
    feature_all = lax.all_to_all(feature_sent, EVERY, 0, 0)
    feature_grad = jnp.sum(feature_all.astype(jnp.float32), axis=0)
    grad_feat = (
        feature_grad - student_hat * jnp.sum(student_hat * feature_grad, axis=1, keepdims=True)
    ) / student_len
    grad_v = lax.all_to_all(grad_block.astype(jnp.bfloat16), "dp", 0, 1, tiled=True)
    return (grad_v.astype(jnp.float32), grad_feat)


def call(kernel, out_shape, flops=0, moved=0, exps=0, **more):
    return pl.pallas_call(
        kernel,
        out_shape=out_shape,
        compiler_params=pltpu.CompilerParams(vmem_limit_bytes=VMEM_BYTES),
        cost_estimate=pl.CostEstimate(flops=flops, bytes_accessed=moved, transcendentals=exps),
        **more,
    )


def units_kernel(teacher_ref, student_ref, sent_ref, teacher_vmem, student_vmem, sems):
    copies = [
        pltpu.make_async_copy(teacher_ref, teacher_vmem, sems.at[0]),
        pltpu.make_async_copy(student_ref, student_vmem, sems.at[1]),
    ]
    for copy in copies:
        copy.start()
    for copy in copies:
        copy.wait()
    width = teacher_vmem.shape[1]
    teacher = unit_rows(teacher_vmem[...])[0].astype(jnp.bfloat16)
    student = unit_rows(student_vmem[...])[0].astype(jnp.bfloat16)
    for chip in range(sent_ref.shape[0]):
        sent_ref[chip, :, :width] = teacher
        sent_ref[chip, :, width:] = student


def directions_kernel(block_ref, teacher_ref, student_ref, teacher_out, student_out, inverse_out):
    teacher, _ = unit_columns(teacher_ref[...])
    teacher_out[...] = jnp.transpose(teacher).astype(jnp.bfloat16)
    student, length = unit_columns(student_ref[...])
    student_out[...] = jnp.transpose(student).astype(jnp.bfloat16)
    inverse_out[...] = 1.0 / length


def in_crop_order(core, own_ref, other_ref, teacher_ref, student_ref):
    chips, rows, _ = own_ref.shape
    width = teacher_ref.shape[1]
    for chip in range(chips):
        for got_ref, side in ((own_ref, core), (other_ref, 1 - core)):
            here = pl.ds(pl.multiple_of((2 * chip + side) * rows, rows), rows)
            teacher_ref[here, :] = got_ref[chip, :, :width]
            student_ref[here, :] = got_ref[chip, :, width:]


def exponentials(directions, units, temperature):
    logits = lax.dot_general(
        directions, units, (((1,), (1,)), ((), ())), preferred_element_type=jnp.float32
    )
    return jnp.exp2(logits * (math.log2(math.e) / temperature))


def fold(values):
    rows, lanes = values.shape
    return jnp.sum(values.reshape(rows // 8, 8, lanes), axis=0)


def as_rows(line):
    return jnp.concatenate([line[:, at : at + LANES] for at in range(0, line.shape[1], LANES)], axis=0)


def as_line(rows):
    return jnp.concatenate([rows[at : at + 1, :] for at in range(rows.shape[0])], axis=1)


def send(sent_ref, total, *more):
    values = jnp.concatenate([as_rows(jnp.sum(total, axis=0, keepdims=True)), *more], axis=0)
    for device in range(sent_ref.shape[0]):
        sent_ref[device] = values


def received(got_ref):
    total = got_ref[0]
    for device in range(1, got_ref.shape[0]):
        total = total + got_ref[device]
    return total


def masses_kernel(
    prototypes, place_ref, teacher_hbm, student_hbm, own_ref, other_ref, weight_ref,
    teacher_ref, student_ref, sent_ref, part_ref, turned_ref, teacher_units, student_units, teacher_w_ref, student_w_ref, sems,
):
    span = FETCH * TILE
    copies = []
    for piece in range(teacher_ref.shape[0] // span):
        rows = pl.ds(piece * span, span)
        copies.append((
            pltpu.make_async_copy(teacher_hbm.at[rows], teacher_w_ref.at[rows], sems.at[0, piece]),
            pltpu.make_async_copy(student_hbm.at[rows], student_w_ref.at[rows], sems.at[1, piece]),
        ))
        copies[-1][0].start()
        copies[-1][1].start()
    in_crop_order(place_ref[2], own_ref, other_ref, teacher_units, student_units)
    total = part = 0.0
    for start in range(0, teacher_ref.shape[0], TILE):
        here = slice(start, start + TILE)
        if start % span == 0:
            copies[start // span][0].wait()
            copies[start // span][1].wait()
        mass = exponentials(teacher_w_ref[here, :], teacher_units[...], teacher_temp)
        teacher_ref[here, :] = mass
        scale = 1.0 / (prototypes * jnp.sum(mass, axis=1, keepdims=True))
        total = total + fold(mass * scale)
        mass = exponentials(student_w_ref[here, :], student_units[...], student_temp)
        student_ref[here, :] = mass
        part = part + fold(mass)
    send(sent_ref, total, weight_ref[...])
    part_ref[...] = as_rows(jnp.sum(part, axis=0, keepdims=True))
    turned_ref[...] = jnp.transpose(student_units[...].astype(jnp.float32)).astype(jnp.bfloat16)


def sweep_kernel(prototypes, crops, last, mass_ref, got_ref, *refs):
    crop_scale = as_line(1.0 / (crops * received(got_ref)[: crops // LANES]))
    total = 0.0
    for start in range(0, mass_ref.shape[0], TILE):
        mass = mass_ref[start : start + TILE, :]
        scale = 1.0 / (prototypes * jnp.sum(mass * crop_scale, axis=1, keepdims=True))
        total = total + fold(mass * scale)
        if last:
            refs[1][start : start + TILE, :] = scale
    if last:
        send(refs[0], total)
    else:
        send(refs[1], total, refs[0][...])


def gradient_kernel(
    place_ref, teacher_ref, student_ref, scale_ref, first_ref, second_ref, third_ref, turned_ref, inverse_ref, directions_ref,
    sent_ref, gradient_ref, grad_ref, copy_ref, sems,
):
    group, block = place_ref[0], place_ref[1]
    chips, rows_each, _ = sent_ref.shape
    count, crops = student_ref.shape
    width = turned_ref.shape[0]
    span = FETCH * TILE
    copies = []
    for piece in range(count // span):
        columns = pl.ds(pl.multiple_of(block * count + piece * span, span), span)
        copies.append(pltpu.make_async_copy(directions_ref.at[:, columns], copy_ref.at[piece], sems.at[piece]))
        copies[-1].start()
    lines = crops // LANES
    own_crops = crops // GROUPS
    weights = received(first_ref)[lines:] / student_temp
    teacher_scale = as_line(weights / received(third_ref))
    student_scale = as_line(weights / received(second_ref)[lines:])
    own_rows = pl.ds(pl.multiple_of(group * (width // GROUPS), width // GROUPS), width // GROUPS)
    own_lanes = pl.ds(pl.multiple_of(group * own_crops, own_crops), own_crops)
    features = 0.0
    for start in range(0, count, TILE):
        here, slot = slice(start, start + TILE), (start // TILE) % 2
        gradient = student_ref[here, :] * student_scale - teacher_ref[here, :] * scale_ref[here, :] * teacher_scale
        gradient_ref[slot] = gradient.astype(jnp.bfloat16)
        if start % span == 0:
            copies[start // span].wait()
        weight_grad = lax.dot_general(
            turned_ref[...], gradient_ref[slot], (((1,), (1,)), ((), ())), preferred_element_type=jnp.float32
        )
        inverse = inverse_ref[:, here]
        piece = slice(start % span, start % span + TILE)
        unit = copy_ref[start // span, :, piece].astype(jnp.float32) * inverse
        dot = jnp.sum(unit * weight_grad, axis=0, keepdims=True)
        grad_ref[slot] = (weight_grad - unit * dot) * inverse
        own = grad_ref[slot, own_rows, :].astype(jnp.bfloat16)
        sent_ref[:, :, here] = own.reshape(chips, rows_each, TILE)
        features = features + jnp.dot(
            unit.astype(jnp.bfloat16), gradient_ref[slot, :, own_lanes], preferred_element_type=jnp.float32
        )

    features = jnp.transpose(features).astype(jnp.bfloat16)
    per_chip = own_crops // chips
    for chip in range(chips):
        for piece in range(per_chip // rows_each):
            start = chip * per_chip + piece * rows_each
            at = count + piece * width
            sent_ref[chip, :, at : at + width] = features[start : start + rows_each, :]


def collect_kernel(place_ref, got_ref, keep_ref, give_ref):
    chips, rows_each, _ = got_ref.shape
    rows, width = keep_ref.shape
    total = got_ref[0].astype(jnp.float32)
    for chip in range(1, chips):
        total = total + got_ref[chip].astype(jnp.float32)
    pieces = rows // rows_each
    for piece in range(pieces):
        first = total[:, piece * width : (piece + 1) * width]
        second = total[:, (pieces + piece) * width : (pieces + piece + 1) * width]
        here = slice(piece * rows_each, (piece + 1) * rows_each)
        keep_ref[here, :] = jnp.where(place_ref[2] == 0, first, second)
        give_ref[here, :] = jnp.where(place_ref[2] == 0, second, first)


def feature_kernel(keep_ref, other_ref, student_ref, out_ref):
    total = keep_ref[...] + other_ref[...]
    hat, length = unit_rows(student_ref[...])
    out_ref[...] = (total - hat * jnp.sum(hat * total, axis=1, keepdims=True)) / length


def widen_kernel(got_ref, out_ref):
    chips, _, columns = got_ref.shape
    for chip in range(chips):
        out_ref[:, chip * columns : (chip + 1) * columns] = got_ref[chip].astype(jnp.float32)


def kernel_body(teacher_feat, student_feat, crop_weight, teacher_v, student_v):
    f32, bf16 = jnp.float32, jnp.bfloat16
    shape = jax.ShapeDtypeStruct
    blocks, fsdp = lax.axis_size("block"), lax.axis_size("fsdp")
    chips = blocks * GROUPS
    members, devices = blocks * fsdp, chips * fsdp
    rows, width = teacher_feat.shape
    crops = rows * devices
    lines = crops // LANES
    kept = teacher_v.shape[1]
    prototypes = kept * fsdp
    count = kept // blocks
    group, block = lax.axis_index("group")[None], lax.axis_index("block")[None]
    core = lax.axis_index("fsdp")[None]
    place = jnp.concatenate([group, block, core])
    elements = count * crops
    smem, vmem = pl.BlockSpec(memory_space=pltpu.SMEM), pl.BlockSpec(memory_space=pltpu.VMEM)

    def swap(values):
        return lax.ppermute(values, "fsdp", [(0, 1), (1, 0)])

    def share(values):
        return lax.all_to_all(values, GROUP, 0, 0)

    dma = pltpu.SemaphoreType.DMA
    hbm = functools.partial(pltpu.with_memory_space_constraint, memory_space=pltpu.HBM)
    sent = call(
        units_kernel,
        shape((chips, rows, 2 * width), bf16),
        in_specs=[pl.BlockSpec(memory_space=pl.ANY)] * 2,
        scratch_shapes=[pltpu.VMEM((rows, width), bf16), pltpu.VMEM((rows, width), bf16), dma((2,))],
    )(hbm(teacher_feat), hbm(student_feat))
    own = lax.all_to_all(sent, CHIPS, 0, 0)

    device = ((group[0] * blocks + block[0]) * fsdp + core[0]) * rows
    weights = lax.dynamic_update_slice(jnp.zeros((crops,), f32), crop_weight.astype(f32), (device,)).reshape(lines, LANES)
    placed = weights
    for move in range(1, GROUPS):
        placed = placed + lax.ppermute(weights, "group", [(at, (at + move) % GROUPS) for at in range(GROUPS)])

    span = 2 * TILE
    spans = count // span
    column = pl.BlockSpec((width, span), lambda step, at: (0, at[0] * spans + step))
    turned = pl.BlockSpec((span, width), lambda step, at: (step, 0))
    line = pl.BlockSpec((1, span), lambda step, at: (0, step))
    teacher_w, student_w, inverse = call(
        directions_kernel,
        (
            pltpu.HBM((count, width), bf16),
            pltpu.HBM((count, width), bf16),
            shape((1, count), f32),
        ),
        flops=12 * count * width,
        moved=8 * count * width,
        grid_spec=pltpu.PrefetchScalarGridSpec(
            num_scalar_prefetch=1,
            grid=(spans,),
            in_specs=[column, column],
            out_specs=[turned, turned, line],
        ),
    )(
        block,
        hbm(teacher_v),
        hbm(student_v),
    )

    own, teacher_w, placed = lax.optimization_barrier((own, teacher_w, placed))
    other = swap(own)
    units = pltpu.VMEM((crops, width), bf16)
    mass, student_mass, sent, student_part, student_turned = call(
        functools.partial(masses_kernel, prototypes),
        (
            shape((count, crops), f32),
            shape((count, crops), f32),
            shape((members, 2 * lines, LANES), f32),
            shape((lines, LANES), f32),
            shape((width, crops), bf16),
        ),
        flops=4 * elements * width,
        exps=2 * elements,
        in_specs=[smem] + [pl.BlockSpec(memory_space=pl.ANY)] * 2 + [vmem] * 3,
        scratch_shapes=[units, units] + [pltpu.VMEM((count, width), bf16)] * 2 + [dma((2, count // (FETCH * TILE)))],
    )(place, hbm(teacher_w), hbm(student_w), own, other, placed)
    first = share(sent)
    sent = call(
        functools.partial(sweep_kernel, prototypes, crops, False),
        shape((members, 2 * lines, LANES), f32),
        flops=4 * elements,
    )(mass, first, student_part)
    second = share(sent)
    sent, scale = call(
        functools.partial(sweep_kernel, prototypes, crops, True),
        (shape((members, lines, LANES), f32), shape((count, 1), f32)),
        flops=4 * elements,
    )(mass, second)
    third = share(sent)

    out_rows = width // chips
    per_chip = rows * fsdp * width // out_rows
    sent = call(
        gradient_kernel,
        shape((blocks, out_rows, count + per_chip), bf16),
        flops=4 * elements * width,
        in_specs=[smem] + [vmem] * 8 + [pl.BlockSpec(memory_space=pl.ANY)],
        scratch_shapes=[
            pltpu.VMEM((2, TILE, crops), bf16),
            pltpu.VMEM((2, width, TILE), f32),
            pltpu.VMEM((count // (FETCH * TILE), width, FETCH * TILE), bf16),
            dma((count // (FETCH * TILE),)),
        ],
    )(
        place, mass, student_mass, scale, first, second, third, student_turned, inverse, hbm(student_v)
    )
    got = lax.all_to_all(sent, "block", 0, 0)
    keep, give = call(
        collect_kernel,
        [shape((rows, width), f32)] * 2,
        grid=(1,),
        in_specs=[smem, pl.BlockSpec((blocks, out_rows, per_chip), lambda step: (0, 0, count // per_chip))],
    )(place, got)
    grad_feat = call(feature_kernel, shape((rows, width), f32))(keep, swap(give), student_feat)
    grad_v = call(
        widen_kernel,
        shape((out_rows, kept), f32),
        grid=(1,),
        in_specs=[pl.BlockSpec((blocks, out_rows, count), lambda step: (0, 0, 0))],
        out_specs=pl.BlockSpec((out_rows, kept), lambda step: (0, 0)),
    )(got)
    return (grad_v, grad_feat)


def solution(mesh):
    dp, fsdp = mesh.shape["dp"], mesh.shape["fsdp"]
    blocks = dp // GROUPS

    def run(teacher_feat, student_feat, crop_weight, teacher_v, student_v):
        crops = teacher_feat.shape[0]
        count = teacher_v.shape[1] // (blocks * fsdp)
        fits = fsdp == 2 and dp == 16 and count % (2 * TILE) == 0 and crops == 1024
        if fits and 8 * count * crops <= KEPT_BYTES:
            grid = Mesh(mesh.devices.reshape(GROUPS, blocks, fsdp), (*CHIPS, "fsdp"))
            body, chips = kernel_body, CHIPS
        else:
            grid, body, chips = mesh, plain_body, ("dp",)
        every = P((*chips, "fsdp"))
        return jax.shard_map(
            body,
            mesh=grid,
            in_specs=(every, every, every, P(None, "fsdp"), P(None, "fsdp")),
            out_specs=(P(chips, "fsdp"), every),
            check_vma=False,
        )(teacher_feat, student_feat, crop_weight, teacher_v, student_v)

    return run
```

profile of v0, /device:TPU:0, one launch (start us, length us, event | category | flops | bytes accessed | tf_op | source)
XLA Modules:
  0.0 85.5 jit_solution(17392537156134969520)
XLA Ops:
  0.6 1.7 %shard_map.68 = bf16[16,32,512]{2,1,0:T(8,128)(2,1)} custom-call(bf16[32,256]{1,0:T(8,128)(2,1)} %teacher_ref.2, bf16[32,256]{1,0:T(8,128)(2,1)} %student_ref.5), custom_call_target="tpu_custom_call" | custom-call | tf_op jit(solution)/shard_map/pallas_call | solution.py:357
  2.4 8.3 %all-to-all-start = ((bf16[16,32,512]{2,1,0:T(8,128)(2,1)}), bf16[16,32,512]{2,1,0:T(8,128)(2,1)S(1)}, u32[]{:S(2)}, u32[]{:S(2)}) async-start(bf16[16,32,512]{2,1,0:T(8,128)(2,1)} %shard_map.68), calls=%async_computation | async-start | bytes 1048576 | tf_op jit(solution)/shard_map/all_to_all | solution.py:363
  10.7 0.8 convert_dynamic-update-slice_fusion
  11.5 2.8 %collective-permute-start = (f32[8,128]{1,0:T(8,128)S(1)}, f32[8,128]{1,0:T(8,128)S(1)}, u32[]{:S(2)}, u32[]{:S(2)}) collective-permute-start(f32[8,128]{1,0:T(8,128)S(1)} %bitcast.5), channel_id=1, source_target_pairs={{0,16},{16,0},{1,17},{17,1},{2,18},{18,2},{3,19},{19,3},{4,20},{20... | collective-permute-start | bytes 12296 | tf_op jit(solution)/shard_map/ppermute | solution.py:369
  14.3 4.1 %shard_map.69 = (bf16[2048,256]{1,0:T(8,128)(2,1)}, bf16[2048,256]{1,0:T(8,128)(2,1)}, f32[1,2048]{1,0:T(1,128)S(1)}) custom-call(s32[1]{0:T(128)} %bitcast.1.block_ref, bf16[256,16384]{1,0:T(8,128)(2,1)} %teacher_ref.3, bf16[256,16384]{1,0:T(8,128)(2,1)} %directions_ref.1), custom_call_target="tpu_custom_call" | custom-call | flops 6291456 | bytes 4194304 | tf_op jit(solution)/shard_map/pallas_call | solution.py:376
  18.4 6.9 %collective-permute-done = f32[8,128]{1,0:T(8,128)S(1)} collective-permute-done((f32[8,128]{1,0:T(8,128)S(1)}, f32[8,128]{1,0:T(8,128)S(1)}, u32[]{:S(2)}, u32[]{:S(2)}) %collective-permute-start) | collective-permute-done | bytes 4128 | tf_op jit(solution)/shard_map/ppermute | solution.py:369
  25.3 0.7 all-to-all-done.own_ref
  25.9 0.0 collective-permute-start.1
  25.9 0.1 pad_add_fusion.place_ref
  26.0 1.8 %collective-permute-done.1.other_ref = bf16[16,32,512]{2,1,0:T(8,128)(2,1)S(1)} collective-permute-done((bf16[16,32,512]{2,1,0:T(8,128)(2,1)S(1)}, bf16[16,32,512]{2,1,0:T(8,128)(2,1)S(1)}, u32[]{:S(2)}, u32[]{:S(2)}) %collective-permute-start.1) | collective-permute-done | bytes 524320 | tf_op jit(solution)/shard_map/ppermute | solution.py:350
  27.8 5.9 %shard_map.70 = (f32[2048,1024]{1,0:T(8,128)S(1)}, f32[2048,1024]{1,0:T(8,128)S(1)}, f32[16,16,128]{2,1,0:T(8,128)S(1)}, f32[8,128]{1,0:T(8,128)S(1)}, bf16[256,1024]{1,0:T(8,128)(2,1)S(1)}) custom-call(s32[3]{0:T(128)S(1)} %pad_add_fusion.place_ref, bf16[2048,256]{1,0:T(8,128)(2,1)} %get-tuple-element.18.teacher_hbm, ...), custom_call_target="tpu_custom_call" | custom-call | flops 2147483648 | tf_op jit(solution)/shard_map/pallas_call | solution.py:400
  33.7 9.2 %all_to_all.25.got_ref.first_ref = f32[16,16,128]{2,1,0:T(8,128)S(1)} all-to-all(f32[16,16,128]{2,1,0:T(8,128)S(1)} %get-tuple-element.24), channel_id=1, replica_groups=mesh['group'=2,'block'=8,'fsdp'=2] {'block','fsdp'}, dimensions={0} | all-to-all | bytes 262144 | tf_op jit(solution)/shard_map/all_to_all | solution.py:353
  42.9 1.2 %shard_map.71 = f32[16,16,128]{2,1,0:T(8,128)S(1)} custom-call(f32[2048,1024]{1,0:T(8,128)S(1)} %get-tuple-element.22.mass_ref.teacher_ref, f32[16,16,128]{2,1,0:T(8,128)S(1)} %all_to_all.25.got_ref.first_ref, f32[8,128]{1,0:T(8,128)S(1)} %get-tuple-element.25.refs_0_), custom_call_target="tpu_custom_call" | custom-call | flops 8388608 | tf_op jit(solution)/shard_map/pallas_call | solution.py:415
  44.1 8.9 %all_to_all.26.got_ref.second_ref = f32[16,16,128]{2,1,0:T(8,128)S(1)} all-to-all(f32[16,16,128]{2,1,0:T(8,128)S(1)} %shard_map.71), channel_id=1, replica_groups=mesh['group'=2,'block'=8,'fsdp'=2] {'block','fsdp'}, dimensions={0} | all-to-all | bytes 262144 | tf_op jit(solution)/shard_map/all_to_all | solution.py:353
  53.0 1.2 %shard_map.72 = (f32[16,8,128]{2,1,0:T(8,128)S(1)}, f32[2048,1]{1,0:T(8,128)S(1)}) custom-call(f32[2048,1024]{1,0:T(8,128)S(1)} %get-tuple-element.22.mass_ref.teacher_ref, f32[16,16,128]{2,1,0:T(8,128)S(1)} %all_to_all.26.got_ref.second_ref), custom_call_target="tpu_custom_call" | custom-call | flops 8388608 | tf_op jit(solution)/shard_map/pallas_call | solution.py:421
  54.2 8.4 %all_to_all.27.third_ref = f32[16,8,128]{2,1,0:T(8,128)S(1)} all-to-all(f32[16,8,128]{2,1,0:T(8,128)S(1)} %get-tuple-element.27), channel_id=1, replica_groups=mesh['group'=2,'block'=8,'fsdp'=2] {'block','fsdp'}, dimensions={0} | all-to-all | bytes 131072 | tf_op jit(solution)/shard_map/all_to_all | solution.py:353
  62.6 0.0 copy-start
  62.6 5.5 %shard_map.73 = bf16[8,16,3072]{2,1,0:T(8,128)(2,1)S(1)} custom-call(s32[3]{0:T(128)S(1)} %pad_add_fusion.place_ref, f32[2048,1024]{1,0:T(8,128)S(1)} %get-tuple-element.22.mass_ref.teacher_ref, f32[2048,1024]{1,0:T(8,128)S(1)} %get-tuple-element.23.student_ref, f32[2048,1]{1,0:T(8,128)S(1)} %get-tuple-element.26.scale_ref, ...), custom_call_target="tpu_custom_call" | custom-call | flops 2147483648 | tf_op jit(solution)/shard_map/pallas_call | solution.py:430
  68.1 14.7 %all_to_all.28.got_ref = bf16[8,16,3072]{2,1,0:T(8,128)(2,1)S(1)} all-to-all(bf16[8,16,3072]{2,1,0:T(8,128)(2,1)S(1)} %shard_map.73), channel_id=1, replica_groups=mesh['group'=2,'block'=8,'fsdp'=2] {'block'}, dimensions={0} | all-to-all | bytes 1572864 | tf_op jit(solution)/shard_map/all_to_all | solution.py:444
  82.8 0.6 shard_map.75
  83.4 0.1 collective-permute-start.2
  83.5 1.0 %shard_map.74 = f32[16,16384]{1,0:T(8,128)} custom-call(bf16[8,16,3072]{2,1,0:T(8,128)(2,1)S(1)} %all_to_all.28.got_ref), custom_call_target="tpu_custom_call" | custom-call | tf_op jit(solution)/shard_map/pallas_call | solution.py:452
  84.5 0.2 collective-permute-done.2.other_ref
  84.7 0.0 copy-done
  84.7 0.8 shard_map.76
  (2 shorter events, 0.0 us)
Async XLA Ops:
  2.4 23.6 %all-to-all-start = ((bf16[16,32,512]{2,1,0:T(8,128)(2,1)}), bf16[16,32,512]{2,1,0:T(8,128)(2,1)S(1)}, u32[]{:S(2)}, u32[]{:S(2)}) async-start(bf16[16,32,512]{2,1,0:T(8,128)(2,1)} %shard_map.68), calls=%async_computation | async-start | bytes 1048576 | tf_op jit(solution)/shard_map/all_to_all | solution.py:363
  11.5 13.8 %collective-permute-start = (f32[8,128]{1,0:T(8,128)S(1)}, f32[8,128]{1,0:T(8,128)S(1)}, u32[]{:S(2)}, u32[]{:S(2)}) collective-permute-start(f32[8,128]{1,0:T(8,128)S(1)} %bitcast.5), channel_id=1, source_target_pairs={{0,16},{16,0},{1,17},{17,1},{2,18},{18,2},{3,19},{19,3},{4,20},{20... | collective-permute-start | bytes 12296 | tf_op jit(solution)/shard_map/ppermute | solution.py:369
  25.9 1.9 %collective-permute-start.1 = (bf16[16,32,512]{2,1,0:T(8,128)(2,1)S(1)}, bf16[16,32,512]{2,1,0:T(8,128)(2,1)S(1)}, u32[]{:S(2)}, u32[]{:S(2)}) collective-permute-start(bf16[16,32,512]{2,1,0:T(8,128)(2,1)S(1)} %all-to-all-done.own_ref), channel_id=1, source_target_pairs={{0,1},{1,0},{2,3},{3,2},{4,5},{5,4},{6,7},{7,6},{8,9},{9,8},{10,11... | collective-permute-start | bytes 1572872 | tf_op jit(solution)/shard_map/ppermute | solution.py:350
  62.6 22.1 %copy-start = (bf16[32,256]{1,0:T(8,128)(2,1)S(1)}, bf16[32,256]{1,0:T(8,128)(2,1)}, u32[]{:S(2)}) copy-start(bf16[32,256]{1,0:T(8,128)(2,1)} %student_ref.5) | copy-start | bytes 49156
  83.4 1.3 %collective-permute-start.2 = (f32[32,256]{1,0:T(8,128)S(1)}, f32[32,256]{1,0:T(8,128)S(1)}, u32[]{:S(2)}, u32[]{:S(2)}) collective-permute-start(f32[32,256]{1,0:T(8,128)S(1)} %get-tuple-element.31), channel_id=1, source_target_pairs={{0,1},{1,0},{2,3},{3,2},{4,5},{5,4},{6,7},{7,6},{8,9},{9,8},{10,11... | collective-permute-start | bytes 98312 | tf_op jit(solution)/shard_map/ppermute | solution.py:350
where the time goes:
time: 86 us; the launch traced here: 85.5 us
  blocking collectives  41.3 us (48%)
  Pallas kernels  21.9 us (25%)
  starting transfers between devices  11.2 us (13%)
  waiting for transfers between devices  9.53 us (11%)
    all_to_all x3, blocking collectives, share(): return lax.all_to_all(values, GROUP, 0, 0)  26.6 us
    all_to_all x1, blocking collectives, kernel_body(): got = lax.all_to_all(sent, 'block', 0, 0)  14.7 us
    all_to_all x1, starting transfers between devices, kernel_body(): own = lax.all_to_all(sent, CHIPS, 0, 0)  8.32 us
    ppermute x1, waiting for transfers between devices, kernel_body(): lax.ppermute(weights, 'group', [(at, (at + move) % GROUPS) for at in rang...  6.89 us
    pallas_call x1, Pallas kernels, kernel_body(): call(functools.partial(masses_kernel, prototypes), (shape((count, crops),...  5.86 us
    pallas_call x1, Pallas kernels, kernel_body(): call(gradient_kernel, shape((blocks, out_rows, count + per_chip), bf16),...  5.47 us
    pallas_call x1, Pallas kernels, kernel_body(): call(directions_kernel, (pltpu.HBM((count, width), bf16), pltpu.HBM((coun...  4.07 us
    ppermute x1, starting transfers between devices, kernel_body(): lax.ppermute(weights, 'group', [(at, (at + move) % GROUPS) for at in rang...  2.81 us
  transfers between devices with their start and end apart: 4, of which 4 were waited for; matrix products, arithmetic and copies ran while one was open for 1% of the time, Pallas kernels for 6%

commit v1 on v0

--- a/solution.py
+++ b/solution.py
@@ -159,16 +159,6 @@
     inverse_out[...] = 1.0 / length
 
 
-def in_crop_order(core, own_ref, other_ref, teacher_ref, student_ref):
-    chips, rows, _ = own_ref.shape
-    width = teacher_ref.shape[1]
-    for chip in range(chips):
-        for got_ref, side in ((own_ref, core), (other_ref, 1 - core)):
-            here = pl.ds(pl.multiple_of((2 * chip + side) * rows, rows), rows)
-            teacher_ref[here, :] = got_ref[chip, :, :width]
-            student_ref[here, :] = got_ref[chip, :, width:]
-
-
 def exponentials(directions, units, temperature):
     logits = lax.dot_general(
         directions, units, (((1,), (1,)), ((), ())), preferred_element_type=jnp.float32
@@ -189,8 +179,19 @@
     return jnp.concatenate([rows[at : at + 1, :] for at in range(rows.shape[0])], axis=1)
 
 
-def send(sent_ref, total, *more):
-    values = jnp.concatenate([as_rows(jnp.sum(total, axis=0, keepdims=True)), *more], axis=0)
+def by_core(core, own, other):
+    return jnp.concatenate([jnp.where(core == 0, own, other), jnp.where(core == 0, other, own)], axis=0)
+
+
+def halves(core, rows):
+    half = rows.shape[0] // 2
+    first, second = rows[:half], rows[half:]
+    return as_line(jnp.where(core == 0, first, second)), as_line(jnp.where(core == 0, second, first))
+
+
+def send(sent_ref, core, own, other, *more):
+    own, other = (as_rows(jnp.sum(total, axis=0, keepdims=True)) for total in (own, other))
+    values = jnp.concatenate([by_core(core, own, other), *more], axis=0)
     for device in range(sent_ref.shape[0]):
         sent_ref[device] = values
 
@@ -202,13 +203,22 @@
     return total
 
 
-def masses_kernel(
-    prototypes, place_ref, teacher_hbm, student_hbm, own_ref, other_ref, weight_ref,
-    teacher_ref, student_ref, sent_ref, part_ref, turned_ref, teacher_units, student_units, teacher_w_ref, student_w_ref, sems,
+def units_of(got_ref, width, side):
+    chips, rows, _ = got_ref.shape
+    return got_ref[:, :, side * width : (side + 1) * width].reshape(chips * rows, width)
+
+
+def turn(units):
+    return jnp.transpose(units.astype(jnp.float32)).astype(jnp.bfloat16)
+
+
+def own_kernel(
+    teacher_hbm, student_hbm, got_ref, teacher_ref, student_ref, teacher_w_ref, student_w_ref, part_ref, turned_ref, sems
 ):
+    count, width = teacher_w_ref.shape
     span = FETCH * TILE
     copies = []
-    for piece in range(teacher_ref.shape[0] // span):
+    for piece in range(count // span):
         rows = pl.ds(piece * span, span)
         copies.append((
             pltpu.make_async_copy(teacher_hbm.at[rows], teacher_w_ref.at[rows], sems.at[0, piece]),
@@ -216,104 +226,142 @@
         ))
         copies[-1][0].start()
         copies[-1][1].start()
-    in_crop_order(place_ref[2], own_ref, other_ref, teacher_units, student_units)
-    total = part = 0.0
-    for start in range(0, teacher_ref.shape[0], TILE):
+    teacher, student = units_of(got_ref, width, 0), units_of(got_ref, width, 1)
+    turned_ref[...] = turn(student)
+    part = 0.0
+    for start in range(0, count, TILE):
         here = slice(start, start + TILE)
         if start % span == 0:
             copies[start // span][0].wait()
             copies[start // span][1].wait()
-        mass = exponentials(teacher_w_ref[here, :], teacher_units[...], teacher_temp)
-        teacher_ref[here, :] = mass
-        scale = 1.0 / (prototypes * jnp.sum(mass, axis=1, keepdims=True))
-        total = total + fold(mass * scale)
-        mass = exponentials(student_w_ref[here, :], student_units[...], student_temp)
+        teacher_ref[here, :] = exponentials(teacher_w_ref[here, :], teacher, teacher_temp)
+        mass = exponentials(student_w_ref[here, :], student, student_temp)
         student_ref[here, :] = mass
         part = part + fold(mass)
-    send(sent_ref, total, weight_ref[...])
-    part_ref[...] = as_rows(jnp.sum(part, axis=0, keepdims=True))
-    turned_ref[...] = jnp.transpose(student_units[...].astype(jnp.float32)).astype(jnp.bfloat16)
-
-
-def sweep_kernel(prototypes, crops, last, mass_ref, got_ref, *refs):
-    crop_scale = as_line(1.0 / (crops * received(got_ref)[: crops // LANES]))
-    total = 0.0
-    for start in range(0, mass_ref.shape[0], TILE):
-        mass = mass_ref[start : start + TILE, :]
-        scale = 1.0 / (prototypes * jnp.sum(mass * crop_scale, axis=1, keepdims=True))
+    part_ref[...] = part
+
+
+def other_kernel(
+    prototypes, place_ref, teacher_w_ref, student_w_ref, got_ref, own_ref, own_part_ref, weight_ref,
+    teacher_ref, student_ref, sent_ref, part_ref, turned_ref,
+):
+    count, width = teacher_w_ref.shape
+    core = place_ref[2]
+    teacher, student = units_of(got_ref, width, 0), units_of(got_ref, width, 1)
+    turned_ref[...] = turn(student)
+    own_total = total = part = 0.0
+    for start in range(0, count, TILE):
+        here = slice(start, start + TILE)
+        mass = exponentials(teacher_w_ref[here, :], teacher, teacher_temp)
+        teacher_ref[here, :] = mass
+        own = own_ref[here, :]
+        proto = jnp.sum(own, axis=1, keepdims=True) + jnp.sum(mass, axis=1, keepdims=True)
+        scale = 1.0 / (prototypes * proto)
+        own_total = own_total + fold(own * scale)
         total = total + fold(mass * scale)
-        if last:
-            refs[1][start : start + TILE, :] = scale
-    if last:
-        send(refs[0], total)
-    else:
-        send(refs[1], total, refs[0][...])
-
-
-def gradient_kernel(
-    place_ref, teacher_ref, student_ref, scale_ref, first_ref, second_ref, third_ref, turned_ref, inverse_ref, directions_ref,
-    sent_ref, gradient_ref, grad_ref, copy_ref, sems,
+        mass = exponentials(student_w_ref[here, :], student, student_temp)
+        student_ref[here, :] = mass
+        part = part + fold(mass)
+    send(sent_ref, core, own_total, total, weight_ref[...])
+    own_part = as_rows(jnp.sum(own_part_ref[...], axis=0, keepdims=True))
+    part_ref[...] = by_core(core, own_part, as_rows(jnp.sum(part, axis=0, keepdims=True)))
+
+
+def sweep(prototypes, crops, place_ref, own_ref, other_ref, got_ref):
+    own_crop, other_crop = halves(place_ref[2], 1.0 / (crops * received(got_ref)[: crops // LANES]))
+    own_total = other_total = 0.0
+    scales = []
+    for start in range(0, own_ref.shape[0], TILE):
+        own, other = own_ref[start : start + TILE, :], other_ref[start : start + TILE, :]
+        proto = jnp.sum(own * own_crop, axis=1, keepdims=True) + jnp.sum(other * other_crop, axis=1, keepdims=True)
+        scales.append(1.0 / (prototypes * proto))
+        own_total = own_total + fold(own * scales[-1])
+        other_total = other_total + fold(other * scales[-1])
+    return own_total, other_total, scales
+
+
+def sweep_kernel(prototypes, crops, place_ref, own_ref, other_ref, got_ref, part_ref, sent_ref):
+    own, other, _ = sweep(prototypes, crops, place_ref, own_ref, other_ref, got_ref)
+    send(sent_ref, place_ref[2], own, other, part_ref[...])
+
+
+def last_sweep_kernel(
+    prototypes, crops, place_ref, own_ref, other_ref, got_ref, directions_ref, sent_ref, scale_ref, copy_ref, sems
 ):
-    group, block = place_ref[0], place_ref[1]
-    chips, rows_each, _ = sent_ref.shape
-    count, crops = student_ref.shape
-    width = turned_ref.shape[0]
-    span = FETCH * TILE
+    pieces, _, span = copy_ref.shape
     copies = []
-    for piece in range(count // span):
-        columns = pl.ds(pl.multiple_of(block * count + piece * span, span), span)
+    for piece in range(pieces):
+        columns = pl.ds(pl.multiple_of((place_ref[1] * pieces + piece) * span, span), span)
         copies.append(pltpu.make_async_copy(directions_ref.at[:, columns], copy_ref.at[piece], sems.at[piece]))
         copies[-1].start()
-    lines = crops // LANES
-    own_crops = crops // GROUPS
+    own, other, scales = sweep(prototypes, crops, place_ref, own_ref, other_ref, got_ref)
+    for index, scale in enumerate(scales):
+        scale_ref[index * TILE : (index + 1) * TILE, :] = scale
+    send(sent_ref, place_ref[2], own, other)
+    for copy in copies:
+        copy.wait()
+
+
+def gradient_kernel(
+    place_ref, own_mass_ref, other_mass_ref, own_student_ref, other_student_ref, scale_ref, first_ref, second_ref, third_ref,
+    own_turned_ref, other_turned_ref, inverse_ref, copy_ref, sent_ref, gradient_ref, grad_ref, unit_ref,
+):
+    group, core = place_ref[0], place_ref[2]
+    chips, rows_each, _ = sent_ref.shape
+    count, half = own_mass_ref.shape
+    width = own_turned_ref.shape[0]
+    span = copy_ref.shape[2]
+    lines = 2 * half // LANES
     weights = received(first_ref)[lines:] / student_temp
-    teacher_scale = as_line(weights / received(third_ref))
-    student_scale = as_line(weights / received(second_ref)[lines:])
+    teacher_scales = halves(core, weights / received(third_ref))
+    student_scales = halves(core, weights / received(second_ref)[lines:])
+    masses, students = (own_mass_ref, other_mass_ref), (own_student_ref, other_student_ref)
     own_rows = pl.ds(pl.multiple_of(group * (width // GROUPS), width // GROUPS), width // GROUPS)
-    own_lanes = pl.ds(pl.multiple_of(group * own_crops, own_crops), own_crops)
-    features = 0.0
+    kept = half // GROUPS
     for start in range(0, count, TILE):
-        here, slot = slice(start, start + TILE), (start // TILE) % 2
-        gradient = student_ref[here, :] * student_scale - teacher_ref[here, :] * scale_ref[here, :] * teacher_scale
-        gradient_ref[slot] = gradient.astype(jnp.bfloat16)
-        if start % span == 0:
-            copies[start // span].wait()
-        weight_grad = lax.dot_general(
-            turned_ref[...], gradient_ref[slot], (((1,), (1,)), ((), ())), preferred_element_type=jnp.float32
-        )
+        here, slot = slice(start, start + TILE), start // TILE
+        piece = slice(start % span, start % span + TILE)
         inverse = inverse_ref[:, here]
-        piece = slice(start % span, start % span + TILE)
         unit = copy_ref[start // span, :, piece].astype(jnp.float32) * inverse
+        for side in range(2):
+            teacher = masses[side][here, :] * scale_ref[here, :] * teacher_scales[side]
+            gradient = students[side][here, :] * student_scales[side] - teacher
+            gradient_ref[slot, side] = gradient.astype(jnp.bfloat16)
+        weight_grad = 0.0
+        for side, turned_ref in enumerate((own_turned_ref, other_turned_ref)):
+            weight_grad = weight_grad + lax.dot_general(
+                turned_ref[...], gradient_ref[slot, side], (((1,), (1,)), ((), ())), preferred_element_type=jnp.float32
+            )
         dot = jnp.sum(unit * weight_grad, axis=0, keepdims=True)
         grad_ref[slot] = (weight_grad - unit * dot) * inverse
         own = grad_ref[slot, own_rows, :].astype(jnp.bfloat16)
         sent_ref[:, :, here] = own.reshape(chips, rows_each, TILE)
-        features = features + jnp.dot(
-            unit.astype(jnp.bfloat16), gradient_ref[slot, :, own_lanes], preferred_element_type=jnp.float32
-        )
-
-    features = jnp.transpose(features).astype(jnp.bfloat16)
-    per_chip = own_crops // chips
-    for chip in range(chips):
-        for piece in range(per_chip // rows_each):
-            start = chip * per_chip + piece * rows_each
-            at = count + piece * width
-            sent_ref[chip, :, at : at + width] = features[start : start + rows_each, :]
-
-
-def collect_kernel(place_ref, got_ref, keep_ref, give_ref):
-    chips, rows_each, _ = got_ref.shape
+        unit_ref[:, here] = unit.astype(jnp.bfloat16)
+
+    per_core = kept // chips
+    pieces = per_core // rows_each
+    for side in range(2):
+        lanes = pl.ds(pl.multiple_of(group * kept, kept), kept)
+        gradient = gradient_ref[:, side, :, lanes].reshape(count, kept)
+        feature = jnp.dot(unit_ref[...], gradient, preferred_element_type=jnp.float32)
+        feature = jnp.transpose(feature).astype(jnp.bfloat16)
+        for chip in range(chips):
+            for piece in range(pieces):
+                start = chip * per_core + piece * rows_each
+                at = count + (side * pieces + piece) * width
+                sent_ref[chip, :, at : at + width] = feature[start : start + rows_each, :]
+
+
+def collect_kernel(got_ref, keep_ref, give_ref):
+    rows_each = got_ref.shape[1]
     rows, width = keep_ref.shape
     total = got_ref[0].astype(jnp.float32)
-    for chip in range(1, chips):
+    for chip in range(1, got_ref.shape[0]):
         total = total + got_ref[chip].astype(jnp.float32)
     pieces = rows // rows_each
-    for piece in range(pieces):
-        first = total[:, piece * width : (piece + 1) * width]
-        second = total[:, (pieces + piece) * width : (pieces + piece + 1) * width]
-        here = slice(piece * rows_each, (piece + 1) * rows_each)
-        keep_ref[here, :] = jnp.where(place_ref[2] == 0, first, second)
-        give_ref[here, :] = jnp.where(place_ref[2] == 0, second, first)
+    for piece in range(2 * pieces):
+        out_ref, at = (keep_ref, piece) if piece < pieces else (give_ref, piece - pieces)
+        out_ref[at * rows_each : (at + 1) * rows_each, :] = total[:, piece * width : (piece + 1) * width]
 
 
 def feature_kernel(keep_ref, other_ref, student_ref, out_ref):
@@ -362,7 +410,7 @@
     )(hbm(teacher_feat), hbm(student_feat))
     own = lax.all_to_all(sent, CHIPS, 0, 0)
 
-    device = ((group[0] * blocks + block[0]) * fsdp + core[0]) * rows
+    device = (core[0] * chips + group[0] * blocks + block[0]) * rows
     weights = lax.dynamic_update_slice(jnp.zeros((crops,), f32), crop_weight.astype(f32), (device,)).reshape(lines, LANES)
     placed = weights
     for move in range(1, GROUPS):
@@ -396,33 +444,55 @@
 
     own, teacher_w, placed = lax.optimization_barrier((own, teacher_w, placed))
     other = swap(own)
-    units = pltpu.VMEM((crops, width), bf16)
-    mass, student_mass, sent, student_part, student_turned = call(
-        functools.partial(masses_kernel, prototypes),
+    half = crops // 2
+    anyspace = pl.BlockSpec(memory_space=pl.ANY)
+    pieces = count // (FETCH * TILE)
+    halved = dict(flops=2 * elements * width, exps=elements)
+    own_mass, own_student, teacher_w, student_w, own_part, own_turned = call(
+        own_kernel,
         (
-            shape((count, crops), f32),
-            shape((count, crops), f32),
+            shape((count, half), f32),
+            shape((count, half), f32),
+            shape((count, width), bf16),
+            shape((count, width), bf16),
+            shape((8, half), f32),
+            shape((width, half), bf16),
+        ),
+        in_specs=[anyspace] * 2 + [vmem],
+        scratch_shapes=[dma((2, pieces))],
+        **halved,
+    )(hbm(teacher_w), hbm(student_w), own)
+    other_mass, other_student, sent, student_part, other_turned = call(
+        functools.partial(other_kernel, prototypes),
+        (
+            shape((count, half), f32),
+            shape((count, half), f32),
             shape((members, 2 * lines, LANES), f32),
             shape((lines, LANES), f32),
-            shape((width, crops), bf16),
+            shape((width, half), bf16),
         ),
-        flops=4 * elements * width,
-        exps=2 * elements,
-        in_specs=[smem] + [pl.BlockSpec(memory_space=pl.ANY)] * 2 + [vmem] * 3,
-        scratch_shapes=[units, units] + [pltpu.VMEM((count, width), bf16)] * 2 + [dma((2, count // (FETCH * TILE)))],
-    )(place, hbm(teacher_w), hbm(student_w), own, other, placed)
+        in_specs=[smem] + [vmem] * 6,
+        **halved,
+    )(place, teacher_w, student_w, other, own_mass, own_part, placed)
     first = share(sent)
     sent = call(
-        functools.partial(sweep_kernel, prototypes, crops, False),
+        functools.partial(sweep_kernel, prototypes, crops),
         shape((members, 2 * lines, LANES), f32),
         flops=4 * elements,
-    )(mass, first, student_part)
+        in_specs=[smem] + [vmem] * 4,
+    )(place, own_mass, other_mass, first, student_part)
     second = share(sent)
-    sent, scale = call(
-        functools.partial(sweep_kernel, prototypes, crops, True),
-        (shape((members, lines, LANES), f32), shape((count, 1), f32)),
+    sent, scale, student_copy = call(
+        functools.partial(last_sweep_kernel, prototypes, crops),
+        (
+            shape((members, lines, LANES), f32),
+            shape((count, 1), f32),
+            shape((pieces, width, count // pieces), bf16),
+        ),
         flops=4 * elements,
-    )(mass, second)
+        in_specs=[smem] + [vmem] * 3 + [anyspace],
+        scratch_shapes=[dma((pieces,))],
+    )(place, own_mass, other_mass, second, hbm(student_v))
     third = share(sent)
 
     out_rows = width // chips
@@ -431,23 +501,23 @@
         gradient_kernel,
         shape((blocks, out_rows, count + per_chip), bf16),
         flops=4 * elements * width,
-        in_specs=[smem] + [vmem] * 8 + [pl.BlockSpec(memory_space=pl.ANY)],
+        in_specs=[smem] + [vmem] * 12,
         scratch_shapes=[
-            pltpu.VMEM((2, TILE, crops), bf16),
-            pltpu.VMEM((2, width, TILE), f32),
-            pltpu.VMEM((count // (FETCH * TILE), width, FETCH * TILE), bf16),
-            dma((count // (FETCH * TILE),)),
+            pltpu.VMEM((count // TILE, 2, TILE, half), bf16),
+            pltpu.VMEM((count // TILE, width, TILE), f32),
+            pltpu.VMEM((width, count), bf16),
         ],
     )(
-        place, mass, student_mass, scale, first, second, third, student_turned, inverse, hbm(student_v)
+        place, own_mass, other_mass, own_student, other_student, scale, first, second, third,
+        own_turned, other_turned, inverse, student_copy,
     )
     got = lax.all_to_all(sent, "block", 0, 0)
     keep, give = call(
         collect_kernel,
         [shape((rows, width), f32)] * 2,
         grid=(1,),
-        in_specs=[smem, pl.BlockSpec((blocks, out_rows, per_chip), lambda step: (0, 0, count // per_chip))],
-    )(place, got)
+        in_specs=[pl.BlockSpec((blocks, out_rows, per_chip), lambda step: (0, 0, count // per_chip))],
+    )(got)
     grad_feat = call(feature_kernel, shape((rows, width), f32))(keep, swap(give), student_feat)
     grad_v = call(
         widen_kernel,

time: 86 us -> 83.7 us (0.973)
  waiting for transfers between devices: 9.53 us -> 7.69 us
    ppermute x2, waiting for transfers between devices: 1.99 us -> 0.16 us  [swap(): return lax.ppermute(values, 'fsdp', [(0, 1), (1, 0)])]
    pallas_call x1, Pallas kernels: 5.47 us -> 4.05 us  [kernel_body(): call(gradient_kernel, shape((blocks, out_rows, count + per_chip), bf16),...]
    pallas_call x3 -> x4, Pallas kernels: 8.19 us -> 9.53 us  [the longest x1 3.03 us: kernel_body(): call(own_kernel, (shape((count, half), f32), shape((count, half), f32), s...]
  transfers between devices with their start and end apart: 4 -> 4, of which waited for: 4 -> 3; matrix products, arithmetic and copies ran while one was open for 1% -> 1% of each run, Pallas kernels for 6% -> 10%
where the time goes in v1:
time: 83.7 us; the launch traced here: 83.2 us
  blocking collectives  41.4 us (49%)
  Pallas kernels  21.3 us (25%)
  starting transfers between devices  11.2 us (13%)
  waiting for transfers between devices  7.69 us (9%)
  other arithmetic  0.85 us (1%)
    all_to_all x3, blocking collectives, share(): return lax.all_to_all(values, GROUP, 0, 0)  26.7 us
    all_to_all x1, blocking collectives, kernel_body(): got = lax.all_to_all(sent, 'block', 0, 0)  14.7 us
    all_to_all x1, starting transfers between devices, kernel_body(): own = lax.all_to_all(sent, CHIPS, 0, 0)  8.32 us
    ppermute x1, waiting for transfers between devices, kernel_body(): lax.ppermute(weights, 'group', [(at, (at + move) % GROUPS) for at in rang...  6.88 us
    pallas_call x1, Pallas kernels, kernel_body(): call(directions_kernel, (pltpu.HBM((count, width), bf16), pltpu.HBM((coun...  4.08 us
    pallas_call x1, Pallas kernels, kernel_body(): call(gradient_kernel, shape((blocks, out_rows, count + per_chip), bf16),...  4.05 us
    pallas_call x1, Pallas kernels, kernel_body(): call(own_kernel, (shape((count, half), f32), shape((count, half), f32), s...  3.03 us
    pallas_call x1, Pallas kernels, kernel_body(): call(functools.partial(other_kernel, prototypes), (shape((count, half), f...  2.96 us
  transfers between devices with their start and end apart: 4, of which 3 were waited for; matrix products, arithmetic and copies ran while one was open for 1% of the time, Pallas kernels for 10%

profile of v1, /device:TPU:0, one launch (start us, length us, event | category | flops | bytes accessed | tf_op | source)
XLA Modules:
  0.0 83.2 jit_solution(15493340796269037244)
XLA Ops:
  0.6 1.7 %shard_map.68 = bf16[16,32,512]{2,1,0:T(8,128)(2,1)} custom-call(bf16[32,256]{1,0:T(8,128)(2,1)} %teacher_ref.2, bf16[32,256]{1,0:T(8,128)(2,1)} %student_ref.5), custom_call_target="tpu_custom_call" | custom-call | tf_op jit(solution)/shard_map/pallas_call | solution.py:405
  2.4 8.3 %all-to-all-start = ((bf16[16,32,512]{2,1,0:T(8,128)(2,1)}), bf16[16,32,512]{2,1,0:T(8,128)(2,1)S(1)}, u32[]{:S(2)}, u32[]{:S(2)}) async-start(bf16[16,32,512]{2,1,0:T(8,128)(2,1)} %shard_map.68), calls=%async_computation | async-start | bytes 1048576 | tf_op jit(solution)/shard_map/all_to_all | solution.py:411
  10.7 0.8 convert_dynamic-update-slice_fusion
  11.5 2.8 %collective-permute-start = (f32[8,128]{1,0:T(8,128)S(1)}, f32[8,128]{1,0:T(8,128)S(1)}, u32[]{:S(2)}, u32[]{:S(2)}) collective-permute-start(f32[8,128]{1,0:T(8,128)S(1)} %bitcast.5), channel_id=1, source_target_pairs={{0,16},{16,0},{1,17},{17,1},{2,18},{18,2},{3,19},{19,3},{4,20},{20... | collective-permute-start | bytes 12296 | tf_op jit(solution)/shard_map/ppermute | solution.py:417
  14.3 4.1 %shard_map.69 = (bf16[2048,256]{1,0:T(8,128)(2,1)}, bf16[2048,256]{1,0:T(8,128)(2,1)}, f32[1,2048]{1,0:T(1,128)S(1)}) custom-call(s32[1]{0:T(128)} %bitcast.1.block_ref, bf16[256,16384]{1,0:T(8,128)(2,1)} %teacher_ref.3, bf16[256,16384]{1,0:T(8,128)(2,1)} %directions_ref.1), custom_call_target="tpu_custom_call" | custom-call | flops 6291456 | bytes 4194304 | tf_op jit(solution)/shard_map/pallas_call | solution.py:424
  18.4 6.9 %collective-permute-done = f32[8,128]{1,0:T(8,128)S(1)} collective-permute-done((f32[8,128]{1,0:T(8,128)S(1)}, f32[8,128]{1,0:T(8,128)S(1)}, u32[]{:S(2)}, u32[]{:S(2)}) %collective-permute-start) | collective-permute-done | bytes 4128 | tf_op jit(solution)/shard_map/ppermute | solution.py:417
  25.3 0.7 all-to-all-done.got_ref
  25.9 0.0 collective-permute-start.1
  25.9 0.1 pad_add_fusion.place_ref
  26.0 3.0 %shard_map.70 = (f32[2048,512]{1,0:T(8,128)S(1)}, f32[2048,512]{1,0:T(8,128)S(1)}, bf16[2048,256]{1,0:T(8,128)(2,1)S(1)}, bf16[2048,256]{1,0:T(8,128)(2,1)S(1)},...) custom-call(bf16[2048,256]{1,0:T(8,128)(2,1)} %get-tuple-element.25.teacher_hbm, ...), custom_call_target="tpu_custom_call" | custom-call | flops 1073741824 | tf_op jit(solution)/shard_map/pallas_call | solution.py:451
  29.1 0.0 collective-permute-done.1.got_ref
  29.1 3.0 %shard_map.71 = (f32[2048,512]{1,0:T(8,128)S(1)}, f32[2048,512]{1,0:T(8,128)S(1)}, f32[16,16,128]{2,1,0:T(8,128)S(1)}, f32[8,128]{1,0:T(8,128)S(1)}, bf16[256,512]{1,0:T(8,128)(2,1)S(1)}) custom-call(s32[3]{0:T(128)S(1)} %pad_add_fusion.place_ref, bf16[2048,256]{1,0:T(8,128)(2,1)S(1)} %get-tuple-element.29.teacher_w_ref, ...), custom_call_target="tpu_custom_call" | custom-call | flops 1073741824 | tf_op jit(solution)/shard_map/pallas_call | solution.py:465
  32.0 9.3 %all_to_all.25.got_ref.first_ref = f32[16,16,128]{2,1,0:T(8,128)S(1)} all-to-all(f32[16,16,128]{2,1,0:T(8,128)S(1)} %get-tuple-element.36), channel_id=1, replica_groups=mesh['group'=2,'block'=8,'fsdp'=2] {'block','fsdp'}, dimensions={0} | all-to-all | bytes 262144 | tf_op jit(solution)/shard_map/all_to_all | solution.py:401
  41.4 1.7 %shard_map.72 = f32[16,16,128]{2,1,0:T(8,128)S(1)} custom-call(s32[3]{0:T(128)S(1)} %pad_add_fusion.place_ref, f32[2048,512]{1,0:T(8,128)S(1)} %get-tuple-element.28.own_ref.own_mass_ref, f32[2048,512]{1,0:T(8,128)S(1)} %get-tuple-element.33.other_ref.other_mass_ref, f32[16,16,128]{2,1,0:T(8,128)S(1)} %all_to_all.25.got_ref.first_ref, ...), custom_call_target="tpu_custom_call" | custom-call | flops 8388608 | tf_op jit(solution)/shard_map/pallas_call | solution.py:478
  43.1 8.9 %all_to_all.26.got_ref.second_ref = f32[16,16,128]{2,1,0:T(8,128)S(1)} all-to-all(f32[16,16,128]{2,1,0:T(8,128)S(1)} %shard_map.72), channel_id=1, replica_groups=mesh['group'=2,'block'=8,'fsdp'=2] {'block','fsdp'}, dimensions={0} | all-to-all | bytes 262144 | tf_op jit(solution)/shard_map/all_to_all | solution.py:401
  52.0 1.8 %shard_map.73 = (f32[16,8,128]{2,1,0:T(8,128)S(1)}, f32[2048,1]{1,0:T(8,128)S(1)}, bf16[4,256,512]{2,1,0:T(8,128)(2,1)S(1)}) custom-call(s32[3]{0:T(128)S(1)} %pad_add_fusion.place_ref, f32[2048,512]{1,0:T(8,128)S(1)} %get-tuple-element.28.own_ref.own_mass_ref, f32[2048,512]{1,0:T(8,128)S(1)} %get-tuple-element.33.other_ref.other_mass_ref, ...), custom_call_target="tpu_custom_call" | custom-call | flops 8388608 | tf_op jit(solution)/shard_map/pallas_call | solution.py:485
  53.8 8.4 %all_to_all.27.third_ref = f32[16,8,128]{2,1,0:T(8,128)S(1)} all-to-all(f32[16,8,128]{2,1,0:T(8,128)S(1)} %get-tuple-element.39), channel_id=1, replica_groups=mesh['group'=2,'block'=8,'fsdp'=2] {'block','fsdp'}, dimensions={0} | all-to-all | bytes 131072 | tf_op jit(solution)/shard_map/all_to_all | solution.py:401
  62.2 4.1 %shard_map.74 = bf16[8,16,3072]{2,1,0:T(8,128)(2,1)S(1)} custom-call(s32[3]{0:T(128)S(1)} %pad_add_fusion.place_ref, f32[2048,512]{1,0:T(8,128)S(1)} %get-tuple-element.28.own_ref.own_mass_ref, f32[2048,512]{1,0:T(8,128)S(1)} %get-tuple-element.33.other_ref.other_mass_ref, f32[2048,512]{1,0:T(8,128)S(1)} %get-tuple-element.34.own_student_ref, ...), custom_call_target="tpu_custom_call" | custom-call | flops 2147483648 | tf_op jit(solution)/shard_map/pallas_call | solution.py:500
  66.3 0.0 copy-start
  66.3 14.7 %all_to_all.28.got_ref = bf16[8,16,3072]{2,1,0:T(8,128)(2,1)S(1)} all-to-all(bf16[8,16,3072]{2,1,0:T(8,128)(2,1)S(1)} %shard_map.74), channel_id=1, replica_groups=mesh['group'=2,'block'=8,'fsdp'=2] {'block'}, dimensions={0} | all-to-all | bytes 1572864 | tf_op jit(solution)/shard_map/all_to_all | solution.py:514
  81.1 0.1 collective-permute-start.2
  81.2 1.0 %shard_map.75 = f32[16,16384]{1,0:T(8,128)} custom-call(bf16[8,16,3072]{2,1,0:T(8,128)(2,1)S(1)} %all_to_all.28.got_ref), custom_call_target="tpu_custom_call" | custom-call | tf_op jit(solution)/shard_map/pallas_call | solution.py:522
  82.2 0.2 collective-permute-done.2.other_ref
  82.4 0.0 copy-done
  82.4 0.8 shard_map.77
  (3 shorter events, 0.0 us)
Async XLA Ops:
  2.4 23.6 %all-to-all-start = ((bf16[16,32,512]{2,1,0:T(8,128)(2,1)}), bf16[16,32,512]{2,1,0:T(8,128)(2,1)S(1)}, u32[]{:S(2)}, u32[]{:S(2)}) async-start(bf16[16,32,512]{2,1,0:T(8,128)(2,1)} %shard_map.68), calls=%async_computation | async-start | bytes 1048576 | tf_op jit(solution)/shard_map/all_to_all | solution.py:411
  11.5 13.8 %collective-permute-start = (f32[8,128]{1,0:T(8,128)S(1)}, f32[8,128]{1,0:T(8,128)S(1)}, u32[]{:S(2)}, u32[]{:S(2)}) collective-permute-start(f32[8,128]{1,0:T(8,128)S(1)} %bitcast.5), channel_id=1, source_target_pairs={{0,16},{16,0},{1,17},{17,1},{2,18},{18,2},{3,19},{19,3},{4,20},{20... | collective-permute-start | bytes 12296 | tf_op jit(solution)/shard_map/ppermute | solution.py:417
  25.9 3.1 %collective-permute-start.1 = (bf16[16,32,512]{2,1,0:T(8,128)(2,1)S(1)}, bf16[16,32,512]{2,1,0:T(8,128)(2,1)S(1)}, u32[]{:S(2)}, u32[]{:S(2)}) collective-permute-start(bf16[16,32,512]{2,1,0:T(8,128)(2,1)S(1)} %all-to-all-done.got_ref), channel_id=1, source_target_pairs={{0,1},{1,0},{2,3},{3,2},{4,5},{5,4},{6,7},{7,6},{8,9},{9,8},{10,11... | collective-permute-start | bytes 1572872 | tf_op jit(solution)/shard_map/ppermute | solution.py:398
  66.3 16.1 %copy-start = (bf16[32,256]{1,0:T(8,128)(2,1)S(1)}, bf16[32,256]{1,0:T(8,128)(2,1)}, u32[]{:S(2)}) copy-start(bf16[32,256]{1,0:T(8,128)(2,1)} %student_ref.5) | copy-start | bytes 49156
  81.1 1.3 %collective-permute-start.2 = (f32[32,256]{1,0:T(8,128)S(1)}, f32[32,256]{1,0:T(8,128)S(1)}, u32[]{:S(2)}, u32[]{:S(2)}) collective-permute-start(f32[32,256]{1,0:T(8,128)S(1)} %get-tuple-element.45), channel_id=1, source_target_pairs={{0,1},{1,0},{2,3},{3,2},{4,5},{5,4},{6,7},{7,6},{8,9},{9,8},{10,11... | collective-permute-start | bytes 98312 | tf_op jit(solution)/shard_map/ppermute | solution.py:398

commit v2 on v1

--- a/solution.py
+++ b/solution.py
@@ -17,6 +17,7 @@
 
 GROUPS = 2
 TILE = 256
+HALF_TILE = 512
 FETCH = 2
 LANES = 128
 VMEM_BYTES = 12 << 20
@@ -191,15 +192,15 @@
 
 def send(sent_ref, core, own, other, *more):
     own, other = (as_rows(jnp.sum(total, axis=0, keepdims=True)) for total in (own, other))
-    values = jnp.concatenate([by_core(core, own, other), *more], axis=0)
+    values = jnp.concatenate([by_core(core, own, other), *more], axis=0).astype(jnp.bfloat16)
     for device in range(sent_ref.shape[0]):
         sent_ref[device] = values
 
 
 def received(got_ref):
-    total = got_ref[0]
+    total = got_ref[0].astype(jnp.float32)
     for device in range(1, got_ref.shape[0]):
-        total = total + got_ref[device]
+        total = total + got_ref[device].astype(jnp.float32)
     return total
 
 
@@ -229,8 +230,8 @@
     teacher, student = units_of(got_ref, width, 0), units_of(got_ref, width, 1)
     turned_ref[...] = turn(student)
     part = 0.0
-    for start in range(0, count, TILE):
-        here = slice(start, start + TILE)
+    for start in range(0, count, HALF_TILE):
+        here = slice(start, start + HALF_TILE)
         if start % span == 0:
             copies[start // span][0].wait()
             copies[start // span][1].wait()
@@ -250,12 +251,12 @@
     teacher, student = units_of(got_ref, width, 0), units_of(got_ref, width, 1)
     turned_ref[...] = turn(student)
     own_total = total = part = 0.0
-    for start in range(0, count, TILE):
-        here = slice(start, start + TILE)
+    for start in range(0, count, HALF_TILE):
+        here = slice(start, start + HALF_TILE)
         mass = exponentials(teacher_w_ref[here, :], teacher, teacher_temp)
         teacher_ref[here, :] = mass
         own = own_ref[here, :]
-        proto = jnp.sum(own, axis=1, keepdims=True) + jnp.sum(mass, axis=1, keepdims=True)
+        proto = jnp.sum(own + mass, axis=1, keepdims=True)
         scale = 1.0 / (prototypes * proto)
         own_total = own_total + fold(own * scale)
         total = total + fold(mass * scale)
@@ -273,7 +274,7 @@
     scales = []
     for start in range(0, own_ref.shape[0], TILE):
         own, other = own_ref[start : start + TILE, :], other_ref[start : start + TILE, :]
-        proto = jnp.sum(own * own_crop, axis=1, keepdims=True) + jnp.sum(other * other_crop, axis=1, keepdims=True)
+        proto = jnp.sum(own * own_crop + other * other_crop, axis=1, keepdims=True)
         scales.append(1.0 / (prototypes * proto))
         own_total = own_total + fold(own * scales[-1])
         other_total = other_total + fold(other * scales[-1])
@@ -467,7 +468,7 @@
         (
             shape((count, half), f32),
             shape((count, half), f32),
-            shape((members, 2 * lines, LANES), f32),
+            shape((members, 2 * lines, LANES), bf16),
             shape((lines, LANES), f32),
             shape((width, half), bf16),
         ),
@@ -477,7 +478,7 @@
     first = share(sent)
     sent = call(
         functools.partial(sweep_kernel, prototypes, crops),
-        shape((members, 2 * lines, LANES), f32),
+        shape((members, 2 * lines, LANES), bf16),
         flops=4 * elements,
         in_specs=[smem] + [vmem] * 4,
     )(place, own_mass, other_mass, first, student_part)
@@ -485,7 +486,7 @@
     sent, scale, student_copy = call(
         functools.partial(last_sweep_kernel, prototypes, crops),
         (
-            shape((members, lines, LANES), f32),
+            shape((members, lines, LANES), bf16),
             shape((count, 1), f32),
             shape((pieces, width, count // pieces), bf16),
         ),

time: 83.7 us -> 82.8 us (0.989)
  blocking collectives: 41.4 us -> 40.3 us
    all_to_all x3, blocking collectives: 26.7 us -> 25.5 us  [share(): return lax.all_to_all(values, GROUP, 0, 0)]
where the time goes in v2:
time: 82.8 us; the launch traced here: 82.2 us
  blocking collectives  40.3 us (49%)
  Pallas kernels  21.5 us (26%)
  starting transfers between devices  11.2 us (14%)
  waiting for transfers between devices  7.69 us (9%)
  other arithmetic  0.85 us (1%)
    all_to_all x3, blocking collectives, share(): return lax.all_to_all(values, GROUP, 0, 0)  25.5 us
    all_to_all x1, blocking collectives, kernel_body(): got = lax.all_to_all(sent, 'block', 0, 0)  14.8 us
    all_to_all x1, starting transfers between devices, kernel_body(): own = lax.all_to_all(sent, CHIPS, 0, 0)  8.32 us
    ppermute x1, waiting for transfers between devices, kernel_body(): lax.ppermute(weights, 'group', [(at, (at + move) % GROUPS) for at in rang...  6.88 us
    pallas_call x1, Pallas kernels, kernel_body(): call(directions_kernel, (pltpu.HBM((count, width), bf16), pltpu.HBM((coun...  4.08 us
    pallas_call x1, Pallas kernels, kernel_body(): call(gradient_kernel, shape((blocks, out_rows, count + per_chip), bf16),...  4.05 us
    pallas_call x1, Pallas kernels, kernel_body(): call(functools.partial(other_kernel, prototypes), (shape((count, half), f...  3.21 us
    pallas_call x1, Pallas kernels, kernel_body(): call(own_kernel, (shape((count, half), f32), shape((count, half), f32), s...  3.03 us
  transfers between devices with their start and end apart: 4, of which 3 were waited for; matrix products, arithmetic and copies ran while one was open for 1% of the time, Pallas kernels for 10%

profile of v2, /device:TPU:0, one launch (start us, length us, event | category | flops | bytes accessed | tf_op | source)
XLA Modules:
  0.0 82.2 jit_solution(6053966032053233845)
XLA Ops:
  0.6 1.7 %shard_map.68 = bf16[16,32,512]{2,1,0:T(8,128)(2,1)} custom-call(bf16[32,256]{1,0:T(8,128)(2,1)} %teacher_ref.2, bf16[32,256]{1,0:T(8,128)(2,1)} %student_ref.5), custom_call_target="tpu_custom_call" | custom-call | tf_op jit(solution)/shard_map/pallas_call | solution.py:406
  2.4 8.3 %all-to-all-start = ((bf16[16,32,512]{2,1,0:T(8,128)(2,1)}), bf16[16,32,512]{2,1,0:T(8,128)(2,1)S(1)}, u32[]{:S(2)}, u32[]{:S(2)}) async-start(bf16[16,32,512]{2,1,0:T(8,128)(2,1)} %shard_map.68), calls=%async_computation | async-start | bytes 1048576 | tf_op jit(solution)/shard_map/all_to_all | solution.py:412
  10.7 0.8 convert_dynamic-update-slice_fusion
  11.5 2.8 %collective-permute-start = (f32[8,128]{1,0:T(8,128)S(1)}, f32[8,128]{1,0:T(8,128)S(1)}, u32[]{:S(2)}, u32[]{:S(2)}) collective-permute-start(f32[8,128]{1,0:T(8,128)S(1)} %bitcast.5), channel_id=1, source_target_pairs={{0,16},{16,0},{1,17},{17,1},{2,18},{18,2},{3,19},{19,3},{4,20},{20... | collective-permute-start | bytes 12296 | tf_op jit(solution)/shard_map/ppermute | solution.py:418
  14.3 4.1 %shard_map.69 = (bf16[2048,256]{1,0:T(8,128)(2,1)}, bf16[2048,256]{1,0:T(8,128)(2,1)}, f32[1,2048]{1,0:T(1,128)S(1)}) custom-call(s32[1]{0:T(128)} %bitcast.1.block_ref, bf16[256,16384]{1,0:T(8,128)(2,1)} %teacher_ref.3, bf16[256,16384]{1,0:T(8,128)(2,1)} %directions_ref.1), custom_call_target="tpu_custom_call" | custom-call | flops 6291456 | bytes 4194304 | tf_op jit(solution)/shard_map/pallas_call | solution.py:425
  18.4 6.9 %collective-permute-done = f32[8,128]{1,0:T(8,128)S(1)} collective-permute-done((f32[8,128]{1,0:T(8,128)S(1)}, f32[8,128]{1,0:T(8,128)S(1)}, u32[]{:S(2)}, u32[]{:S(2)}) %collective-permute-start) | collective-permute-done | bytes 4128 | tf_op jit(solution)/shard_map/ppermute | solution.py:418
  25.3 0.7 all-to-all-done.got_ref
  25.9 0.0 collective-permute-start.1
  25.9 0.1 pad_add_fusion.place_ref
  26.0 3.0 %shard_map.70 = (f32[2048,512]{1,0:T(8,128)S(1)}, f32[2048,512]{1,0:T(8,128)S(1)}, bf16[2048,256]{1,0:T(8,128)(2,1)S(1)}, bf16[2048,256]{1,0:T(8,128)(2,1)S(1)},...) custom-call(bf16[2048,256]{1,0:T(8,128)(2,1)} %get-tuple-element.25.teacher_hbm, ...), custom_call_target="tpu_custom_call" | custom-call | flops 1073741824 | tf_op jit(solution)/shard_map/pallas_call | solution.py:452
  29.0 0.0 collective-permute-done.1.got_ref
  29.1 3.2 %shard_map.71 = (f32[2048,512]{1,0:T(8,128)S(1)}, f32[2048,512]{1,0:T(8,128)S(1)}, bf16[16,16,128]{2,1,0:T(8,128)(2,1)S(1)}, f32[8,128]{1,0:T(8,128)S(1)}, bf16[256,512]{1,0:T(8,128)(2,1)S(1)}) custom-call(s32[3]{0:T(128)S(1)} %pad_add_fusion.place_ref, bf16[2048,256]{1,0:T(8,128)(2,1)S(1)} %get-tuple-element.29.teacher_w_ref, ...), custom_call_target="tpu_custom_call" | custom-call | flops 1073741824 | tf_op jit(solution)/shard_map/pallas_call | solution.py:466
  32.3 8.8 %all_to_all.25.got_ref.first_ref = bf16[16,16,128]{2,1,0:T(8,128)(2,1)S(1)} all-to-all(bf16[16,16,128]{2,1,0:T(8,128)(2,1)S(1)} %get-tuple-element.36), channel_id=1, replica_groups=mesh['group'=2,'block'=8,'fsdp'=2] {'block','fsdp'}, dimensions={0} | all-to-all | bytes 131072 | tf_op jit(solution)/shard_map/all_to_all | solution.py:402
  41.1 1.7 %shard_map.72 = bf16[16,16,128]{2,1,0:T(8,128)(2,1)S(1)} custom-call(s32[3]{0:T(128)S(1)} %pad_add_fusion.place_ref, f32[2048,512]{1,0:T(8,128)S(1)} %get-tuple-element.28.own_ref.own_mass_ref, f32[2048,512]{1,0:T(8,128)S(1)} %get-tuple-element.33.other_ref.other_mass_ref, bf16[16,16,128]{2,1,0:T(8,128)(2,1)S(1)} %all_to_all.25.got_ref.first_ref, ...), custom_call_target="tpu_custom_call" | custom-call | flops 8388608 | tf_op jit(solution)/shard_map/pallas_call | solution.py:479
  42.8 8.4 %all_to_all.26.got_ref.second_ref = bf16[16,16,128]{2,1,0:T(8,128)(2,1)S(1)} all-to-all(bf16[16,16,128]{2,1,0:T(8,128)(2,1)S(1)} %shard_map.72), channel_id=1, replica_groups=mesh['group'=2,'block'=8,'fsdp'=2] {'block','fsdp'}, dimensions={0} | all-to-all | bytes 131072 | tf_op jit(solution)/shard_map/all_to_all | solution.py:402
  51.2 1.8 %shard_map.73 = (bf16[16,8,128]{2,1,0:T(8,128)(2,1)S(1)}, f32[2048,1]{1,0:T(8,128)S(1)}, bf16[4,256,512]{2,1,0:T(8,128)(2,1)S(1)}) custom-call(s32[3]{0:T(128)S(1)} %pad_add_fusion.place_ref, f32[2048,512]{1,0:T(8,128)S(1)} %get-tuple-element.28.own_ref.own_mass_ref, f32[2048,512]{1,0:T(8,128)S(1)} %get-tuple-element.33.other_ref.other_mass_ref, ...), custom_call_target="tpu_custom_call" | custom-call | flops 8388608 | tf_op jit(solution)/shard_map/pallas_call | solution.py:486
  53.0 8.2 %all_to_all.27.third_ref = bf16[16,8,128]{2,1,0:T(8,128)(2,1)S(1)} all-to-all(bf16[16,8,128]{2,1,0:T(8,128)(2,1)S(1)} %get-tuple-element.39), channel_id=1, replica_groups=mesh['group'=2,'block'=8,'fsdp'=2] {'block','fsdp'}, dimensions={0} | all-to-all | bytes 65536 | tf_op jit(solution)/shard_map/all_to_all | solution.py:402
  61.2 4.0 %shard_map.74 = bf16[8,16,3072]{2,1,0:T(8,128)(2,1)S(1)} custom-call(s32[3]{0:T(128)S(1)} %pad_add_fusion.place_ref, f32[2048,512]{1,0:T(8,128)S(1)} %get-tuple-element.28.own_ref.own_mass_ref, f32[2048,512]{1,0:T(8,128)S(1)} %get-tuple-element.33.other_ref.other_mass_ref, f32[2048,512]{1,0:T(8,128)S(1)} %get-tuple-element.34.own_student_ref, ...), custom_call_target="tpu_custom_call" | custom-call | flops 2147483648 | tf_op jit(solution)/shard_map/pallas_call | solution.py:501
  65.3 0.0 copy-start
  65.3 14.8 %all_to_all.28.got_ref = bf16[8,16,3072]{2,1,0:T(8,128)(2,1)S(1)} all-to-all(bf16[8,16,3072]{2,1,0:T(8,128)(2,1)S(1)} %shard_map.74), channel_id=1, replica_groups=mesh['group'=2,'block'=8,'fsdp'=2] {'block'}, dimensions={0} | all-to-all | bytes 1572864 | tf_op jit(solution)/shard_map/all_to_all | solution.py:515
  80.2 0.1 collective-permute-start.2
  80.2 1.0 %shard_map.75 = f32[16,16384]{1,0:T(8,128)} custom-call(bf16[8,16,3072]{2,1,0:T(8,128)(2,1)S(1)} %all_to_all.28.got_ref), custom_call_target="tpu_custom_call" | custom-call | tf_op jit(solution)/shard_map/pallas_call | solution.py:523
  81.3 0.2 collective-permute-done.2.other_ref
  81.4 0.0 copy-done
  81.4 0.8 shard_map.77
  (3 shorter events, 0.0 us)
Async XLA Ops:
  2.4 23.6 %all-to-all-start = ((bf16[16,32,512]{2,1,0:T(8,128)(2,1)}), bf16[16,32,512]{2,1,0:T(8,128)(2,1)S(1)}, u32[]{:S(2)}, u32[]{:S(2)}) async-start(bf16[16,32,512]{2,1,0:T(8,128)(2,1)} %shard_map.68), calls=%async_computation | async-start | bytes 1048576 | tf_op jit(solution)/shard_map/all_to_all | solution.py:412
  11.5 13.8 %collective-permute-start = (f32[8,128]{1,0:T(8,128)S(1)}, f32[8,128]{1,0:T(8,128)S(1)}, u32[]{:S(2)}, u32[]{:S(2)}) collective-permute-start(f32[8,128]{1,0:T(8,128)S(1)} %bitcast.5), channel_id=1, source_target_pairs={{0,16},{16,0},{1,17},{17,1},{2,18},{18,2},{3,19},{19,3},{4,20},{20... | collective-permute-start | bytes 12296 | tf_op jit(solution)/shard_map/ppermute | solution.py:418
  25.9 3.1 %collective-permute-start.1 = (bf16[16,32,512]{2,1,0:T(8,128)(2,1)S(1)}, bf16[16,32,512]{2,1,0:T(8,128)(2,1)S(1)}, u32[]{:S(2)}, u32[]{:S(2)}) collective-permute-start(bf16[16,32,512]{2,1,0:T(8,128)(2,1)S(1)} %all-to-all-done.got_ref), channel_id=1, source_target_pairs={{0,1},{1,0},{2,3},{3,2},{4,5},{5,4},{6,7},{7,6},{8,9},{9,8},{10,11... | collective-permute-start | bytes 1572872 | tf_op jit(solution)/shard_map/ppermute | solution.py:399
  65.3 16.2 %copy-start = (bf16[32,256]{1,0:T(8,128)(2,1)S(1)}, bf16[32,256]{1,0:T(8,128)(2,1)}, u32[]{:S(2)}) copy-start(bf16[32,256]{1,0:T(8,128)(2,1)} %student_ref.5) | copy-start | bytes 49156
  80.2 1.3 %collective-permute-start.2 = (f32[32,256]{1,0:T(8,128)S(1)}, f32[32,256]{1,0:T(8,128)S(1)}, u32[]{:S(2)}, u32[]{:S(2)}) collective-permute-start(f32[32,256]{1,0:T(8,128)S(1)} %get-tuple-element.45), channel_id=1, source_target_pairs={{0,1},{1,0},{2,3},{3,2},{4,5},{5,4},{6,7},{7,6},{8,9},{9,8},{10,11... | collective-permute-start | bytes 98312 | tf_op jit(solution)/shard_map/ppermute | solution.py:399

commit v3 on v2

--- a/solution.py
+++ b/solution.py
@@ -180,21 +180,31 @@
     return jnp.concatenate([rows[at : at + 1, :] for at in range(rows.shape[0])], axis=1)
 
 
-def by_core(core, own, other):
-    return jnp.concatenate([jnp.where(core == 0, own, other), jnp.where(core == 0, other, own)], axis=0)
-
-
-def halves(core, rows):
-    half = rows.shape[0] // 2
-    first, second = rows[:half], rows[half:]
-    return as_line(jnp.where(core == 0, first, second)), as_line(jnp.where(core == 0, second, first))
-
-
-def send(sent_ref, core, own, other, *more):
-    own, other = (as_rows(jnp.sum(total, axis=0, keepdims=True)) for total in (own, other))
-    values = jnp.concatenate([by_core(core, own, other), *more], axis=0).astype(jnp.bfloat16)
+def in_core_order(core, own, other, body):
+    @pl.when(core == 0)
+    def _():
+        body(own, other)
+
+    @pl.when(core == 1)
+    def _():
+        body(other, own)
+
+
+def sums(first, second):
+    lines = [as_rows(jnp.sum(total, axis=0, keepdims=True)) for total in (first, second)]
+    return jnp.concatenate(lines, axis=0)
+
+
+def send(sent_ref, *rows):
+    values = jnp.concatenate(rows, axis=0).astype(jnp.bfloat16)
     for device in range(sent_ref.shape[0]):
         sent_ref[device] = values
+
+
+def halves(rows):
+    line = as_line(rows)
+    half = line.shape[1] // 2
+    return line[:, :half], line[:, half:]
 
 
 def received(got_ref):
@@ -263,27 +273,32 @@
         mass = exponentials(student_w_ref[here, :], student, student_temp)
         student_ref[here, :] = mass
         part = part + fold(mass)
-    send(sent_ref, core, own_total, total, weight_ref[...])
-    own_part = as_rows(jnp.sum(own_part_ref[...], axis=0, keepdims=True))
-    part_ref[...] = by_core(core, own_part, as_rows(jnp.sum(part, axis=0, keepdims=True)))
-
-
-def sweep(prototypes, crops, place_ref, own_ref, other_ref, got_ref):
-    own_crop, other_crop = halves(place_ref[2], 1.0 / (crops * received(got_ref)[: crops // LANES]))
-    own_total = other_total = 0.0
+
+    def finish(first, second):
+        send(sent_ref, sums(first[0], second[0]), weight_ref[...])
+        part_ref[...] = sums(first[1], second[1])
+
+    in_core_order(core, (own_total, own_part_ref[...]), (total, part), finish)
+
+
+def sweep(prototypes, crops, first_ref, second_ref, got_ref):
+    first_crop, second_crop = halves(1.0 / (crops * received(got_ref)[: crops // LANES]))
+    first_total = second_total = 0.0
     scales = []
-    for start in range(0, own_ref.shape[0], TILE):
-        own, other = own_ref[start : start + TILE, :], other_ref[start : start + TILE, :]
-        proto = jnp.sum(own * own_crop + other * other_crop, axis=1, keepdims=True)
+    for start in range(0, first_ref.shape[0], TILE):
+        first, second = first_ref[start : start + TILE, :], second_ref[start : start + TILE, :]
+        proto = jnp.sum(first * first_crop + second * second_crop, axis=1, keepdims=True)
         scales.append(1.0 / (prototypes * proto))
-        own_total = own_total + fold(own * scales[-1])
-        other_total = other_total + fold(other * scales[-1])
-    return own_total, other_total, scales
+        first_total = first_total + fold(first * scales[-1])
+        second_total = second_total + fold(second * scales[-1])
+    return sums(first_total, second_total), scales
 
 
 def sweep_kernel(prototypes, crops, place_ref, own_ref, other_ref, got_ref, part_ref, sent_ref):
-    own, other, _ = sweep(prototypes, crops, place_ref, own_ref, other_ref, got_ref)
-    send(sent_ref, place_ref[2], own, other, part_ref[...])
+    def body(first_ref, second_ref):
+        send(sent_ref, sweep(prototypes, crops, first_ref, second_ref, got_ref)[0], part_ref[...])
+
+    in_core_order(place_ref[2], own_ref, other_ref, body)
 
 
 def last_sweep_kernel(
@@ -295,86 +310,99 @@
         columns = pl.ds(pl.multiple_of((place_ref[1] * pieces + piece) * span, span), span)
         copies.append(pltpu.make_async_copy(directions_ref.at[:, columns], copy_ref.at[piece], sems.at[piece]))
         copies[-1].start()
-    own, other, scales = sweep(prototypes, crops, place_ref, own_ref, other_ref, got_ref)
-    for index, scale in enumerate(scales):
-        scale_ref[index * TILE : (index + 1) * TILE, :] = scale
-    send(sent_ref, place_ref[2], own, other)
+
+    def body(first_ref, second_ref):
+        total, scales = sweep(prototypes, crops, first_ref, second_ref, got_ref)
+        for index, scale in enumerate(scales):
+            scale_ref[index * TILE : (index + 1) * TILE, :] = scale
+        send(sent_ref, total)
+
+    in_core_order(place_ref[2], own_ref, other_ref, body)
     for copy in copies:
         copy.wait()
 
 
+def units_tile(copy_ref, inverse_ref, start):
+    span = copy_ref.shape[2]
+    at = start % span
+    return copy_ref[start // span, :, at : at + TILE].astype(jnp.float32) * inverse_ref[:, start : start + TILE]
+
+
 def gradient_kernel(
     place_ref, own_mass_ref, other_mass_ref, own_student_ref, other_student_ref, scale_ref, first_ref, second_ref, third_ref,
-    own_turned_ref, other_turned_ref, inverse_ref, copy_ref, sent_ref, gradient_ref, grad_ref, unit_ref,
+    inverse_ref, copy_ref, gradient_ref, keep_ref, give_ref, unit_ref,
 ):
     group, core = place_ref[0], place_ref[2]
-    chips, rows_each, _ = sent_ref.shape
     count, half = own_mass_ref.shape
-    width = own_turned_ref.shape[0]
-    span = copy_ref.shape[2]
     lines = 2 * half // LANES
     weights = received(first_ref)[lines:] / student_temp
-    teacher_scales = halves(core, weights / received(third_ref))
-    student_scales = halves(core, weights / received(second_ref)[lines:])
-    masses, students = (own_mass_ref, other_mass_ref), (own_student_ref, other_student_ref)
-    own_rows = pl.ds(pl.multiple_of(group * (width // GROUPS), width // GROUPS), width // GROUPS)
+    teacher_scales = halves(weights / received(third_ref))
+    student_scales = halves(weights / received(second_ref)[lines:])
+
+    def body(first_refs, second_refs):
+        for start in range(0, count, TILE):
+            here = slice(start, start + TILE)
+            for (side, mass_ref, student_ref), teacher_scale, student_scale in zip(
+                (first_refs, second_refs), teacher_scales, student_scales
+            ):
+                teacher = mass_ref[here, :] * scale_ref[here, :] * teacher_scale
+                gradient = student_ref[here, :] * student_scale - teacher
+                gradient_ref[side, start : start + TILE, :] = gradient.astype(jnp.bfloat16)
+
+    in_core_order(core, (0, own_mass_ref, own_student_ref), (1, other_mass_ref, other_student_ref), body)
+    for start in range(0, count, TILE):
+        unit_ref[:, start : start + TILE] = units_tile(copy_ref, inverse_ref, start).astype(jnp.bfloat16)
     kept = half // GROUPS
+    lanes = pl.ds(pl.multiple_of(group * kept, kept), kept)
+    for side, out_ref in enumerate((keep_ref, give_ref)):
+        feature = jnp.dot(unit_ref[...], gradient_ref[side, :, lanes], preferred_element_type=jnp.float32)
+        out_ref[...] = jnp.transpose(feature).astype(out_ref.dtype)
+
+
+def weight_kernel(place_ref, gradient_ref, own_turned_ref, other_turned_ref, inverse_ref, copy_ref, sent_ref, grad_ref):
+    chips, rows_each, _ = sent_ref.shape
+    count = gradient_ref.shape[1]
+    width = own_turned_ref.shape[0]
+    own_rows = pl.ds(pl.multiple_of(place_ref[0] * (width // GROUPS), width // GROUPS), width // GROUPS)
     for start in range(0, count, TILE):
         here, slot = slice(start, start + TILE), start // TILE
-        piece = slice(start % span, start % span + TILE)
-        inverse = inverse_ref[:, here]
-        unit = copy_ref[start // span, :, piece].astype(jnp.float32) * inverse
-        for side in range(2):
-            teacher = masses[side][here, :] * scale_ref[here, :] * teacher_scales[side]
-            gradient = students[side][here, :] * student_scales[side] - teacher
-            gradient_ref[slot, side] = gradient.astype(jnp.bfloat16)
         weight_grad = 0.0
         for side, turned_ref in enumerate((own_turned_ref, other_turned_ref)):
             weight_grad = weight_grad + lax.dot_general(
-                turned_ref[...], gradient_ref[slot, side], (((1,), (1,)), ((), ())), preferred_element_type=jnp.float32
+                turned_ref[...], gradient_ref[side, here, :], (((1,), (1,)), ((), ())), preferred_element_type=jnp.float32
             )
+        unit = units_tile(copy_ref, inverse_ref, start)
         dot = jnp.sum(unit * weight_grad, axis=0, keepdims=True)
-        grad_ref[slot] = (weight_grad - unit * dot) * inverse
+        grad_ref[slot] = (weight_grad - unit * dot) * inverse_ref[:, here]
         own = grad_ref[slot, own_rows, :].astype(jnp.bfloat16)
         sent_ref[:, :, here] = own.reshape(chips, rows_each, TILE)
-        unit_ref[:, here] = unit.astype(jnp.bfloat16)
-
-    per_core = kept // chips
-    pieces = per_core // rows_each
-    for side in range(2):
-        lanes = pl.ds(pl.multiple_of(group * kept, kept), kept)
-        gradient = gradient_ref[:, side, :, lanes].reshape(count, kept)
-        feature = jnp.dot(unit_ref[...], gradient, preferred_element_type=jnp.float32)
-        feature = jnp.transpose(feature).astype(jnp.bfloat16)
-        for chip in range(chips):
-            for piece in range(pieces):
-                start = chip * per_core + piece * rows_each
-                at = count + (side * pieces + piece) * width
-                sent_ref[chip, :, at : at + width] = feature[start : start + rows_each, :]
-
-
-def collect_kernel(got_ref, keep_ref, give_ref):
-    rows_each = got_ref.shape[1]
-    rows, width = keep_ref.shape
-    total = got_ref[0].astype(jnp.float32)
-    for chip in range(1, got_ref.shape[0]):
-        total = total + got_ref[chip].astype(jnp.float32)
+
+
+def pack_kernel(keep_ref, other_ref, _, sent_ref, packed_ref, sem):
+    chips, rows_each, lanes = packed_ref.shape
+    width = keep_ref.shape[1]
+    total = (keep_ref[...] + other_ref[...].astype(jnp.float32)).astype(jnp.bfloat16)
+    total = total.reshape(chips, -1, width)
+    for piece in range(lanes // width):
+        packed_ref[:, :, piece * width : (piece + 1) * width] = total[:, piece * rows_each : (piece + 1) * rows_each, :]
+    copy = pltpu.make_async_copy(packed_ref, sent_ref.at[:, :, pl.ds(sent_ref.shape[2] - lanes, lanes)], sem)
+    copy.start()
+    copy.wait()
+
+
+def outputs_kernel(got_ref, student_ref, weight_out, feature_out):
+    chips, rows_each, columns = got_ref.shape
+    rows, width = student_ref.shape
     pieces = rows // rows_each
-    for piece in range(2 * pieces):
-        out_ref, at = (keep_ref, piece) if piece < pieces else (give_ref, piece - pieces)
-        out_ref[at * rows_each : (at + 1) * rows_each, :] = total[:, piece * width : (piece + 1) * width]
-
-
-def feature_kernel(keep_ref, other_ref, student_ref, out_ref):
-    total = keep_ref[...] + other_ref[...]
+    count = columns - pieces * width
+    total = got_ref[0, :, count:].astype(jnp.float32)
+    for chip in range(1, chips):
+        total = total + got_ref[chip, :, count:].astype(jnp.float32)
+    total = jnp.concatenate([total[:, piece * width : (piece + 1) * width] for piece in range(pieces)], axis=0)
     hat, length = unit_rows(student_ref[...])
-    out_ref[...] = (total - hat * jnp.sum(hat * total, axis=1, keepdims=True)) / length
-
-
-def widen_kernel(got_ref, out_ref):
-    chips, _, columns = got_ref.shape
+    feature_out[...] = (total - hat * jnp.sum(hat * total, axis=1, keepdims=True)) / length
     for chip in range(chips):
-        out_ref[:, chip * columns : (chip + 1) * columns] = got_ref[chip].astype(jnp.float32)
+        weight_out[:, chip * count : (chip + 1) * count] = got_ref[chip, :, :count].astype(jnp.float32)
 
 
 def kernel_body(teacher_feat, student_feat, crop_weight, teacher_v, student_v):
@@ -496,38 +524,35 @@
     )(place, own_mass, other_mass, second, hbm(student_v))
     third = share(sent)
 
+    gradient, keep, give = call(
+        gradient_kernel,
+        (shape((2, count, half), bf16), shape((half // GROUPS, width), f32), shape((half // GROUPS, width), bf16)),
+        flops=2 * elements * width // GROUPS,
+        in_specs=[smem] + [vmem] * 10,
+        scratch_shapes=[pltpu.VMEM((width, count), bf16)],
+    )(place, own_mass, other_mass, own_student, other_student, scale, first, second, third, inverse, student_copy)
+    other = swap(give)
     out_rows = width // chips
-    per_chip = rows * fsdp * width // out_rows
+    per_chip = rows * width // out_rows
     sent = call(
-        gradient_kernel,
+        weight_kernel,
         shape((blocks, out_rows, count + per_chip), bf16),
-        flops=4 * elements * width,
-        in_specs=[smem] + [vmem] * 12,
-        scratch_shapes=[
-            pltpu.VMEM((count // TILE, 2, TILE, half), bf16),
-            pltpu.VMEM((count // TILE, width, TILE), f32),
-            pltpu.VMEM((width, count), bf16),
-        ],
-    )(
-        place, own_mass, other_mass, own_student, other_student, scale, first, second, third,
-        own_turned, other_turned, inverse, student_copy,
-    )
+        flops=2 * elements * width,
+        in_specs=[smem] + [vmem] * 5,
+        scratch_shapes=[pltpu.VMEM((count // TILE, width, TILE), f32)],
+    )(place, gradient, own_turned, other_turned, inverse, student_copy)
+    sent = call(
+        pack_kernel,
+        shape((blocks, out_rows, count + per_chip), bf16),
+        in_specs=[vmem] * 2 + [anyspace],
+        out_specs=anyspace,
+        input_output_aliases={2: 0},
+        scratch_shapes=[pltpu.VMEM((blocks, out_rows, per_chip), bf16), dma],
+    )(keep, other, sent)
     got = lax.all_to_all(sent, "block", 0, 0)
-    keep, give = call(
-        collect_kernel,
-        [shape((rows, width), f32)] * 2,
-        grid=(1,),
-        in_specs=[pl.BlockSpec((blocks, out_rows, per_chip), lambda step: (0, 0, count // per_chip))],
-    )(got)
-    grad_feat = call(feature_kernel, shape((rows, width), f32))(keep, swap(give), student_feat)
-    grad_v = call(
-        widen_kernel,
-        shape((out_rows, kept), f32),
-        grid=(1,),
-        in_specs=[pl.BlockSpec((blocks, out_rows, count), lambda step: (0, 0, 0))],
-        out_specs=pl.BlockSpec((out_rows, kept), lambda step: (0, 0)),
-    )(got)
-    return (grad_v, grad_feat)
+    return call(
+        outputs_kernel, (shape((out_rows, kept), f32), shape((rows, width), f32))
+    )(got, student_feat)
 
 
 def solution(mesh):

time: 82.8 us -> 82.2 us (level)
  transfers between devices with their start and end apart: 4 -> 4, of which waited for: 3 -> 2; matrix products, arithmetic and copies ran while one was open for 1% -> 1% of each run, Pallas kernels for 10% -> 11%
where the time goes in v3:
time: 82.2 us; the launch traced here: 81.7 us
  blocking collectives  39.8 us (48%)
  Pallas kernels  21.6 us (26%)
  starting transfers between devices  11.2 us (14%)
  waiting for transfers between devices  7.54 us (9%)
  other arithmetic  0.85 us (1%)
    all_to_all x3, blocking collectives, share(): return lax.all_to_all(values, GROUP, 0, 0)  25.5 us
    all_to_all x1, blocking collectives, kernel_body(): got = lax.all_to_all(sent, 'block', 0, 0)  14.3 us
    all_to_all x1, starting transfers between devices, kernel_body(): own = lax.all_to_all(sent, CHIPS, 0, 0)  8.32 us
    ppermute x1, waiting for transfers between devices, kernel_body(): lax.ppermute(weights, 'group', [(at, (at + move) % GROUPS) for at in rang...  6.88 us
    pallas_call x1, Pallas kernels, kernel_body(): call(directions_kernel, (pltpu.HBM((count, width), bf16), pltpu.HBM((coun...  4.08 us
    pallas_call x1, Pallas kernels, kernel_body(): call(gradient_kernel, (shape((2, count, half), bf16), shape((half // GROU...  3.02 us
    pallas_call x1, Pallas kernels, kernel_body(): call(own_kernel, (shape((count, half), f32), shape((count, half), f32), s...  3.02 us
    pallas_call x1, Pallas kernels, kernel_body(): call(functools.partial(other_kernel, prototypes), (shape((count, half), f...  2.88 us
  transfers between devices with their start and end apart: 4, of which 2 were waited for; matrix products, arithmetic and copies ran while one was open for 1% of the time, Pallas kernels for 11%

profile of v3, /device:TPU:0, one launch (start us, length us, event | category | flops | bytes accessed | tf_op | source)
XLA Modules:
  0.0 81.7 jit_solution(17856245323671973311)
XLA Ops:
  0.6 1.7 %shard_map.68 = bf16[16,32,512]{2,1,0:T(8,128)(2,1)} custom-call(bf16[32,256]{1,0:T(8,128)(2,1)} %teacher_ref.2, bf16[32,256]{1,0:T(8,128)(2,1)} %student_ref.5), custom_call_target="tpu_custom_call" | custom-call | tf_op jit(solution)/shard_map/pallas_call | solution.py:434
  2.4 8.3 %all-to-all-start = ((bf16[16,32,512]{2,1,0:T(8,128)(2,1)}), bf16[16,32,512]{2,1,0:T(8,128)(2,1)S(1)}, u32[]{:S(2)}, u32[]{:S(2)}) async-start(bf16[16,32,512]{2,1,0:T(8,128)(2,1)} %shard_map.68), calls=%async_computation | async-start | bytes 1048576 | tf_op jit(solution)/shard_map/all_to_all | solution.py:440
  10.7 0.8 convert_dynamic-update-slice_fusion
  11.5 2.8 %collective-permute-start = (f32[8,128]{1,0:T(8,128)S(1)}, f32[8,128]{1,0:T(8,128)S(1)}, u32[]{:S(2)}, u32[]{:S(2)}) collective-permute-start(f32[8,128]{1,0:T(8,128)S(1)} %bitcast.5), channel_id=1, source_target_pairs={{0,16},{16,0},{1,17},{17,1},{2,18},{18,2},{3,19},{19,3},{4,20},{20... | collective-permute-start | bytes 12296 | tf_op jit(solution)/shard_map/ppermute | solution.py:446
  14.3 4.1 %shard_map.69 = (bf16[2048,256]{1,0:T(8,128)(2,1)}, bf16[2048,256]{1,0:T(8,128)(2,1)}, f32[1,2048]{1,0:T(1,128)S(1)}) custom-call(s32[1]{0:T(128)} %bitcast.1.block_ref, bf16[256,16384]{1,0:T(8,128)(2,1)} %teacher_ref.3, bf16[256,16384]{1,0:T(8,128)(2,1)} %directions_ref.1), custom_call_target="tpu_custom_call" | custom-call | flops 6291456 | bytes 4194304 | tf_op jit(solution)/shard_map/pallas_call | solution.py:453
  18.4 6.9 %collective-permute-done = f32[8,128]{1,0:T(8,128)S(1)} collective-permute-done((f32[8,128]{1,0:T(8,128)S(1)}, f32[8,128]{1,0:T(8,128)S(1)}, u32[]{:S(2)}, u32[]{:S(2)}) %collective-permute-start) | collective-permute-done | bytes 4128 | tf_op jit(solution)/shard_map/ppermute | solution.py:446
  25.3 0.7 all-to-all-done.got_ref
  25.9 0.0 collective-permute-start.1
  25.9 0.1 pad_add_fusion.place_ref
  26.0 3.0 %shard_map.70 = (f32[2048,512]{1,0:T(8,128)S(1)}, f32[2048,512]{1,0:T(8,128)S(1)}, bf16[2048,256]{1,0:T(8,128)(2,1)S(1)}, bf16[2048,256]{1,0:T(8,128)(2,1)S(1)},...) custom-call(bf16[2048,256]{1,0:T(8,128)(2,1)} %get-tuple-element.26.teacher_hbm, ...), custom_call_target="tpu_custom_call" | custom-call | flops 1073741824 | tf_op jit(solution)/shard_map/pallas_call | solution.py:480
  29.0 0.0 collective-permute-done.1.got_ref
  29.1 2.9 %shard_map.71 = (f32[2048,512]{1,0:T(8,128)S(1)}, f32[2048,512]{1,0:T(8,128)S(1)}, bf16[16,16,128]{2,1,0:T(8,128)(2,1)S(1)}, f32[8,128]{1,0:T(8,128)S(1)}, bf16[256,512]{1,0:T(8,128)(2,1)S(1)}) custom-call(s32[3]{0:T(128)S(1)} %pad_add_fusion.place_ref, bf16[2048,256]{1,0:T(8,128)(2,1)S(1)} %get-tuple-element.30.teacher_w_ref, ...), custom_call_target="tpu_custom_call" | custom-call | flops 1073741824 | tf_op jit(solution)/shard_map/pallas_call | solution.py:494
  31.9 8.8 %all_to_all.25.got_ref.first_ref = bf16[16,16,128]{2,1,0:T(8,128)(2,1)S(1)} all-to-all(bf16[16,16,128]{2,1,0:T(8,128)(2,1)S(1)} %get-tuple-element.37), channel_id=1, replica_groups=mesh['group'=2,'block'=8,'fsdp'=2] {'block','fsdp'}, dimensions={0} | all-to-all | bytes 131072 | tf_op jit(solution)/shard_map/all_to_all | solution.py:430
  40.8 1.7 %shard_map.72 = bf16[16,16,128]{2,1,0:T(8,128)(2,1)S(1)} custom-call(s32[3]{0:T(128)S(1)} %pad_add_fusion.place_ref, f32[2048,512]{1,0:T(8,128)S(1)} %get-tuple-element.29.own_ref.own_mass_ref, f32[2048,512]{1,0:T(8,128)S(1)} %get-tuple-element.34.other_ref.other_mass_ref, bf16[16,16,128]{2,1,0:T(8,128)(2,1)S(1)} %all_to_all.25.got_ref.first_ref, ...), custom_call_target="tpu_custom_call" | custom-call | flops 8388608 | tf_op jit(solution)/shard_map/pallas_call | solution.py:507
  42.5 8.4 %all_to_all.26.got_ref.second_ref = bf16[16,16,128]{2,1,0:T(8,128)(2,1)S(1)} all-to-all(bf16[16,16,128]{2,1,0:T(8,128)(2,1)S(1)} %shard_map.72), channel_id=1, replica_groups=mesh['group'=2,'block'=8,'fsdp'=2] {'block','fsdp'}, dimensions={0} | all-to-all | bytes 131072 | tf_op jit(solution)/shard_map/all_to_all | solution.py:430
  50.9 1.8 %shard_map.73 = (bf16[16,8,128]{2,1,0:T(8,128)(2,1)S(1)}, f32[2048,1]{1,0:T(8,128)S(1)}, bf16[4,256,512]{2,1,0:T(8,128)(2,1)S(1)}) custom-call(s32[3]{0:T(128)S(1)} %pad_add_fusion.place_ref, f32[2048,512]{1,0:T(8,128)S(1)} %get-tuple-element.29.own_ref.own_mass_ref, f32[2048,512]{1,0:T(8,128)S(1)} %get-tuple-element.34.other_ref.other_mass_ref, ...), custom_call_target="tpu_custom_call" | custom-call | flops 8388608 | tf_op jit(solution)/shard_map/pallas_call | solution.py:514
  52.7 8.2 %all_to_all.27.third_ref = bf16[16,8,128]{2,1,0:T(8,128)(2,1)S(1)} all-to-all(bf16[16,8,128]{2,1,0:T(8,128)(2,1)S(1)} %get-tuple-element.40), channel_id=1, replica_groups=mesh['group'=2,'block'=8,'fsdp'=2] {'block','fsdp'}, dimensions={0} | all-to-all | bytes 65536 | tf_op jit(solution)/shard_map/all_to_all | solution.py:430
  60.9 3.0 %shard_map.74 = (bf16[2,2048,512]{2,1,0:T(8,128)(2,1)S(1)}, f32[256,256]{1,0:T(8,128)S(1)}, bf16[256,256]{1,0:T(8,128)(2,1)S(1)}) custom-call(s32[3]{0:T(128)S(1)} %pad_add_fusion.place_ref, f32[2048,512]{1,0:T(8,128)S(1)} %get-tuple-element.29.own_ref.own_mass_ref, f32[2048,512]{1,0:T(8,128)S(1)} %get-tuple-element.34.other_ref.other_mass_ref, ...), custom_call_target="tpu_custom_call" | custom-call | flops 536870912 | tf_op jit(solution)/shard_map/pallas_call | solution.py:527
  63.9 0.1 collective-permute-start.2
  64.0 0.0 copy-start
  64.0 2.1 %shard_map.75._ = bf16[8,16,2560]{2,1,0:T(8,128)(2,1)S(1)} custom-call(s32[3]{0:T(128)S(1)} %pad_add_fusion.place_ref, bf16[2,2048,512]{2,1,0:T(8,128)(2,1)S(1)} %get-tuple-element.45.gradient_ref, bf16[256,512]{1,0:T(8,128)(2,1)S(1)} %get-tuple-element.46.own_turned_ref, bf16[256,512]{1,0:T(8,128)(2,1)S(1)} %get-tuple-element.47.other_turned_ref, ...), custom_call_target="tpu_custom_call" | custom-call | flops 1073741824 | tf_op jit(solution)/shard_map/pallas_call | solution.py:537
  66.2 0.0 collective-permute-done.2.other_ref
  66.2 0.1 shard_map.76
  66.2 14.3 %all_to_all.28.got_ref = bf16[8,16,2560]{2,1,0:T(8,128)(2,1)S(1)} all-to-all(bf16[8,16,2560]{2,1,0:T(8,128)(2,1)S(1)} %shard_map.76), channel_id=1, replica_groups=mesh['group'=2,'block'=8,'fsdp'=2] {'block'}, dimensions={0} | all-to-all | bytes 1310720 | tf_op jit(solution)/shard_map/all_to_all | solution.py:552
  80.6 0.0 copy-done
  80.6 1.1 %shard_map.77 = (f32[16,16384]{1,0:T(8,128)}, f32[32,256]{1,0:T(8,128)}) custom-call(bf16[8,16,2560]{2,1,0:T(8,128)(2,1)S(1)} %all_to_all.28.got_ref, bf16[32,256]{1,0:T(8,128)(2,1)S(1)} %copy-done), custom_call_target="tpu_custom_call" | custom-call | tf_op jit(solution)/shard_map/pallas_call | solution.py:553
  (2 shorter events, 0.0 us)
Async XLA Ops:
  2.4 23.6 %all-to-all-start = ((bf16[16,32,512]{2,1,0:T(8,128)(2,1)}), bf16[16,32,512]{2,1,0:T(8,128)(2,1)S(1)}, u32[]{:S(2)}, u32[]{:S(2)}) async-start(bf16[16,32,512]{2,1,0:T(8,128)(2,1)} %shard_map.68), calls=%async_computation | async-start | bytes 1048576 | tf_op jit(solution)/shard_map/all_to_all | solution.py:440
  11.5 13.8 %collective-permute-start = (f32[8,128]{1,0:T(8,128)S(1)}, f32[8,128]{1,0:T(8,128)S(1)}, u32[]{:S(2)}, u32[]{:S(2)}) collective-permute-start(f32[8,128]{1,0:T(8,128)S(1)} %bitcast.5), channel_id=1, source_target_pairs={{0,16},{16,0},{1,17},{17,1},{2,18},{18,2},{3,19},{19,3},{4,20},{20... | collective-permute-start | bytes 12296 | tf_op jit(solution)/shard_map/ppermute | solution.py:446
  25.9 3.1 %collective-permute-start.1 = (bf16[16,32,512]{2,1,0:T(8,128)(2,1)S(1)}, bf16[16,32,512]{2,1,0:T(8,128)(2,1)S(1)}, u32[]{:S(2)}, u32[]{:S(2)}) collective-permute-start(bf16[16,32,512]{2,1,0:T(8,128)(2,1)S(1)} %all-to-all-done.got_ref), channel_id=1, source_target_pairs={{0,1},{1,0},{2,3},{3,2},{4,5},{5,4},{6,7},{7,6},{8,9},{9,8},{10,11... | collective-permute-start | bytes 1572872 | tf_op jit(solution)/shard_map/ppermute | solution.py:427
  63.9 2.2 %collective-permute-start.2 = (bf16[256,256]{1,0:T(8,128)(2,1)S(1)}, bf16[256,256]{1,0:T(8,128)(2,1)S(1)}, u32[]{:S(2)}, u32[]{:S(2)}) collective-permute-start(bf16[256,256]{1,0:T(8,128)(2,1)S(1)} %get-tuple-element.44), channel_id=1, source_target_pairs={{0,1},{1,0},{2,3},{3,2},{4,5},{5,4},{6,7},{7,6},{8,9},{9,8},{10,11... | collective-permute-start | bytes 393224 | tf_op jit(solution)/shard_map/ppermute | solution.py:427
  64.0 16.6 %copy-start = (bf16[32,256]{1,0:T(8,128)(2,1)S(1)}, bf16[32,256]{1,0:T(8,128)(2,1)}, u32[]{:S(2)}) copy-start(bf16[32,256]{1,0:T(8,128)(2,1)} %student_ref.5) | copy-start | bytes 49156

commit v4 on v3

--- a/solution.py
+++ b/solution.py
@@ -253,11 +253,11 @@
 
 
 def other_kernel(
-    prototypes, place_ref, teacher_w_ref, student_w_ref, got_ref, own_ref, own_part_ref, weight_ref,
+    prototypes, teacher_w_ref, student_w_ref, got_ref, own_ref, own_part_ref, weight_ref,
     teacher_ref, student_ref, sent_ref, part_ref, turned_ref,
 ):
     count, width = teacher_w_ref.shape
-    core = place_ref[2]
+    core = lax.axis_index("fsdp")
     teacher, student = units_of(got_ref, width, 0), units_of(got_ref, width, 1)
     turned_ref[...] = turn(student)
     own_total = total = part = 0.0
@@ -294,20 +294,20 @@
     return sums(first_total, second_total), scales
 
 
-def sweep_kernel(prototypes, crops, place_ref, own_ref, other_ref, got_ref, part_ref, sent_ref):
+def sweep_kernel(prototypes, crops, own_ref, other_ref, got_ref, part_ref, sent_ref):
     def body(first_ref, second_ref):
         send(sent_ref, sweep(prototypes, crops, first_ref, second_ref, got_ref)[0], part_ref[...])
 
-    in_core_order(place_ref[2], own_ref, other_ref, body)
+    in_core_order(lax.axis_index("fsdp"), own_ref, other_ref, body)
 
 
 def last_sweep_kernel(
-    prototypes, crops, place_ref, own_ref, other_ref, got_ref, directions_ref, sent_ref, scale_ref, copy_ref, sems
+    prototypes, crops, own_ref, other_ref, got_ref, directions_ref, sent_ref, scale_ref, copy_ref, sems
 ):
     pieces, _, span = copy_ref.shape
     copies = []
     for piece in range(pieces):
-        columns = pl.ds(pl.multiple_of((place_ref[1] * pieces + piece) * span, span), span)
+        columns = pl.ds(pl.multiple_of((lax.axis_index("block") * pieces + piece) * span, span), span)
         copies.append(pltpu.make_async_copy(directions_ref.at[:, columns], copy_ref.at[piece], sems.at[piece]))
         copies[-1].start()
 
@@ -317,7 +317,7 @@
             scale_ref[index * TILE : (index + 1) * TILE, :] = scale
         send(sent_ref, total)
 
-    in_core_order(place_ref[2], own_ref, other_ref, body)
+    in_core_order(lax.axis_index("fsdp"), own_ref, other_ref, body)
     for copy in copies:
         copy.wait()
 
@@ -329,10 +329,10 @@
 
 
 def gradient_kernel(
-    place_ref, own_mass_ref, other_mass_ref, own_student_ref, other_student_ref, scale_ref, first_ref, second_ref, third_ref,
+    own_mass_ref, other_mass_ref, own_student_ref, other_student_ref, scale_ref, first_ref, second_ref, third_ref,
     inverse_ref, copy_ref, gradient_ref, keep_ref, give_ref, unit_ref,
 ):
-    group, core = place_ref[0], place_ref[2]
+    group, core = lax.axis_index("group"), lax.axis_index("fsdp")
     count, half = own_mass_ref.shape
     lines = 2 * half // LANES
     weights = received(first_ref)[lines:] / student_temp
@@ -359,11 +359,12 @@
         out_ref[...] = jnp.transpose(feature).astype(out_ref.dtype)
 
 
-def weight_kernel(place_ref, gradient_ref, own_turned_ref, other_turned_ref, inverse_ref, copy_ref, sent_ref, grad_ref):
+def weight_kernel(gradient_ref, own_turned_ref, other_turned_ref, inverse_ref, copy_ref, sent_ref, grad_ref):
     chips, rows_each, _ = sent_ref.shape
     count = gradient_ref.shape[1]
     width = own_turned_ref.shape[0]
-    own_rows = pl.ds(pl.multiple_of(place_ref[0] * (width // GROUPS), width // GROUPS), width // GROUPS)
+    kept = width // GROUPS
+    own_rows = pl.ds(pl.multiple_of(lax.axis_index("group") * kept, kept), kept)
     for start in range(0, count, TILE):
         here, slot = slice(start, start + TILE), start // TILE
         weight_grad = 0.0
@@ -419,9 +420,8 @@
     count = kept // blocks
     group, block = lax.axis_index("group")[None], lax.axis_index("block")[None]
     core = lax.axis_index("fsdp")[None]
-    place = jnp.concatenate([group, block, core])
     elements = count * crops
-    smem, vmem = pl.BlockSpec(memory_space=pltpu.SMEM), pl.BlockSpec(memory_space=pltpu.VMEM)
+    vmem = pl.BlockSpec(memory_space=pltpu.VMEM)
 
     def swap(values):
         return lax.ppermute(values, "fsdp", [(0, 1), (1, 0)])
@@ -500,16 +500,16 @@
             shape((lines, LANES), f32),
             shape((width, half), bf16),
         ),
-        in_specs=[smem] + [vmem] * 6,
+        in_specs=[vmem] * 6,
         **halved,
-    )(place, teacher_w, student_w, other, own_mass, own_part, placed)
+    )(teacher_w, student_w, other, own_mass, own_part, placed)
     first = share(sent)
     sent = call(
         functools.partial(sweep_kernel, prototypes, crops),
         shape((members, 2 * lines, LANES), bf16),
         flops=4 * elements,
-        in_specs=[smem] + [vmem] * 4,
-    )(place, own_mass, other_mass, first, student_part)
+        in_specs=[vmem] * 4,
+    )(own_mass, other_mass, first, student_part)
     second = share(sent)
     sent, scale, student_copy = call(
         functools.partial(last_sweep_kernel, prototypes, crops),
@@ -519,18 +519,18 @@
             shape((pieces, width, count // pieces), bf16),
         ),
         flops=4 * elements,
-        in_specs=[smem] + [vmem] * 3 + [anyspace],
+        in_specs=[vmem] * 3 + [anyspace],
         scratch_shapes=[dma((pieces,))],
-    )(place, own_mass, other_mass, second, hbm(student_v))
+    )(own_mass, other_mass, second, hbm(student_v))
     third = share(sent)
 
     gradient, keep, give = call(
         gradient_kernel,
         (shape((2, count, half), bf16), shape((half // GROUPS, width), f32), shape((half // GROUPS, width), bf16)),
         flops=2 * elements * width // GROUPS,
-        in_specs=[smem] + [vmem] * 10,
+        in_specs=[vmem] * 10,
         scratch_shapes=[pltpu.VMEM((width, count), bf16)],
-    )(place, own_mass, other_mass, own_student, other_student, scale, first, second, third, inverse, student_copy)
+    )(own_mass, other_mass, own_student, other_student, scale, first, second, third, inverse, student_copy)
     other = swap(give)
     out_rows = width // chips
     per_chip = rows * width // out_rows
@@ -538,9 +538,9 @@
         weight_kernel,
         shape((blocks, out_rows, count + per_chip), bf16),
         flops=2 * elements * width,
-        in_specs=[smem] + [vmem] * 5,
+        in_specs=[vmem] * 5,
         scratch_shapes=[pltpu.VMEM((count // TILE, width, TILE), f32)],
-    )(place, gradient, own_turned, other_turned, inverse, student_copy)
+    )(gradient, own_turned, other_turned, inverse, student_copy)
     sent = call(
         pack_kernel,
         shape((blocks, out_rows, count + per_chip), bf16),

time: 82.2 us -> 79.2 us (0.964)
  Pallas kernels: 21.6 us -> 18.6 us
where the time goes in v4:
time: 79.2 us; the launch traced here: 78.7 us
  blocking collectives  39.8 us (50%)
  Pallas kernels  18.6 us (23%)
  starting transfers between devices  11.2 us (14%)
  waiting for transfers between devices  7.54 us (10%)
    all_to_all x3, blocking collectives, share(): return lax.all_to_all(values, GROUP, 0, 0)  25.5 us
    all_to_all x1, blocking collectives, kernel_body(): got = lax.all_to_all(sent, 'block', 0, 0)  14.3 us
    all_to_all x1, starting transfers between devices, kernel_body(): own = lax.all_to_all(sent, CHIPS, 0, 0)  8.32 us
    ppermute x1, waiting for transfers between devices, kernel_body(): lax.ppermute(weights, 'group', [(at, (at + move) % GROUPS) for at in rang...  6.88 us
    pallas_call x1, Pallas kernels, kernel_body(): call(directions_kernel, (pltpu.HBM((count, width), bf16), pltpu.HBM((coun...  4.08 us
    pallas_call x1, Pallas kernels, kernel_body(): call(own_kernel, (shape((count, half), f32), shape((count, half), f32), s...  3.02 us
    ppermute x1, starting transfers between devices, kernel_body(): lax.ppermute(weights, 'group', [(at, (at + move) % GROUPS) for at in rang...  2.81 us
    pallas_call x1, Pallas kernels, kernel_body(): call(functools.partial(other_kernel, prototypes), (shape((count, half), f...  2.34 us
  transfers between devices with their start and end apart: 4, of which 2 were waited for; matrix products, arithmetic and copies ran while one was open for 1% of the time, Pallas kernels for 11%

profile of v4, /device:TPU:0, one launch (start us, length us, event | category | flops | bytes accessed | tf_op | source)
XLA Modules:
  0.0 78.7 jit_solution(2088907489119956569)
XLA Ops:
  0.6 1.7 %shard_map.68 = bf16[16,32,512]{2,1,0:T(8,128)(2,1)} custom-call(bf16[32,256]{1,0:T(8,128)(2,1)} %teacher_ref.2, bf16[32,256]{1,0:T(8,128)(2,1)} %student_ref.5), custom_call_target="tpu_custom_call" | custom-call | tf_op jit(solution)/shard_map/pallas_call | solution.py:434
  2.4 8.3 %all-to-all-start = ((bf16[16,32,512]{2,1,0:T(8,128)(2,1)}), bf16[16,32,512]{2,1,0:T(8,128)(2,1)S(1)}, u32[]{:S(2)}, u32[]{:S(2)}) async-start(bf16[16,32,512]{2,1,0:T(8,128)(2,1)} %shard_map.68), calls=%async_computation | async-start | bytes 1048576 | tf_op jit(solution)/shard_map/all_to_all | solution.py:440
  10.7 0.8 convert_dynamic-update-slice_fusion
  11.5 2.8 %collective-permute-start = (f32[8,128]{1,0:T(8,128)S(1)}, f32[8,128]{1,0:T(8,128)S(1)}, u32[]{:S(2)}, u32[]{:S(2)}) collective-permute-start(f32[8,128]{1,0:T(8,128)S(1)} %bitcast.3), channel_id=1, source_target_pairs={{0,16},{16,0},{1,17},{17,1},{2,18},{18,2},{3,19},{19,3},{4,20},{20... | collective-permute-start | bytes 12296 | tf_op jit(solution)/shard_map/ppermute | solution.py:446
  14.3 4.1 %shard_map.69 = (bf16[2048,256]{1,0:T(8,128)(2,1)}, bf16[2048,256]{1,0:T(8,128)(2,1)}, f32[1,2048]{1,0:T(1,128)S(1)}) custom-call(s32[1]{0:T(128)} %bitcast.block_ref, bf16[256,16384]{1,0:T(8,128)(2,1)} %teacher_ref.3, bf16[256,16384]{1,0:T(8,128)(2,1)} %directions_ref.1), custom_call_target="tpu_custom_call" | custom-call | flops 6291456 | bytes 4194304 | tf_op jit(solution)/shard_map/pallas_call | solution.py:453
  18.4 6.9 %collective-permute-done = f32[8,128]{1,0:T(8,128)S(1)} collective-permute-done((f32[8,128]{1,0:T(8,128)S(1)}, f32[8,128]{1,0:T(8,128)S(1)}, u32[]{:S(2)}, u32[]{:S(2)}) %collective-permute-start) | collective-permute-done | bytes 4128 | tf_op jit(solution)/shard_map/ppermute | solution.py:446
  25.3 0.7 all-to-all-done.got_ref
  25.9 0.0 collective-permute-start.1
  25.9 3.0 %shard_map.70 = (f32[2048,512]{1,0:T(8,128)S(1)}, f32[2048,512]{1,0:T(8,128)S(1)}, bf16[2048,256]{1,0:T(8,128)(2,1)S(1)}, bf16[2048,256]{1,0:T(8,128)(2,1)S(1)},...) custom-call(bf16[2048,256]{1,0:T(8,128)(2,1)} %get-tuple-element.26.teacher_hbm, ...), custom_call_target="tpu_custom_call" | custom-call | flops 1073741824 | tf_op jit(solution)/shard_map/pallas_call | solution.py:480
  29.0 0.0 collective-permute-done.1.got_ref
  29.0 2.3 %shard_map.71 = (f32[2048,512]{1,0:T(8,128)S(1)}, f32[2048,512]{1,0:T(8,128)S(1)}, bf16[16,16,128]{2,1,0:T(8,128)(2,1)S(1)}, f32[8,128]{1,0:T(8,128)S(1)}, bf16[256,512]{1,0:T(8,128)(2,1)S(1)}) custom-call(bf16[2048,256]{1,0:T(8,128)(2,1)S(1)} %get-tuple-element.30.teacher_w_ref, bf16[2048,256]{1,0:T(8,128)(2,1)S(1)} %get-tuple-element.31.student_w_ref, ...), custom_call_target="tpu_custom_call" | custom-call | flops 1073741824 | tf_op jit(solution)/shard_map/pallas_call | solution.py:494
  31.3 8.8 %all_to_all.25.got_ref.first_ref = bf16[16,16,128]{2,1,0:T(8,128)(2,1)S(1)} all-to-all(bf16[16,16,128]{2,1,0:T(8,128)(2,1)S(1)} %get-tuple-element.37), channel_id=1, replica_groups=mesh['group'=2,'block'=8,'fsdp'=2] {'block','fsdp'}, dimensions={0} | all-to-all | bytes 131072 | tf_op jit(solution)/shard_map/all_to_all | solution.py:430
  40.2 1.2 %shard_map.72 = bf16[16,16,128]{2,1,0:T(8,128)(2,1)S(1)} custom-call(f32[2048,512]{1,0:T(8,128)S(1)} %get-tuple-element.29.own_ref.own_mass_ref, f32[2048,512]{1,0:T(8,128)S(1)} %get-tuple-element.34.other_ref.other_mass_ref, bf16[16,16,128]{2,1,0:T(8,128)(2,1)S(1)} %all_to_all.25.got_ref.first_ref, f32[8,128]{1,0:T(8,128)S(1)} %get-tuple-element.38.part_ref), custom_call_target="tpu_custom_call" | custom-call | flops 8388608 | tf_op jit(solution)/shard_map/pallas_call | solution.py:507
  41.4 8.4 %all_to_all.26.got_ref.second_ref = bf16[16,16,128]{2,1,0:T(8,128)(2,1)S(1)} all-to-all(bf16[16,16,128]{2,1,0:T(8,128)(2,1)S(1)} %shard_map.72), channel_id=1, replica_groups=mesh['group'=2,'block'=8,'fsdp'=2] {'block','fsdp'}, dimensions={0} | all-to-all | bytes 131072 | tf_op jit(solution)/shard_map/all_to_all | solution.py:430
  49.8 1.2 %shard_map.73 = (bf16[16,8,128]{2,1,0:T(8,128)(2,1)S(1)}, f32[2048,1]{1,0:T(8,128)S(1)}, bf16[4,256,512]{2,1,0:T(8,128)(2,1)S(1)}) custom-call(f32[2048,512]{1,0:T(8,128)S(1)} %get-tuple-element.29.own_ref.own_mass_ref, f32[2048,512]{1,0:T(8,128)S(1)} %get-tuple-element.34.other_ref.other_mass_ref, bf16[16,16,128]{2,1,0:T(8,128)(2,1)S(1)} %all_to_all.26.got_ref.second_ref, ...), custom_call_target="tpu_custom_call" | custom-call | flops 8388608 | tf_op jit(solution)/shard_map/pallas_call | solution.py:514
  51.0 8.2 %all_to_all.27.third_ref = bf16[16,8,128]{2,1,0:T(8,128)(2,1)S(1)} all-to-all(bf16[16,8,128]{2,1,0:T(8,128)(2,1)S(1)} %get-tuple-element.40), channel_id=1, replica_groups=mesh['group'=2,'block'=8,'fsdp'=2] {'block','fsdp'}, dimensions={0} | all-to-all | bytes 65536 | tf_op jit(solution)/shard_map/all_to_all | solution.py:430
  59.2 2.3 %shard_map.74 = (bf16[2,2048,512]{2,1,0:T(8,128)(2,1)S(1)}, f32[256,256]{1,0:T(8,128)S(1)}, bf16[256,256]{1,0:T(8,128)(2,1)S(1)}) custom-call(f32[2048,512]{1,0:T(8,128)S(1)} %get-tuple-element.29.own_ref.own_mass_ref, f32[2048,512]{1,0:T(8,128)S(1)} %get-tuple-element.34.other_ref.other_mass_ref, f32[2048,512]{1,0:T(8,128)S(1)} %get-tuple-element.35.own_student_ref, ...), custom_call_target="tpu_custom_call" | custom-call | flops 536870912 | tf_op jit(solution)/shard_map/pallas_call | solution.py:527
  61.5 0.1 collective-permute-start.2
  61.6 0.0 copy-start
  61.6 1.5 %shard_map.75._ = bf16[8,16,2560]{2,1,0:T(8,128)(2,1)S(1)} custom-call(bf16[2,2048,512]{2,1,0:T(8,128)(2,1)S(1)} %get-tuple-element.45.gradient_ref, bf16[256,512]{1,0:T(8,128)(2,1)S(1)} %get-tuple-element.46.own_turned_ref, bf16[256,512]{1,0:T(8,128)(2,1)S(1)} %get-tuple-element.47.other_turned_ref, f32[1,2048]{1,0:T(1,128)S(1)} %get-tuple-element.41.inverse_ref, ...), custom_call_target="tpu_custom_call" | custom-call | flops 1073741824 | tf_op jit(solution)/shard_map/pallas_call | solution.py:537
  63.1 0.0 collective-permute-done.2.other_ref
  63.1 0.1 shard_map.76
  63.2 14.3 %all_to_all.28.got_ref = bf16[8,16,2560]{2,1,0:T(8,128)(2,1)S(1)} all-to-all(bf16[8,16,2560]{2,1,0:T(8,128)(2,1)S(1)} %shard_map.76), channel_id=1, replica_groups=mesh['group'=2,'block'=8,'fsdp'=2] {'block'}, dimensions={0} | all-to-all | bytes 1310720 | tf_op jit(solution)/shard_map/all_to_all | solution.py:552
  77.5 0.0 copy-done
  77.5 1.1 %shard_map.77 = (f32[16,16384]{1,0:T(8,128)}, f32[32,256]{1,0:T(8,128)}) custom-call(bf16[8,16,2560]{2,1,0:T(8,128)(2,1)S(1)} %all_to_all.28.got_ref, bf16[32,256]{1,0:T(8,128)(2,1)S(1)} %copy-done), custom_call_target="tpu_custom_call" | custom-call | tf_op jit(solution)/shard_map/pallas_call | solution.py:553
  (2 shorter events, 0.0 us)
Async XLA Ops:
  2.4 23.6 %all-to-all-start = ((bf16[16,32,512]{2,1,0:T(8,128)(2,1)}), bf16[16,32,512]{2,1,0:T(8,128)(2,1)S(1)}, u32[]{:S(2)}, u32[]{:S(2)}) async-start(bf16[16,32,512]{2,1,0:T(8,128)(2,1)} %shard_map.68), calls=%async_computation | async-start | bytes 1048576 | tf_op jit(solution)/shard_map/all_to_all | solution.py:440
  11.5 13.8 %collective-permute-start = (f32[8,128]{1,0:T(8,128)S(1)}, f32[8,128]{1,0:T(8,128)S(1)}, u32[]{:S(2)}, u32[]{:S(2)}) collective-permute-start(f32[8,128]{1,0:T(8,128)S(1)} %bitcast.3), channel_id=1, source_target_pairs={{0,16},{16,0},{1,17},{17,1},{2,18},{18,2},{3,19},{19,3},{4,20},{20... | collective-permute-start | bytes 12296 | tf_op jit(solution)/shard_map/ppermute | solution.py:446
  25.9 3.0 %collective-permute-start.1 = (bf16[16,32,512]{2,1,0:T(8,128)(2,1)S(1)}, bf16[16,32,512]{2,1,0:T(8,128)(2,1)S(1)}, u32[]{:S(2)}, u32[]{:S(2)}) collective-permute-start(bf16[16,32,512]{2,1,0:T(8,128)(2,1)S(1)} %all-to-all-done.got_ref), channel_id=1, source_target_pairs={{0,1},{1,0},{2,3},{3,2},{4,5},{5,4},{6,7},{7,6},{8,9},{9,8},{10,11... | collective-permute-start | bytes 1572872 | tf_op jit(solution)/shard_map/ppermute | solution.py:427
  61.5 1.6 %collective-permute-start.2 = (bf16[256,256]{1,0:T(8,128)(2,1)S(1)}, bf16[256,256]{1,0:T(8,128)(2,1)S(1)}, u32[]{:S(2)}, u32[]{:S(2)}) collective-permute-start(bf16[256,256]{1,0:T(8,128)(2,1)S(1)} %get-tuple-element.44), channel_id=1, source_target_pairs={{0,1},{1,0},{2,3},{3,2},{4,5},{5,4},{6,7},{7,6},{8,9},{9,8},{10,11... | collective-permute-start | bytes 393224 | tf_op jit(solution)/shard_map/ppermute | solution.py:427
  61.6 15.9 %copy-start = (bf16[32,256]{1,0:T(8,128)(2,1)S(1)}, bf16[32,256]{1,0:T(8,128)(2,1)}, u32[]{:S(2)}) copy-start(bf16[32,256]{1,0:T(8,128)(2,1)} %student_ref.5) | copy-start | bytes 49156

commit v5 on v4

--- a/solution.py
+++ b/solution.py
@@ -223,29 +223,22 @@
     return jnp.transpose(units.astype(jnp.float32)).astype(jnp.bfloat16)
 
 
-def own_kernel(
-    teacher_hbm, student_hbm, got_ref, teacher_ref, student_ref, teacher_w_ref, student_w_ref, part_ref, turned_ref, sems
-):
+def own_kernel(teacher_w_ref, student_hbm, got_ref, teacher_ref, student_ref, student_w_ref, part_ref, turned_ref, sems):
     count, width = teacher_w_ref.shape
     span = FETCH * TILE
     copies = []
     for piece in range(count // span):
         rows = pl.ds(piece * span, span)
-        copies.append((
-            pltpu.make_async_copy(teacher_hbm.at[rows], teacher_w_ref.at[rows], sems.at[0, piece]),
-            pltpu.make_async_copy(student_hbm.at[rows], student_w_ref.at[rows], sems.at[1, piece]),
-        ))
-        copies[-1][0].start()
-        copies[-1][1].start()
+        copies.append(pltpu.make_async_copy(student_hbm.at[rows], student_w_ref.at[rows], sems.at[piece]))
+        copies[-1].start()
     teacher, student = units_of(got_ref, width, 0), units_of(got_ref, width, 1)
     turned_ref[...] = turn(student)
     part = 0.0
     for start in range(0, count, HALF_TILE):
         here = slice(start, start + HALF_TILE)
+        teacher_ref[here, :] = exponentials(teacher_w_ref[here, :], teacher, teacher_temp)
         if start % span == 0:
-            copies[start // span][0].wait()
-            copies[start // span][1].wait()
-        teacher_ref[here, :] = exponentials(teacher_w_ref[here, :], teacher, teacher_temp)
+            copies[start // span].wait()
         mass = exponentials(student_w_ref[here, :], student, student_temp)
         student_ref[here, :] = mass
         part = part + fold(mass)
@@ -281,28 +274,32 @@
     in_core_order(core, (own_total, own_part_ref[...]), (total, part), finish)
 
 
-def sweep(prototypes, crops, first_ref, second_ref, got_ref):
+def sweep(prototypes, crops, first_ref, second_ref, got_ref, scaled_refs=None):
     first_crop, second_crop = halves(1.0 / (crops * received(got_ref)[: crops // LANES]))
     first_total = second_total = 0.0
-    scales = []
     for start in range(0, first_ref.shape[0], TILE):
-        first, second = first_ref[start : start + TILE, :], second_ref[start : start + TILE, :]
+        here = slice(start, start + TILE)
+        first, second = first_ref[here, :], second_ref[here, :]
         proto = jnp.sum(first * first_crop + second * second_crop, axis=1, keepdims=True)
-        scales.append(1.0 / (prototypes * proto))
-        first_total = first_total + fold(first * scales[-1])
-        second_total = second_total + fold(second * scales[-1])
-    return sums(first_total, second_total), scales
+        scale = 1.0 / (prototypes * proto)
+        first, second = first * scale, second * scale
+        if scaled_refs is not None:
+            scaled_refs[0][here, :], scaled_refs[1][here, :] = first, second
+        first_total = first_total + fold(first)
+        second_total = second_total + fold(second)
+    return sums(first_total, second_total)
 
 
 def sweep_kernel(prototypes, crops, own_ref, other_ref, got_ref, part_ref, sent_ref):
     def body(first_ref, second_ref):
-        send(sent_ref, sweep(prototypes, crops, first_ref, second_ref, got_ref)[0], part_ref[...])
+        send(sent_ref, sweep(prototypes, crops, first_ref, second_ref, got_ref), part_ref[...])
 
     in_core_order(lax.axis_index("fsdp"), own_ref, other_ref, body)
 
 
 def last_sweep_kernel(
-    prototypes, crops, own_ref, other_ref, got_ref, directions_ref, sent_ref, scale_ref, copy_ref, sems
+    prototypes, crops, own_ref, other_ref, got_ref, directions_ref,
+    sent_ref, own_scaled_ref, other_scaled_ref, copy_ref, sems,
 ):
     pieces, _, span = copy_ref.shape
     copies = []
@@ -311,13 +308,11 @@
         copies.append(pltpu.make_async_copy(directions_ref.at[:, columns], copy_ref.at[piece], sems.at[piece]))
         copies[-1].start()
 
-    def body(first_ref, second_ref):
-        total, scales = sweep(prototypes, crops, first_ref, second_ref, got_ref)
-        for index, scale in enumerate(scales):
-            scale_ref[index * TILE : (index + 1) * TILE, :] = scale
-        send(sent_ref, total)
-
-    in_core_order(lax.axis_index("fsdp"), own_ref, other_ref, body)
+    def body(first_refs, second_refs):
+        (first_ref, *scaled_refs), (second_ref, second_scaled_ref) = first_refs, second_refs
+        send(sent_ref, sweep(prototypes, crops, first_ref, second_ref, got_ref, (*scaled_refs, second_scaled_ref)))
+
+    in_core_order(lax.axis_index("fsdp"), (own_ref, own_scaled_ref), (other_ref, other_scaled_ref), body)
     for copy in copies:
         copy.wait()
 
@@ -329,7 +324,7 @@
 
 
 def gradient_kernel(
-    own_mass_ref, other_mass_ref, own_student_ref, other_student_ref, scale_ref, first_ref, second_ref, third_ref,
+    own_mass_ref, other_mass_ref, own_student_ref, other_student_ref, first_ref, second_ref, third_ref,
     inverse_ref, copy_ref, gradient_ref, keep_ref, give_ref, unit_ref,
 ):
     group, core = lax.axis_index("group"), lax.axis_index("fsdp")
@@ -345,8 +340,7 @@
             for (side, mass_ref, student_ref), teacher_scale, student_scale in zip(
                 (first_refs, second_refs), teacher_scales, student_scales
             ):
-                teacher = mass_ref[here, :] * scale_ref[here, :] * teacher_scale
-                gradient = student_ref[here, :] * student_scale - teacher
+                gradient = student_ref[here, :] * student_scale - mass_ref[here, :] * teacher_scale
                 gradient_ref[side, start : start + TILE, :] = gradient.astype(jnp.bfloat16)
 
     in_core_order(core, (0, own_mass_ref, own_student_ref), (1, other_mass_ref, other_student_ref), body)
@@ -391,19 +385,26 @@
     copy.wait()
 
 
-def outputs_kernel(got_ref, student_ref, weight_out, feature_out):
+def outputs_kernel(got_ref, student_ref, weight_out, feature_out, wide_ref, sems):
     chips, rows_each, columns = got_ref.shape
     rows, width = student_ref.shape
     pieces = rows // rows_each
     count = columns - pieces * width
+    copies = []
+    for chip in range(chips):
+        here = slice(chip * count, (chip + 1) * count)
+        wide_ref[:, here] = got_ref[chip, :, :count].astype(jnp.float32)
+        here = pl.ds(chip * count, count)
+        copies.append(pltpu.make_async_copy(wide_ref.at[:, here], weight_out.at[:, here], sems.at[chip]))
+        copies[-1].start()
     total = got_ref[0, :, count:].astype(jnp.float32)
     for chip in range(1, chips):
         total = total + got_ref[chip, :, count:].astype(jnp.float32)
     total = jnp.concatenate([total[:, piece * width : (piece + 1) * width] for piece in range(pieces)], axis=0)
     hat, length = unit_rows(student_ref[...])
     feature_out[...] = (total - hat * jnp.sum(hat * total, axis=1, keepdims=True)) / length
-    for chip in range(chips):
-        weight_out[:, chip * count : (chip + 1) * count] = got_ref[chip, :, :count].astype(jnp.float32)
+    for copy in copies:
+        copy.wait()
 
 
 def kernel_body(teacher_feat, student_feat, crop_weight, teacher_v, student_v):
@@ -453,7 +454,7 @@
     teacher_w, student_w, inverse = call(
         directions_kernel,
         (
-            pltpu.HBM((count, width), bf16),
+            shape((count, width), bf16),
             pltpu.HBM((count, width), bf16),
             shape((1, count), f32),
         ),
@@ -477,20 +478,19 @@
     anyspace = pl.BlockSpec(memory_space=pl.ANY)
     pieces = count // (FETCH * TILE)
     halved = dict(flops=2 * elements * width, exps=elements)
-    own_mass, own_student, teacher_w, student_w, own_part, own_turned = call(
+    own_mass, own_student, student_w, own_part, own_turned = call(
         own_kernel,
         (
             shape((count, half), f32),
             shape((count, half), f32),
             shape((count, width), bf16),
-            shape((count, width), bf16),
             shape((8, half), f32),
             shape((width, half), bf16),
         ),
-        in_specs=[anyspace] * 2 + [vmem],
-        scratch_shapes=[dma((2, pieces))],
+        in_specs=[vmem, anyspace, vmem],
+        scratch_shapes=[dma((pieces,))],
         **halved,
-    )(hbm(teacher_w), hbm(student_w), own)
+    )(teacher_w, hbm(student_w), own)
     other_mass, other_student, sent, student_part, other_turned = call(
         functools.partial(other_kernel, prototypes),
         (
@@ -511,11 +511,12 @@
         in_specs=[vmem] * 4,
     )(own_mass, other_mass, first, student_part)
     second = share(sent)
-    sent, scale, student_copy = call(
+    sent, own_scaled, other_scaled, student_copy = call(
         functools.partial(last_sweep_kernel, prototypes, crops),
         (
             shape((members, lines, LANES), bf16),
-            shape((count, 1), f32),
+            shape((count, half), f32),
+            shape((count, half), f32),
             shape((pieces, width, count // pieces), bf16),
         ),
         flops=4 * elements,
@@ -528,9 +529,9 @@
         gradient_kernel,
         (shape((2, count, half), bf16), shape((half // GROUPS, width), f32), shape((half // GROUPS, width), bf16)),
         flops=2 * elements * width // GROUPS,
-        in_specs=[vmem] * 10,
+        in_specs=[vmem] * 9,
         scratch_shapes=[pltpu.VMEM((width, count), bf16)],
-    )(own_mass, other_mass, own_student, other_student, scale, first, second, third, inverse, student_copy)
+    )(own_scaled, other_scaled, own_student, other_student, first, second, third, inverse, student_copy)
     other = swap(give)
     out_rows = width // chips
     per_chip = rows * width // out_rows
@@ -551,7 +552,10 @@
     )(keep, other, sent)
     got = lax.all_to_all(sent, "block", 0, 0)
     return call(
-        outputs_kernel, (shape((out_rows, kept), f32), shape((rows, width), f32))
+        outputs_kernel,
+        (shape((out_rows, kept), f32), shape((rows, width), f32)),
+        out_specs=[anyspace, vmem],
+        scratch_shapes=[pltpu.VMEM((out_rows, kept), f32), dma((blocks,))],
     )(got, student_feat)
 
 

time: 79.2 us -> 79.4 us (level)
  no operation moved by 1% of the time
where the time goes in v5:
time: 79.4 us; the launch traced here: 78.9 us
  blocking collectives  39.8 us (50%)
  Pallas kernels  18.6 us (23%)
  starting transfers between devices  11.2 us (14%)
  waiting for transfers between devices  7.58 us (10%)
  between operations  0.91 us (1%)
    all_to_all x3, blocking collectives, share(): return lax.all_to_all(values, GROUP, 0, 0)  25.5 us
    all_to_all x1, blocking collectives, kernel_body(): got = lax.all_to_all(sent, 'block', 0, 0)  14.3 us
    all_to_all x1, starting transfers between devices, kernel_body(): own = lax.all_to_all(sent, CHIPS, 0, 0)  8.32 us
    ppermute x1, waiting for transfers between devices, kernel_body(): lax.ppermute(weights, 'group', [(at, (at + move) % GROUPS) for at in rang...  6.92 us
    pallas_call x1, Pallas kernels, kernel_body(): call(directions_kernel, (shape((count, width), bf16), pltpu.HBM((count, w...  4.04 us
    ppermute x1, starting transfers between devices, kernel_body(): lax.ppermute(weights, 'group', [(at, (at + move) % GROUPS) for at in rang...  2.81 us
    pallas_call x1, Pallas kernels, kernel_body(): call(own_kernel, (shape((count, half), f32), shape((count, half), f32), s...  2.78 us
    pallas_call x1, Pallas kernels, kernel_body(): call(gradient_kernel, (shape((2, count, half), bf16), shape((half // GROU...  2.22 us
  transfers between devices with their start and end apart: 4, of which 2 were waited for; matrix products, arithmetic and copies ran while one was open for 1% of the time, Pallas kernels for 11%

profile of v5, /device:TPU:0, one launch (start us, length us, event | category | flops | bytes accessed | tf_op | source)
XLA Modules:
  0.0 78.9 jit_solution(14092303721480584019)
XLA Ops:
  0.6 1.7 %shard_map.68 = bf16[16,32,512]{2,1,0:T(8,128)(2,1)} custom-call(bf16[32,256]{1,0:T(8,128)(2,1)} %teacher_ref.2, bf16[32,256]{1,0:T(8,128)(2,1)} %student_ref.5), custom_call_target="tpu_custom_call" | custom-call | tf_op jit(solution)/shard_map/pallas_call | solution.py:435
  2.3 8.3 %all-to-all-start = ((bf16[16,32,512]{2,1,0:T(8,128)(2,1)}), bf16[16,32,512]{2,1,0:T(8,128)(2,1)S(1)}, u32[]{:S(2)}, u32[]{:S(2)}) async-start(bf16[16,32,512]{2,1,0:T(8,128)(2,1)} %shard_map.68), calls=%async_computation | async-start | bytes 1048576 | tf_op jit(solution)/shard_map/all_to_all | solution.py:441
  10.7 0.8 convert_dynamic-update-slice_fusion
  11.5 2.8 %collective-permute-start = (f32[8,128]{1,0:T(8,128)S(1)}, f32[8,128]{1,0:T(8,128)S(1)}, u32[]{:S(2)}, u32[]{:S(2)}) collective-permute-start(f32[8,128]{1,0:T(8,128)S(1)} %bitcast.3), channel_id=1, source_target_pairs={{0,16},{16,0},{1,17},{17,1},{2,18},{18,2},{3,19},{19,3},{4,20},{20... | collective-permute-start | bytes 12296 | tf_op jit(solution)/shard_map/ppermute | solution.py:447
  14.3 4.0 %shard_map.69 = (bf16[2048,256]{1,0:T(8,128)(2,1)S(1)}, bf16[2048,256]{1,0:T(8,128)(2,1)}, f32[1,2048]{1,0:T(1,128)S(1)}) custom-call(s32[1]{0:T(128)} %bitcast.block_ref, bf16[256,16384]{1,0:T(8,128)(2,1)} %teacher_ref.3, bf16[256,16384]{1,0:T(8,128)(2,1)} %directions_ref.1), custom_call_target="tpu_custom_call" | custom-call | flops 6291456 | bytes 4194304 | tf_op jit(solution)/shard_map/pallas_call | solution.py:454
  18.3 6.9 %collective-permute-done = f32[8,128]{1,0:T(8,128)S(1)} collective-permute-done((f32[8,128]{1,0:T(8,128)S(1)}, f32[8,128]{1,0:T(8,128)S(1)}, u32[]{:S(2)}, u32[]{:S(2)}) %collective-permute-start) | collective-permute-done | bytes 4128 | tf_op jit(solution)/shard_map/ppermute | solution.py:447
  25.2 0.7 all-to-all-done.got_ref
  25.9 0.0 collective-permute-start.1
  25.9 2.8 %shard_map.70 = (f32[2048,512]{1,0:T(8,128)S(1)}, f32[2048,512]{1,0:T(8,128)S(1)}, bf16[2048,256]{1,0:T(8,128)(2,1)S(1)}, f32[8,512]{1,0:T(8,128)S(1)}, bf16[256,512]{1,0:T(8,128)(2,1)S(1)}) custom-call(bf16[2048,256]{1,0:T(8,128)(2,1)S(1)} %get-tuple-element.26.teacher_w_ref, bf16[2048,256]{1,0:T(8,128)(2,1)} %get-tuple-element.27.student_hbm, ...), custom_call_target="tpu_custom_call" | custom-call | flops 1073741824 | tf_op jit(solution)/shard_map/pallas_call | solution.py:481
  28.7 0.0 collective-permute-done.1.got_ref
  28.7 2.1 %shard_map.71 = (f32[2048,512]{1,0:T(8,128)S(1)}, f32[2048,512]{1,0:T(8,128)S(1)}, bf16[16,16,128]{2,1,0:T(8,128)(2,1)S(1)}, f32[8,128]{1,0:T(8,128)S(1)}, bf16[256,512]{1,0:T(8,128)(2,1)S(1)}) custom-call(bf16[2048,256]{1,0:T(8,128)(2,1)S(1)} %get-tuple-element.26.teacher_w_ref, bf16[2048,256]{1,0:T(8,128)(2,1)S(1)} %get-tuple-element.30.student_w_ref, ...), custom_call_target="tpu_custom_call" | custom-call | flops 1073741824 | tf_op jit(solution)/shard_map/pallas_call | solution.py:494
  30.8 8.8 %all_to_all.25.got_ref.first_ref = bf16[16,16,128]{2,1,0:T(8,128)(2,1)S(1)} all-to-all(bf16[16,16,128]{2,1,0:T(8,128)(2,1)S(1)} %get-tuple-element.34), channel_id=1, replica_groups=mesh['group'=2,'block'=8,'fsdp'=2] {'block','fsdp'}, dimensions={0} | all-to-all | bytes 131072 | tf_op jit(solution)/shard_map/all_to_all | solution.py:431
  39.6 1.2 %shard_map.72 = bf16[16,16,128]{2,1,0:T(8,128)(2,1)S(1)} custom-call(f32[2048,512]{1,0:T(8,128)S(1)} %get-tuple-element.29.own_ref, f32[2048,512]{1,0:T(8,128)S(1)} %get-tuple-element.33.other_ref, bf16[16,16,128]{2,1,0:T(8,128)(2,1)S(1)} %all_to_all.25.got_ref.first_ref, f32[8,128]{1,0:T(8,128)S(1)} %get-tuple-element.35.part_ref), custom_call_target="tpu_custom_call" | custom-call | flops 8388608 | tf_op jit(solution)/shard_map/pallas_call | solution.py:507
  40.8 8.4 %all_to_all.26.got_ref.second_ref = bf16[16,16,128]{2,1,0:T(8,128)(2,1)S(1)} all-to-all(bf16[16,16,128]{2,1,0:T(8,128)(2,1)S(1)} %shard_map.72), channel_id=1, replica_groups=mesh['group'=2,'block'=8,'fsdp'=2] {'block','fsdp'}, dimensions={0} | all-to-all | bytes 131072 | tf_op jit(solution)/shard_map/all_to_all | solution.py:431
  49.2 1.3 %shard_map.73 = (bf16[16,8,128]{2,1,0:T(8,128)(2,1)S(1)}, f32[2048,512]{1,0:T(8,128)S(1)}, f32[2048,512]{1,0:T(8,128)S(1)}, bf16[4,256,512]{2,1,0:T(8,128)(2,1)S(1)}) custom-call(f32[2048,512]{1,0:T(8,128)S(1)} %get-tuple-element.29.own_ref, f32[2048,512]{1,0:T(8,128)S(1)} %get-tuple-element.33.other_ref, ...), custom_call_target="tpu_custom_call" | custom-call | flops 8388608 | tf_op jit(solution)/shard_map/pallas_call | solution.py:514
  50.5 8.2 %all_to_all.27.third_ref = bf16[16,8,128]{2,1,0:T(8,128)(2,1)S(1)} all-to-all(bf16[16,8,128]{2,1,0:T(8,128)(2,1)S(1)} %get-tuple-element.40), channel_id=1, replica_groups=mesh['group'=2,'block'=8,'fsdp'=2] {'block','fsdp'}, dimensions={0} | all-to-all | bytes 65536 | tf_op jit(solution)/shard_map/all_to_all | solution.py:431
  58.7 2.2 %shard_map.74 = (bf16[2,2048,512]{2,1,0:T(8,128)(2,1)S(1)}, f32[256,256]{1,0:T(8,128)S(1)}, bf16[256,256]{1,0:T(8,128)(2,1)S(1)}) custom-call(f32[2048,512]{1,0:T(8,128)S(1)} %get-tuple-element.36.own_mass_ref, f32[2048,512]{1,0:T(8,128)S(1)} %get-tuple-element.37.other_mass_ref, f32[2048,512]{1,0:T(8,128)S(1)} %get-tuple-element.38.own_student_ref, ...), custom_call_target="tpu_custom_call" | custom-call | flops 536870912 | tf_op jit(solution)/shard_map/pallas_call | solution.py:528
  61.0 0.1 collective-permute-start.2
  61.0 0.0 copy-start
  61.1 1.5 %shard_map.75._ = bf16[8,16,2560]{2,1,0:T(8,128)(2,1)S(1)} custom-call(bf16[2,2048,512]{2,1,0:T(8,128)(2,1)S(1)} %get-tuple-element.45.gradient_ref, bf16[256,512]{1,0:T(8,128)(2,1)S(1)} %get-tuple-element.46.own_turned_ref, bf16[256,512]{1,0:T(8,128)(2,1)S(1)} %get-tuple-element.47.other_turned_ref, f32[1,2048]{1,0:T(1,128)S(1)} %get-tuple-element.41.inverse_ref, ...), custom_call_target="tpu_custom_call" | custom-call | flops 1073741824 | tf_op jit(solution)/shard_map/pallas_call | solution.py:538
  62.6 0.0 collective-permute-done.2.other_ref
  62.6 0.1 shard_map.76
  62.7 14.3 %all_to_all.28.got_ref = bf16[8,16,2560]{2,1,0:T(8,128)(2,1)S(1)} all-to-all(bf16[8,16,2560]{2,1,0:T(8,128)(2,1)S(1)} %shard_map.76), channel_id=1, replica_groups=mesh['group'=2,'block'=8,'fsdp'=2] {'block'}, dimensions={0} | all-to-all | bytes 1310720 | tf_op jit(solution)/shard_map/all_to_all | solution.py:553
  77.0 0.0 copy-done
  77.0 1.7 %shard_map.77 = (f32[16,16384]{1,0:T(8,128)}, f32[32,256]{1,0:T(8,128)}) custom-call(bf16[8,16,2560]{2,1,0:T(8,128)(2,1)S(1)} %all_to_all.28.got_ref, bf16[32,256]{1,0:T(8,128)(2,1)S(1)} %copy-done), custom_call_target="tpu_custom_call" | custom-call | tf_op jit(solution)/shard_map/pallas_call | solution.py:554
  (2 shorter events, 0.0 us)
Async XLA Ops:
  2.3 23.6 %all-to-all-start = ((bf16[16,32,512]{2,1,0:T(8,128)(2,1)}), bf16[16,32,512]{2,1,0:T(8,128)(2,1)S(1)}, u32[]{:S(2)}, u32[]{:S(2)}) async-start(bf16[16,32,512]{2,1,0:T(8,128)(2,1)} %shard_map.68), calls=%async_computation | async-start | bytes 1048576 | tf_op jit(solution)/shard_map/all_to_all | solution.py:441
  11.5 13.8 %collective-permute-start = (f32[8,128]{1,0:T(8,128)S(1)}, f32[8,128]{1,0:T(8,128)S(1)}, u32[]{:S(2)}, u32[]{:S(2)}) collective-permute-start(f32[8,128]{1,0:T(8,128)S(1)} %bitcast.3), channel_id=1, source_target_pairs={{0,16},{16,0},{1,17},{17,1},{2,18},{18,2},{3,19},{19,3},{4,20},{20... | collective-permute-start | bytes 12296 | tf_op jit(solution)/shard_map/ppermute | solution.py:447
  25.9 2.8 %collective-permute-start.1 = (bf16[16,32,512]{2,1,0:T(8,128)(2,1)S(1)}, bf16[16,32,512]{2,1,0:T(8,128)(2,1)S(1)}, u32[]{:S(2)}, u32[]{:S(2)}) collective-permute-start(bf16[16,32,512]{2,1,0:T(8,128)(2,1)S(1)} %all-to-all-done.got_ref), channel_id=1, source_target_pairs={{0,1},{1,0},{2,3},{3,2},{4,5},{5,4},{6,7},{7,6},{8,9},{9,8},{10,11... | collective-permute-start | bytes 1572872 | tf_op jit(solution)/shard_map/ppermute | solution.py:428
  61.0 1.6 %collective-permute-start.2 = (bf16[256,256]{1,0:T(8,128)(2,1)S(1)}, bf16[256,256]{1,0:T(8,128)(2,1)S(1)}, u32[]{:S(2)}, u32[]{:S(2)}) collective-permute-start(bf16[256,256]{1,0:T(8,128)(2,1)S(1)} %get-tuple-element.44), channel_id=1, source_target_pairs={{0,1},{1,0},{2,3},{3,2},{4,5},{5,4},{6,7},{7,6},{8,9},{9,8},{10,11... | collective-permute-start | bytes 393224 | tf_op jit(solution)/shard_map/ppermute | solution.py:428
  61.0 15.9 %copy-start = (bf16[32,256]{1,0:T(8,128)(2,1)S(1)}, bf16[32,256]{1,0:T(8,128)(2,1)}, u32[]{:S(2)}) copy-start(bf16[32,256]{1,0:T(8,128)(2,1)} %student_ref.5) | copy-start | bytes 49156

commit v6 on v5

--- a/solution.py
+++ b/solution.py
@@ -135,7 +135,7 @@
     )
 
 
-def units_kernel(teacher_ref, student_ref, sent_ref, teacher_vmem, student_vmem, sems):
+def units_kernel(teacher_ref, student_ref, teacher_out, student_out, teacher_vmem, student_vmem, sems):
     copies = [
         pltpu.make_async_copy(teacher_ref, teacher_vmem, sems.at[0]),
         pltpu.make_async_copy(student_ref, student_vmem, sems.at[1]),
@@ -144,12 +144,10 @@
         copy.start()
     for copy in copies:
         copy.wait()
-    width = teacher_vmem.shape[1]
     teacher = unit_rows(teacher_vmem[...])[0].astype(jnp.bfloat16)
-    student = unit_rows(student_vmem[...])[0].astype(jnp.bfloat16)
-    for chip in range(sent_ref.shape[0]):
-        sent_ref[chip, :, :width] = teacher
-        sent_ref[chip, :, width:] = student
+    student_out[...] = unit_rows(student_vmem[...])[0].astype(jnp.bfloat16)
+    for chip in range(teacher_out.shape[0]):
+        teacher_out[chip] = teacher
 
 
 def directions_kernel(block_ref, teacher_ref, student_ref, teacher_out, student_out, inverse_out):
@@ -207,75 +205,102 @@
     return line[:, :half], line[:, half:]
 
 
-def received(got_ref):
-    total = got_ref[0].astype(jnp.float32)
+def received(got_ref, at=0):
+    total = got_ref[0, at:, :].astype(jnp.float32)
     for device in range(1, got_ref.shape[0]):
-        total = total + got_ref[device].astype(jnp.float32)
+        total = total + got_ref[device, at:, :].astype(jnp.float32)
     return total
 
 
-def units_of(got_ref, width, side):
-    chips, rows, _ = got_ref.shape
-    return got_ref[:, :, side * width : (side + 1) * width].reshape(chips * rows, width)
+def units_of(got_ref):
+    chips, rows, width = got_ref.shape
+    return got_ref[...].reshape(chips * rows, width)
+
+
+def in_chip_order(got_ref, units_ref):
+    chips = got_ref.shape[0]
+    rows = units_ref.shape[0] // (GROUPS * chips)
+    group = lax.axis_index("group")
+    for back in range(GROUPS):
+        for chip in range(chips):
+            at = (((group + GROUPS - back) % GROUPS) * chips + chip) * rows
+            here = pl.ds(pl.multiple_of(at, rows), rows)
+            units_ref[here, :] = got_ref[chip, back * rows : (back + 1) * rows, :]
 
 
 def turn(units):
     return jnp.transpose(units.astype(jnp.float32)).astype(jnp.bfloat16)
 
 
-def own_kernel(teacher_w_ref, student_hbm, got_ref, teacher_ref, student_ref, student_w_ref, part_ref, turned_ref, sems):
-    count, width = teacher_w_ref.shape
+def own_teacher_kernel(teacher_w_ref, got_ref, mass_ref):
+    units = units_of(got_ref)
+    for start in range(0, mass_ref.shape[0], HALF_TILE):
+        here = slice(start, start + HALF_TILE)
+        mass_ref[here, :] = exponentials(teacher_w_ref[here, :], units, teacher_temp)
+
+
+def other_teacher_kernel(prototypes, teacher_w_ref, got_ref, own_ref, weight_ref, *refs):
+    *student_refs, mass_ref, sent_ref = refs
+    units = units_of(got_ref)
+    own_total = total = 0.0
+    for start in range(0, mass_ref.shape[0], HALF_TILE):
+        here = slice(start, start + HALF_TILE)
+        mass = exponentials(teacher_w_ref[here, :], units, teacher_temp)
+        mass_ref[here, :] = mass
+        own = own_ref[here, :]
+        scale = 1.0 / (prototypes * jnp.sum(own + mass, axis=1, keepdims=True))
+        own_total = own_total + fold(own * scale)
+        total = total + fold(mass * scale)
+
+    def finish(first, second):
+        extra = jnp.concatenate([sums(first, second), weight_ref[...]], axis=1)
+        extra = jnp.concatenate([extra, jnp.zeros_like(extra)], axis=0)
+        values = jnp.concatenate([ref[...] for ref in student_refs] + [extra.astype(jnp.bfloat16)], axis=0)
+        for chip in range(sent_ref.shape[0]):
+            sent_ref[chip] = values
+
+    in_core_order(lax.axis_index("fsdp"), own_total, total, finish)
+
+
+def own_student_kernel(student_hbm, got_ref, mass_ref, student_w_ref, part_ref, turned_ref, units_ref, sems):
+    count = student_w_ref.shape[0]
     span = FETCH * TILE
     copies = []
     for piece in range(count // span):
         rows = pl.ds(piece * span, span)
         copies.append(pltpu.make_async_copy(student_hbm.at[rows], student_w_ref.at[rows], sems.at[piece]))
         copies[-1].start()
-    teacher, student = units_of(got_ref, width, 0), units_of(got_ref, width, 1)
-    turned_ref[...] = turn(student)
+    in_chip_order(got_ref, units_ref)
+    turned_ref[...] = turn(units_ref[...])
     part = 0.0
     for start in range(0, count, HALF_TILE):
         here = slice(start, start + HALF_TILE)
-        teacher_ref[here, :] = exponentials(teacher_w_ref[here, :], teacher, teacher_temp)
         if start % span == 0:
             copies[start // span].wait()
-        mass = exponentials(student_w_ref[here, :], student, student_temp)
-        student_ref[here, :] = mass
+        mass = exponentials(student_w_ref[here, :], units_ref[...], student_temp)
+        mass_ref[here, :] = mass
         part = part + fold(mass)
     part_ref[...] = part
 
 
-def other_kernel(
-    prototypes, teacher_w_ref, student_w_ref, got_ref, own_ref, own_part_ref, weight_ref,
-    teacher_ref, student_ref, sent_ref, part_ref, turned_ref,
-):
-    count, width = teacher_w_ref.shape
-    core = lax.axis_index("fsdp")
-    teacher, student = units_of(got_ref, width, 0), units_of(got_ref, width, 1)
-    turned_ref[...] = turn(student)
-    own_total = total = part = 0.0
-    for start in range(0, count, HALF_TILE):
+def other_student_kernel(student_w_ref, got_ref, own_part_ref, mass_ref, part_ref, turned_ref, units_ref):
+    in_chip_order(got_ref, units_ref)
+    turned_ref[...] = turn(units_ref[...])
+    part = 0.0
+    for start in range(0, student_w_ref.shape[0], HALF_TILE):
         here = slice(start, start + HALF_TILE)
-        mass = exponentials(teacher_w_ref[here, :], teacher, teacher_temp)
-        teacher_ref[here, :] = mass
-        own = own_ref[here, :]
-        proto = jnp.sum(own + mass, axis=1, keepdims=True)
-        scale = 1.0 / (prototypes * proto)
-        own_total = own_total + fold(own * scale)
-        total = total + fold(mass * scale)
-        mass = exponentials(student_w_ref[here, :], student, student_temp)
-        student_ref[here, :] = mass
+        mass = exponentials(student_w_ref[here, :], units_ref[...], student_temp)
+        mass_ref[here, :] = mass
         part = part + fold(mass)
 
     def finish(first, second):
-        send(sent_ref, sums(first[0], second[0]), weight_ref[...])
-        part_ref[...] = sums(first[1], second[1])
-
-    in_core_order(core, (own_total, own_part_ref[...]), (total, part), finish)
-
-
-def sweep(prototypes, crops, first_ref, second_ref, got_ref, scaled_refs=None):
-    first_crop, second_crop = halves(1.0 / (crops * received(got_ref)[: crops // LANES]))
+        part_ref[...] = sums(first, second)
+
+    in_core_order(lax.axis_index("fsdp"), own_part_ref[...], part, finish)
+
+
+def sweep(prototypes, crops, first_ref, second_ref, received_sums, scaled_refs=None):
+    first_crop, second_crop = halves(1.0 / (crops * received_sums))
     first_total = second_total = 0.0
     for start in range(0, first_ref.shape[0], TILE):
         here = slice(start, start + TILE)
@@ -290,9 +315,14 @@
     return sums(first_total, second_total)
 
 
-def sweep_kernel(prototypes, crops, own_ref, other_ref, got_ref, part_ref, sent_ref):
+def sweep_kernel(prototypes, crops, own_ref, other_ref, got_ref, other_got_ref, part_ref, sent_ref, weight_ref):
+    lines = crops // LANES
+    at = got_ref.shape[1] - 2 * lines
+    extra = received(got_ref, at) + received(other_got_ref, at)
+    weight_ref[...] = extra[:lines, LANES:]
+
     def body(first_ref, second_ref):
-        send(sent_ref, sweep(prototypes, crops, first_ref, second_ref, got_ref), part_ref[...])
+        send(sent_ref, sweep(prototypes, crops, first_ref, second_ref, extra[:lines, :LANES]), part_ref[...])
 
     in_core_order(lax.axis_index("fsdp"), own_ref, other_ref, body)
 
@@ -308,9 +338,11 @@
         copies.append(pltpu.make_async_copy(directions_ref.at[:, columns], copy_ref.at[piece], sems.at[piece]))
         copies[-1].start()
 
+    total = received(got_ref)[: crops // LANES]
+
     def body(first_refs, second_refs):
         (first_ref, *scaled_refs), (second_ref, second_scaled_ref) = first_refs, second_refs
-        send(sent_ref, sweep(prototypes, crops, first_ref, second_ref, got_ref, (*scaled_refs, second_scaled_ref)))
+        send(sent_ref, sweep(prototypes, crops, first_ref, second_ref, total, (*scaled_refs, second_scaled_ref)))
 
     in_core_order(lax.axis_index("fsdp"), (own_ref, own_scaled_ref), (other_ref, other_scaled_ref), body)
     for copy in copies:
@@ -324,13 +356,13 @@
 
 
 def gradient_kernel(
-    own_mass_ref, other_mass_ref, own_student_ref, other_student_ref, first_ref, second_ref, third_ref,
+    own_mass_ref, other_mass_ref, own_student_ref, other_student_ref, weight_ref, second_ref, third_ref,
     inverse_ref, copy_ref, gradient_ref, keep_ref, give_ref, unit_ref,
 ):
     group, core = lax.axis_index("group"), lax.axis_index("fsdp")
     count, half = own_mass_ref.shape
     lines = 2 * half // LANES
-    weights = received(first_ref)[lines:] / student_temp
+    weights = weight_ref[...] / student_temp
     teacher_scales = halves(weights / received(third_ref))
     student_scales = halves(weights / received(second_ref)[lines:])
 
@@ -385,26 +417,19 @@
     copy.wait()
 
 
-def outputs_kernel(got_ref, student_ref, weight_out, feature_out, wide_ref, sems):
+def outputs_kernel(got_ref, student_ref, weight_out, feature_out):
     chips, rows_each, columns = got_ref.shape
     rows, width = student_ref.shape
     pieces = rows // rows_each
     count = columns - pieces * width
-    copies = []
-    for chip in range(chips):
-        here = slice(chip * count, (chip + 1) * count)
-        wide_ref[:, here] = got_ref[chip, :, :count].astype(jnp.float32)
-        here = pl.ds(chip * count, count)
-        copies.append(pltpu.make_async_copy(wide_ref.at[:, here], weight_out.at[:, here], sems.at[chip]))
-        copies[-1].start()
     total = got_ref[0, :, count:].astype(jnp.float32)
     for chip in range(1, chips):
         total = total + got_ref[chip, :, count:].astype(jnp.float32)
     total = jnp.concatenate([total[:, piece * width : (piece + 1) * width] for piece in range(pieces)], axis=0)
     hat, length = unit_rows(student_ref[...])
     feature_out[...] = (total - hat * jnp.sum(hat * total, axis=1, keepdims=True)) / length
-    for copy in copies:
-        copy.wait()
+    for chip in range(chips):
+        weight_out[:, chip * count : (chip + 1) * count] = got_ref[chip, :, :count].astype(jnp.float32)
 
 
 def kernel_body(teacher_feat, student_feat, crop_weight, teacher_v, student_v):
@@ -432,19 +457,23 @@
 
     dma = pltpu.SemaphoreType.DMA
     hbm = functools.partial(pltpu.with_memory_space_constraint, memory_space=pltpu.HBM)
-    sent = call(
+    teacher_sent, student_unit = call(
         units_kernel,
-        shape((chips, rows, 2 * width), bf16),
+        (shape((chips, rows, width), bf16), shape((rows, width), bf16)),
         in_specs=[pl.BlockSpec(memory_space=pl.ANY)] * 2,
         scratch_shapes=[pltpu.VMEM((rows, width), bf16), pltpu.VMEM((rows, width), bf16), dma((2,))],
     )(hbm(teacher_feat), hbm(student_feat))
-    own = lax.all_to_all(sent, CHIPS, 0, 0)
+    teacher_own = lax.all_to_all(teacher_sent, CHIPS, 0, 0)
+
+    def groups_back(values, back):
+        return lax.ppermute(values, "group", [(at, (at + back) % GROUPS) for at in range(GROUPS)])
 
     device = (core[0] * chips + group[0] * blocks + block[0]) * rows
     weights = lax.dynamic_update_slice(jnp.zeros((crops,), f32), crop_weight.astype(f32), (device,)).reshape(lines, LANES)
     placed = weights
     for move in range(1, GROUPS):
-        placed = placed + lax.ppermute(weights, "group", [(at, (at + move) % GROUPS) for at in range(GROUPS)])
+        placed = placed + groups_back(weights, move)
+    student_units = [student_unit] + [groups_back(student_unit, back) for back in range(1, GROUPS)]
 
     span = 2 * TILE
     spans = count // span
@@ -472,44 +501,41 @@
         hbm(student_v),
     )
 
-    own, teacher_w, placed = lax.optimization_barrier((own, teacher_w, placed))
-    other = swap(own)
+    teacher_own, teacher_w, placed, student_units = lax.optimization_barrier(
+        (teacher_own, teacher_w, placed, student_units)
+    )
+    teacher_other = swap(teacher_own)
     half = crops // 2
     anyspace = pl.BlockSpec(memory_space=pl.ANY)
     pieces = count // (FETCH * TILE)
-    halved = dict(flops=2 * elements * width, exps=elements)
-    own_mass, own_student, student_w, own_part, own_turned = call(
-        own_kernel,
-        (
-            shape((count, half), f32),
-            shape((count, half), f32),
-            shape((count, width), bf16),
-            shape((8, half), f32),
-            shape((width, half), bf16),
-        ),
-        in_specs=[vmem, anyspace, vmem],
-        scratch_shapes=[dma((pieces,))],
-        **halved,
-    )(teacher_w, hbm(student_w), own)
-    other_mass, other_student, sent, student_part, other_turned = call(
-        functools.partial(other_kernel, prototypes),
-        (
-            shape((count, half), f32),
-            shape((count, half), f32),
-            shape((members, 2 * lines, LANES), bf16),
-            shape((lines, LANES), f32),
-            shape((width, half), bf16),
-        ),
-        in_specs=[vmem] * 6,
-        **halved,
-    )(teacher_w, student_w, other, own_mass, own_part, placed)
-    first = share(sent)
-    sent = call(
+    quarter = dict(flops=elements * width, exps=elements // 2)
+    own_mass = call(own_teacher_kernel, shape((count, half), f32), **quarter)(teacher_w, teacher_own)
+    other_mass, sent = call(
+        functools.partial(other_teacher_kernel, prototypes),
+        (shape((count, half), f32), shape((blocks, GROUPS * rows + 2 * lines, width), bf16)),
+        **quarter,
+    )(teacher_w, teacher_other, own_mass, placed, *student_units)
+    first = lax.all_to_all(sent, "block", 0, 0)
+    first_other = swap(first)
+    units = pltpu.VMEM((half, width), bf16)
+    own_student, student_w, own_part, own_turned = call(
+        own_student_kernel,
+        (shape((count, half), f32), shape((count, width), bf16), shape((8, half), f32), shape((width, half), bf16)),
+        in_specs=[anyspace, vmem],
+        scratch_shapes=[units, dma((pieces,))],
+        **quarter,
+    )(hbm(student_w), first)
+    other_student, student_part, other_turned = call(
+        other_student_kernel,
+        (shape((count, half), f32), shape((lines, LANES), f32), shape((width, half), bf16)),
+        scratch_shapes=[units],
+        **quarter,
+    )(student_w, first_other, own_part)
+    sent, weights = call(
         functools.partial(sweep_kernel, prototypes, crops),
-        shape((members, 2 * lines, LANES), bf16),
+        (shape((members, 2 * lines, LANES), bf16), shape((lines, LANES), f32)),
         flops=4 * elements,
-        in_specs=[vmem] * 4,
-    )(own_mass, other_mass, first, student_part)
+    )(own_mass, other_mass, first, first_other, student_part)
     second = share(sent)
     sent, own_scaled, other_scaled, student_copy = call(
         functools.partial(last_sweep_kernel, prototypes, crops),
@@ -531,7 +557,7 @@
         flops=2 * elements * width // GROUPS,
         in_specs=[vmem] * 9,
         scratch_shapes=[pltpu.VMEM((width, count), bf16)],
-    )(own_scaled, other_scaled, own_student, other_student, first, second, third, inverse, student_copy)
+    )(own_scaled, other_scaled, own_student, other_student, weights, second, third, inverse, student_copy)
     other = swap(give)
     out_rows = width // chips
     per_chip = rows * width // out_rows
@@ -552,10 +578,7 @@
     )(keep, other, sent)
     got = lax.all_to_all(sent, "block", 0, 0)
     return call(
-        outputs_kernel,
-        (shape((out_rows, kept), f32), shape((rows, width), f32)),
-        out_specs=[anyspace, vmem],
-        scratch_shapes=[pltpu.VMEM((out_rows, kept), f32), dma((blocks,))],
+        outputs_kernel, (shape((out_rows, kept), f32), shape((rows, width), f32))
     )(got, student_feat)
 
 

time: 79.4 us -> 76.7 us (0.966)
  waiting for transfers between devices: 7.58 us -> 3.55 us
  blocking collectives: 39.8 us -> 41.5 us
    all_to_all x0 -> x1, blocking collectives: none -> 10.5 us  [kernel_body(): first = lax.all_to_all(sent, 'block', 0, 0)]
    all_to_all x3 -> x2, blocking collectives: 25.5 us -> 16.6 us  [share(): return lax.all_to_all(values, GROUP, 0, 0)]
    ppermute x1 -> x2, waiting for transfers between devices: 6.92 us -> 1.89 us  [groups_back(): lax.ppermute(values, 'group', [(at, (at + back) % GROUPS) for at in range...]
    pallas_call x4 -> x6, Pallas kernels: 7.74 us -> 8.11 us  [the longest x1 2.38 us: kernel_body(): call(own_student_kernel, (shape((count, half), f32), shape((count, width)...]
    ppermute x1 -> x2, starting transfers between devices: 2.81 us -> 2.92 us  [groups_back(): lax.ppermute(values, 'group', [(at, (at + back) % GROUPS) for at in range...]
  transfers between devices with their start and end apart: 4 -> 6, of which waited for: 2 -> 4; matrix products, arithmetic and copies ran while one was open for 1% -> 1% of each run, Pallas kernels for 11% -> 12%
where the time goes in v6:
time: 76.7 us; the launch traced here: 76.2 us
  blocking collectives  41.5 us (54%)
  Pallas kernels  18.2 us (24%)
  starting transfers between devices  11.3 us (15%)
  waiting for transfers between devices  3.55 us (5%)
  other arithmetic  0.77 us (1%)
  between operations  0.77 us (1%)
    all_to_all x2, blocking collectives, share(): return lax.all_to_all(values, GROUP, 0, 0)  16.6 us
    all_to_all x1, blocking collectives, kernel_body(): got = lax.all_to_all(sent, 'block', 0, 0)  14.3 us
    all_to_all x1, blocking collectives, kernel_body(): first = lax.all_to_all(sent, 'block', 0, 0)  10.5 us
    all_to_all x1, starting transfers between devices, kernel_body(): teacher_own = lax.all_to_all(teacher_sent, CHIPS, 0, 0)  8.32 us
    pallas_call x1, Pallas kernels, kernel_body(): call(directions_kernel, (shape((count, width), bf16), pltpu.HBM((count, w...  4.04 us
    ppermute x2, starting transfers between devices, groups_back(): lax.ppermute(values, 'group', [(at, (at + back) % GROUPS) for at in range...  2.92 us
    pallas_call x1, Pallas kernels, kernel_body(): call(own_student_kernel, (shape((count, half), f32), shape((count, width)...  2.38 us
    pallas_call x1, Pallas kernels, kernel_body(): call(gradient_kernel, (shape((2, count, half), bf16), shape((half // GROU...  1.99 us
  transfers between devices with their start and end apart: 6, of which 4 were waited for; matrix products, arithmetic and copies ran while one was open for 1% of the time, Pallas kernels for 12%

profile of v6, /device:TPU:0, one launch (start us, length us, event | category | flops | bytes accessed | tf_op | source)
XLA Modules:
  0.0 76.2 jit_solution(10314247516103325014)
XLA Ops:
  0.6 1.6 %shard_map.68 = (bf16[16,32,256]{2,1,0:T(8,128)(2,1)}, bf16[32,256]{1,0:T(8,128)(2,1)S(1)}) custom-call(bf16[32,256]{1,0:T(8,128)(2,1)} %teacher_ref.2, bf16[32,256]{1,0:T(8,128)(2,1)} %student_ref.5), custom_call_target="tpu_custom_call" | custom-call | tf_op jit(solution)/shard_map/pallas_call | solution.py:460
  2.2 8.3 %all-to-all-start = ((bf16[16,32,256]{2,1,0:T(8,128)(2,1)}), bf16[16,32,256]{2,1,0:T(8,128)(2,1)S(1)}, u32[]{:S(2)}, u32[]{:S(2)}) async-start(bf16[16,32,256]{2,1,0:T(8,128)(2,1)} %get-tuple-element.30), calls=%async_computation | async-start | bytes 524288 | tf_op jit(solution)/shard_map/all_to_all | solution.py:466
  10.6 0.8 %convert_dynamic-update-slice_fusion = f32[1024]{0:T(1024)S(1)} fusion(f32[1024]{0:T(1024)S(1)} %broadcast_in_dim.7, s32[]{:T(128)S(6)} %select_n.3, bf16[32]{0:T(256)(128)(2,1)} %param.7), kind=kLoop, calls=%fused_computation | loop fusion | flops 32 | bytes 580 | tf_op jit(solution)/shard_map/dynamic_update_slice | solution.py:472
  11.3 2.8 %collective-permute-start = (f32[8,128]{1,0:T(8,128)S(1)}, f32[8,128]{1,0:T(8,128)S(1)}, u32[]{:S(2)}, u32[]{:S(2)}) collective-permute-start(f32[8,128]{1,0:T(8,128)S(1)} %bitcast.3), channel_id=1, source_target_pairs={{0,16},{16,0},{1,17},{17,1},{2,18},{18,2},{3,19},{19,3},{4,20},{20... | collective-permute-start | bytes 12296 | tf_op jit(solution)/shard_map/ppermute | solution.py:469
  14.1 0.1 collective-permute-start.1
  14.3 4.0 %shard_map.69 = (bf16[2048,256]{1,0:T(8,128)(2,1)S(1)}, bf16[2048,256]{1,0:T(8,128)(2,1)}, f32[1,2048]{1,0:T(1,128)S(1)}) custom-call(s32[1]{0:T(128)} %bitcast.block_ref, bf16[256,16384]{1,0:T(8,128)(2,1)} %teacher_ref.3, bf16[256,16384]{1,0:T(8,128)(2,1)} %directions_ref.1), custom_call_target="tpu_custom_call" | custom-call | flops 6291456 | bytes 4194304 | tf_op jit(solution)/shard_map/pallas_call | solution.py:483
  18.3 1.7 %collective-permute-done = f32[8,128]{1,0:T(8,128)S(1)} collective-permute-done((f32[8,128]{1,0:T(8,128)S(1)}, f32[8,128]{1,0:T(8,128)S(1)}, u32[]{:S(2)}, u32[]{:S(2)}) %collective-permute-start) | collective-permute-done | bytes 4128 | tf_op jit(solution)/shard_map/ppermute | solution.py:469
  20.0 0.2 collective-permute-done.1.refs_1_
  20.2 0.9 %all-to-all-done.got_ref = bf16[16,32,256]{2,1,0:T(8,128)(2,1)S(1)} async-done(((bf16[16,32,256]{2,1,0:T(8,128)(2,1)}), bf16[16,32,256]{2,1,0:T(8,128)(2,1)S(1)}, u32[]{:S(2)}, u32[]{:S(2)}) %all-to-all-start) | async-done | bytes 262176 | tf_op jit(solution)/shard_map/all_to_all | solution.py:466
  21.1 0.0 collective-permute-start.2
  21.1 0.7 shard_map.70.own_ref
  21.8 0.8 %collective-permute-done.2.got_ref = bf16[16,32,256]{2,1,0:T(8,128)(2,1)S(1)} collective-permute-done((bf16[16,32,256]{2,1,0:T(8,128)(2,1)S(1)}, bf16[16,32,256]{2,1,0:T(8,128)(2,1)S(1)}, u32[]{:S(2)}, u32[]{:S(2)}) %collective-permute-start.2) | collective-permute-done | bytes 262176 | tf_op jit(solution)/shard_map/ppermute | solution.py:453
  22.6 1.5 %shard_map.71 = (f32[2048,512]{1,0:T(8,128)S(1)}, bf16[8,80,256]{2,1,0:T(8,128)(2,1)S(1)}) custom-call(bf16[2048,256]{1,0:T(8,128)(2,1)S(1)} %get-tuple-element.33.teacher_w_ref, bf16[16,32,256]{2,1,0:T(8,128)(2,1)S(1)} %collective-permute-done.2.got_ref, f32[2048,512]{1,0:T(8,128)S(1)} %shard_map.70.own_ref, f32[8,128]{1,0:T(8,128)S(1)} %bitcast_add_fusion.weight_ref, ...), custom_call_target="tpu_custom_call" | custom-call | flops 536870912 | tf_op jit(solution)/shard_map/pallas_call | solution.py:513
  24.1 10.5 %all_to_all.25.got_ref = bf16[8,80,256]{2,1,0:T(8,128)(2,1)S(1)} all-to-all(bf16[8,80,256]{2,1,0:T(8,128)(2,1)S(1)} %get-tuple-element.39), channel_id=1, replica_groups=mesh['group'=2,'block'=8,'fsdp'=2] {'block'}, dimensions={0} | all-to-all | bytes 655360 | tf_op jit(solution)/shard_map/all_to_all | solution.py:518
  34.6 0.0 collective-permute-start.3
  34.6 2.4 %shard_map.72 = (f32[2048,512]{1,0:T(8,128)S(1)}, bf16[2048,256]{1,0:T(8,128)(2,1)S(1)}, f32[8,512]{1,0:T(8,128)S(1)}, bf16[256,512]{1,0:T(8,128)(2,1)S(1)}) custom-call(bf16[2048,256]{1,0:T(8,128)(2,1)} %get-tuple-element.40.student_hbm, bf16[8,80,256]{2,1,0:T(8,128)(2,1)S(1)} %all_to_all.25.got_ref), custom_call_target="tpu_custom_call" | custom-call | flops 536870912 | tf_op jit(solution)/shard_map/pallas_call | solution.py:521
  37.0 0.0 collective-permute-done.3.got_ref.other_got_ref
  37.0 0.8 %shard_map.73 = (f32[2048,512]{1,0:T(8,128)S(1)}, f32[8,128]{1,0:T(8,128)S(1)}, bf16[256,512]{1,0:T(8,128)(2,1)S(1)}) custom-call(bf16[2048,256]{1,0:T(8,128)(2,1)S(1)} %get-tuple-element.41.student_w_ref, bf16[8,80,256]{2,1,0:T(8,128)(2,1)S(1)} %collective-permute-done.3.got_ref.other_got_ref, f32[8,512]{1,0:T(8,128)S(1)} %get-tuple-element.42.own_part_ref), custom_call_target="tpu_custom_call" | custom-call | flops 536870912 | tf_op jit(solution)/shard_map/pallas_call | solution.py:528
  37.8 1.2 %shard_map.74 = (bf16[16,16,128]{2,1,0:T(8,128)(2,1)S(1)}, f32[8,128]{1,0:T(8,128)S(1)}) custom-call(f32[2048,512]{1,0:T(8,128)S(1)} %shard_map.70.own_ref, f32[2048,512]{1,0:T(8,128)S(1)} %get-tuple-element.38.other_ref, bf16[8,80,256]{2,1,0:T(8,128)(2,1)S(1)} %all_to_all.25.got_ref, bf16[8,80,256]{2,1,0:T(8,128)(2,1)S(1)} %collective-permute-done.3.got_ref.other_got_ref, ...), custom_call_target="tpu_custom_call" | custom-call | flops 8388608 | tf_op jit(solution)/shard_map/pallas_call | solution.py:534
  39.0 8.4 %all_to_all.26.got_ref.second_ref = bf16[16,16,128]{2,1,0:T(8,128)(2,1)S(1)} all-to-all(bf16[16,16,128]{2,1,0:T(8,128)(2,1)S(1)} %get-tuple-element.44), channel_id=1, replica_groups=mesh['group'=2,'block'=8,'fsdp'=2] {'block','fsdp'}, dimensions={0} | all-to-all | bytes 131072 | tf_op jit(solution)/shard_map/all_to_all | solution.py:456
  47.4 1.3 %shard_map.75 = (bf16[16,8,128]{2,1,0:T(8,128)(2,1)S(1)}, f32[2048,512]{1,0:T(8,128)S(1)}, f32[2048,512]{1,0:T(8,128)S(1)}, bf16[4,256,512]{2,1,0:T(8,128)(2,1)S(1)}) custom-call(f32[2048,512]{1,0:T(8,128)S(1)} %shard_map.70.own_ref, f32[2048,512]{1,0:T(8,128)S(1)} %get-tuple-element.38.other_ref, bf16[16,16,128]{2,1,0:T(8,128)(2,1)S(1)} %all_to_all.26.got_ref.second_ref, ...), custom_call_target="tpu_custom_call" | custom-call | flops 8388608 | tf_op jit(solution)/shard_map/pallas_call | solution.py:540
  48.7 8.2 %all_to_all.27.third_ref = bf16[16,8,128]{2,1,0:T(8,128)(2,1)S(1)} all-to-all(bf16[16,8,128]{2,1,0:T(8,128)(2,1)S(1)} %get-tuple-element.50), channel_id=1, replica_groups=mesh['group'=2,'block'=8,'fsdp'=2] {'block','fsdp'}, dimensions={0} | all-to-all | bytes 65536 | tf_op jit(solution)/shard_map/all_to_all | solution.py:456
  56.9 2.0 %shard_map.76 = (bf16[2,2048,512]{2,1,0:T(8,128)(2,1)S(1)}, f32[256,256]{1,0:T(8,128)S(1)}, bf16[256,256]{1,0:T(8,128)(2,1)S(1)}) custom-call(f32[2048,512]{1,0:T(8,128)S(1)} %get-tuple-element.45.own_mass_ref, f32[2048,512]{1,0:T(8,128)S(1)} %get-tuple-element.46.other_mass_ref, f32[2048,512]{1,0:T(8,128)S(1)} %get-tuple-element.47.own_student_ref, ...), custom_call_target="tpu_custom_call" | custom-call | flops 536870912 | tf_op jit(solution)/shard_map/pallas_call | solution.py:554
  58.9 0.1 collective-permute-start.4
  59.0 0.0 copy-start
  59.0 1.6 %shard_map.77._ = bf16[8,16,2560]{2,1,0:T(8,128)(2,1)S(1)} custom-call(bf16[2,2048,512]{2,1,0:T(8,128)(2,1)S(1)} %get-tuple-element.55.gradient_ref, bf16[256,512]{1,0:T(8,128)(2,1)S(1)} %get-tuple-element.56.own_turned_ref, bf16[256,512]{1,0:T(8,128)(2,1)S(1)} %get-tuple-element.57.other_turned_ref, f32[1,2048]{1,0:T(1,128)S(1)} %get-tuple-element.51.inverse_ref, ...), custom_call_target="tpu_custom_call" | custom-call | flops 1073741824 | tf_op jit(solution)/shard_map/pallas_call | solution.py:564
  60.6 0.0 collective-permute-done.4.other_ref
  60.6 0.1 shard_map.78
  60.7 14.3 %all_to_all.28.got_ref = bf16[8,16,2560]{2,1,0:T(8,128)(2,1)S(1)} all-to-all(bf16[8,16,2560]{2,1,0:T(8,128)(2,1)S(1)} %shard_map.78), channel_id=1, replica_groups=mesh['group'=2,'block'=8,'fsdp'=2] {'block'}, dimensions={0} | all-to-all | bytes 1310720 | tf_op jit(solution)/shard_map/all_to_all | solution.py:579
  75.0 0.0 copy-done
  75.0 1.1 %shard_map.79 = (f32[16,16384]{1,0:T(8,128)}, f32[32,256]{1,0:T(8,128)}) custom-call(bf16[8,16,2560]{2,1,0:T(8,128)(2,1)S(1)} %all_to_all.28.got_ref, bf16[32,256]{1,0:T(8,128)(2,1)S(1)} %copy-done), custom_call_target="tpu_custom_call" | custom-call | tf_op jit(solution)/shard_map/pallas_call | solution.py:580
  (2 shorter events, 0.0 us)
Async XLA Ops:
  2.2 18.9 %all-to-all-start = ((bf16[16,32,256]{2,1,0:T(8,128)(2,1)}), bf16[16,32,256]{2,1,0:T(8,128)(2,1)S(1)}, u32[]{:S(2)}, u32[]{:S(2)}) async-start(bf16[16,32,256]{2,1,0:T(8,128)(2,1)} %get-tuple-element.30), calls=%async_computation | async-start | bytes 524288 | tf_op jit(solution)/shard_map/all_to_all | solution.py:466
  11.3 8.7 %collective-permute-start = (f32[8,128]{1,0:T(8,128)S(1)}, f32[8,128]{1,0:T(8,128)S(1)}, u32[]{:S(2)}, u32[]{:S(2)}) collective-permute-start(f32[8,128]{1,0:T(8,128)S(1)} %bitcast.3), channel_id=1, source_target_pairs={{0,16},{16,0},{1,17},{17,1},{2,18},{18,2},{3,19},{19,3},{4,20},{20... | collective-permute-start | bytes 12296 | tf_op jit(solution)/shard_map/ppermute | solution.py:469
  14.1 6.0 %collective-permute-start.1 = (bf16[32,256]{1,0:T(8,128)(2,1)S(1)}, bf16[32,256]{1,0:T(8,128)(2,1)S(1)}, u32[]{:S(2)}, u32[]{:S(2)}) collective-permute-start(bf16[32,256]{1,0:T(8,128)(2,1)S(1)} %get-tuple-element.36.refs_0_), channel_id=1, source_target_pairs={{0,16},{16,0},{1,17},{17,1},{2,18},{18,2},{3,19},{19,3},{4,20},{20... | collective-permute-start | bytes 49160 | tf_op jit(solution)/shard_map/ppermute | solution.py:469
  21.1 1.5 %collective-permute-start.2 = (bf16[16,32,256]{2,1,0:T(8,128)(2,1)S(1)}, bf16[16,32,256]{2,1,0:T(8,128)(2,1)S(1)}, u32[]{:S(2)}, u32[]{:S(2)}) collective-permute-start(bf16[16,32,256]{2,1,0:T(8,128)(2,1)S(1)} %all-to-all-done.got_ref), channel_id=1, source_target_pairs={{0,1},{1,0},{2,3},{3,2},{4,5},{5,4},{6,7},{7,6},{8,9},{9,8},{10,11... | collective-permute-start | bytes 786440 | tf_op jit(solution)/shard_map/ppermute | solution.py:453
  34.6 2.4 %collective-permute-start.3 = (bf16[8,80,256]{2,1,0:T(8,128)(2,1)S(1)}, bf16[8,80,256]{2,1,0:T(8,128)(2,1)S(1)}, u32[]{:S(2)}, u32[]{:S(2)}) collective-permute-start(bf16[8,80,256]{2,1,0:T(8,128)(2,1)S(1)} %all_to_all.25.got_ref), channel_id=1, source_target_pairs={{0,1},{1,0},{2,3},{3,2},{4,5},{5,4},{6,7},{7,6},{8,9},{9,8},{10,11... | collective-permute-start | bytes 983048 | tf_op jit(solution)/shard_map/ppermute | solution.py:453
  58.9 1.7 %collective-permute-start.4 = (bf16[256,256]{1,0:T(8,128)(2,1)S(1)}, bf16[256,256]{1,0:T(8,128)(2,1)S(1)}, u32[]{:S(2)}, u32[]{:S(2)}) collective-permute-start(bf16[256,256]{1,0:T(8,128)(2,1)S(1)} %get-tuple-element.54), channel_id=1, source_target_pairs={{0,1},{1,0},{2,3},{3,2},{4,5},{5,4},{6,7},{7,6},{8,9},{9,8},{10,11... | collective-permute-start | bytes 393224 | tf_op jit(solution)/shard_map/ppermute | solution.py:453
  59.0 16.0 %copy-start = (bf16[32,256]{1,0:T(8,128)(2,1)S(1)}, bf16[32,256]{1,0:T(8,128)(2,1)}, u32[]{:S(2)}) copy-start(bf16[32,256]{1,0:T(8,128)(2,1)} %student_ref.5) | copy-start | bytes 49156

commit v7 on v6

--- a/solution.py
+++ b/solution.py
@@ -150,6 +150,21 @@
         teacher_out[chip] = teacher
 
 
+def placed_weights(student_refs, lines, rows, chips):
+    group, block = lax.axis_index("group"), lax.axis_index("block")
+    line = lax.broadcasted_iota(jnp.int32, (lines, LANES), 0)
+    part = lax.broadcasted_iota(jnp.int32, (lines, LANES), 1) // rows
+    each = LANES // rows
+    placed = jnp.zeros((lines, LANES), jnp.float32)
+    for back, ref in enumerate(student_refs):
+        at = lax.axis_index("fsdp") * chips * GROUPS + ((group + GROUPS - back) % GROUPS) * chips + block
+        weights = ref[rows:, :rows].astype(jnp.float32)[0:1, :]
+        weights = jnp.concatenate([weights] * each, axis=1)
+        here = (line == at // each) & (part == at % each)
+        placed = placed + jnp.where(here, jnp.broadcast_to(weights, (lines, LANES)), 0.0)
+    return placed
+
+
 def directions_kernel(block_ref, teacher_ref, student_ref, teacher_out, student_out, inverse_out):
     teacher, _ = unit_columns(teacher_ref[...])
     teacher_out[...] = jnp.transpose(teacher).astype(jnp.bfloat16)
@@ -239,8 +254,12 @@
         mass_ref[here, :] = exponentials(teacher_w_ref[here, :], units, teacher_temp)
 
 
-def other_teacher_kernel(prototypes, teacher_w_ref, got_ref, own_ref, weight_ref, *refs):
-    *student_refs, mass_ref, sent_ref = refs
+def other_teacher_kernel(prototypes, teacher_w_ref, got_ref, own_ref, student_hbm, *refs):
+    *student_refs, mass_ref, sent_ref, student_w_ref, sem = refs
+    copy = pltpu.make_async_copy(student_hbm, student_w_ref, sem)
+    copy.start()
+    chips, rows = sent_ref.shape[0], got_ref.shape[1]
+    placed = placed_weights(student_refs, 2 * own_ref.shape[1] // LANES, rows, chips)
     units = units_of(got_ref)
     own_total = total = 0.0
     for start in range(0, mass_ref.shape[0], HALF_TILE):
@@ -253,30 +272,23 @@
         total = total + fold(mass * scale)
 
     def finish(first, second):
-        extra = jnp.concatenate([sums(first, second), weight_ref[...]], axis=1)
+        extra = jnp.concatenate([sums(first, second), placed], axis=1)
         extra = jnp.concatenate([extra, jnp.zeros_like(extra)], axis=0)
-        values = jnp.concatenate([ref[...] for ref in student_refs] + [extra.astype(jnp.bfloat16)], axis=0)
+        values = jnp.concatenate([ref[:rows, :] for ref in student_refs] + [extra.astype(jnp.bfloat16)], axis=0)
         for chip in range(sent_ref.shape[0]):
             sent_ref[chip] = values
 
     in_core_order(lax.axis_index("fsdp"), own_total, total, finish)
-
-
-def own_student_kernel(student_hbm, got_ref, mass_ref, student_w_ref, part_ref, turned_ref, units_ref, sems):
+    copy.wait()
+
+
+def own_student_kernel(student_w_ref, got_ref, mass_ref, part_ref, turned_ref, units_ref):
     count = student_w_ref.shape[0]
-    span = FETCH * TILE
-    copies = []
-    for piece in range(count // span):
-        rows = pl.ds(piece * span, span)
-        copies.append(pltpu.make_async_copy(student_hbm.at[rows], student_w_ref.at[rows], sems.at[piece]))
-        copies[-1].start()
     in_chip_order(got_ref, units_ref)
     turned_ref[...] = turn(units_ref[...])
     part = 0.0
     for start in range(0, count, HALF_TILE):
         here = slice(start, start + HALF_TILE)
-        if start % span == 0:
-            copies[start // span].wait()
         mass = exponentials(student_w_ref[here, :], units_ref[...], student_temp)
         mass_ref[here, :] = mass
         part = part + fold(mass)
@@ -342,7 +354,8 @@
 
     def body(first_refs, second_refs):
         (first_ref, *scaled_refs), (second_ref, second_scaled_ref) = first_refs, second_refs
-        send(sent_ref, sweep(prototypes, crops, first_ref, second_ref, total, (*scaled_refs, second_scaled_ref)))
+        sent = sweep(prototypes, crops, first_ref, second_ref, total, (*scaled_refs, second_scaled_ref))
+        send(sent_ref, sent, jnp.zeros_like(sent))
 
     in_core_order(lax.axis_index("fsdp"), (own_ref, own_scaled_ref), (other_ref, other_scaled_ref), body)
     for copy in copies:
@@ -363,7 +376,7 @@
     count, half = own_mass_ref.shape
     lines = 2 * half // LANES
     weights = weight_ref[...] / student_temp
-    teacher_scales = halves(weights / received(third_ref))
+    teacher_scales = halves(weights / received(third_ref)[:lines])
     student_scales = halves(weights / received(second_ref)[lines:])
 
     def body(first_refs, second_refs):
@@ -468,11 +481,8 @@
     def groups_back(values, back):
         return lax.ppermute(values, "group", [(at, (at + back) % GROUPS) for at in range(GROUPS)])
 
-    device = (core[0] * chips + group[0] * blocks + block[0]) * rows
-    weights = lax.dynamic_update_slice(jnp.zeros((crops,), f32), crop_weight.astype(f32), (device,)).reshape(lines, LANES)
-    placed = weights
-    for move in range(1, GROUPS):
-        placed = placed + groups_back(weights, move)
+    weights = jnp.pad(crop_weight[None, :], ((0, 15), (0, width - rows)))
+    student_unit = jnp.concatenate([student_unit, weights], axis=0)
     student_units = [student_unit] + [groups_back(student_unit, back) for back in range(1, GROUPS)]
 
     span = 2 * TILE
@@ -501,30 +511,33 @@
         hbm(student_v),
     )
 
-    teacher_own, teacher_w, placed, student_units = lax.optimization_barrier(
-        (teacher_own, teacher_w, placed, student_units)
-    )
+    teacher_own, teacher_w, student_units = lax.optimization_barrier((teacher_own, teacher_w, student_units))
     teacher_other = swap(teacher_own)
     half = crops // 2
     anyspace = pl.BlockSpec(memory_space=pl.ANY)
     pieces = count // (FETCH * TILE)
     quarter = dict(flops=elements * width, exps=elements // 2)
     own_mass = call(own_teacher_kernel, shape((count, half), f32), **quarter)(teacher_w, teacher_own)
-    other_mass, sent = call(
+    other_mass, sent, student_w = call(
         functools.partial(other_teacher_kernel, prototypes),
-        (shape((count, half), f32), shape((blocks, GROUPS * rows + 2 * lines, width), bf16)),
+        (
+            shape((count, half), f32),
+            shape((blocks, GROUPS * rows + 2 * lines, width), bf16),
+            shape((count, width), bf16),
+        ),
+        in_specs=[vmem] * 3 + [anyspace] + [vmem] * GROUPS,
+        scratch_shapes=[dma],
         **quarter,
-    )(teacher_w, teacher_other, own_mass, placed, *student_units)
+    )(teacher_w, teacher_other, own_mass, hbm(student_w), *student_units)
     first = lax.all_to_all(sent, "block", 0, 0)
     first_other = swap(first)
     units = pltpu.VMEM((half, width), bf16)
-    own_student, student_w, own_part, own_turned = call(
+    own_student, own_part, own_turned = call(
         own_student_kernel,
-        (shape((count, half), f32), shape((count, width), bf16), shape((8, half), f32), shape((width, half), bf16)),
-        in_specs=[anyspace, vmem],
-        scratch_shapes=[units, dma((pieces,))],
+        (shape((count, half), f32), shape((8, half), f32), shape((width, half), bf16)),
+        scratch_shapes=[units],
         **quarter,
-    )(hbm(student_w), first)
+    )(student_w, first)
     other_student, student_part, other_turned = call(
         other_student_kernel,
         (shape((count, half), f32), shape((lines, LANES), f32), shape((width, half), bf16)),
@@ -540,7 +553,7 @@
     sent, own_scaled, other_scaled, student_copy = call(
         functools.partial(last_sweep_kernel, prototypes, crops),
         (
-            shape((members, lines, LANES), bf16),
+            shape((members, 2 * lines, LANES), bf16),
             shape((count, half), f32),
             shape((count, half), f32),
             shape((pieces, width, count // pieces), bf16),

time: 76.7 us -> 77.2 us (level)
  waiting for transfers between devices: 3.55 us -> 4.92 us
  Pallas kernels: 18.2 us -> 17.4 us
    pallas_call x1, Pallas kernels: 2.38 us -> 0.79 us  [kernel_body(): call(own_student_kernel, (shape((count, half), f32), shape((8, half), f32...]
    ppermute x3, waiting for transfers between devices: 0.79 us -> 1.62 us  [swap(): return lax.ppermute(values, 'fsdp', [(0, 1), (1, 0)])]
    ppermute x2 -> x1, waiting for transfers between devices: 1.89 us -> 2.29 us  [groups_back(): lax.ppermute(values, 'group', [(at, (at + back) % GROUPS) for at in range...]
    ppermute x2 -> x1, starting transfers between devices: 2.92 us -> 2.82 us  [groups_back(): lax.ppermute(values, 'group', [(at, (at + back) % GROUPS) for at in range...]
  transfers between devices with their start and end apart: 6 -> 5, of which waited for: 4 -> 4; matrix products, arithmetic and copies ran while one was open for 1% -> 1% of each run, Pallas kernels for 12% -> 9%
where the time goes in v7:
time: 77.2 us; the launch traced here: 76.6 us
  blocking collectives  41.7 us (54%)
  Pallas kernels  17.4 us (23%)
  starting transfers between devices  11.2 us (15%)
  waiting for transfers between devices  4.92 us (6%)
    all_to_all x2, blocking collectives, share(): return lax.all_to_all(values, GROUP, 0, 0)  16.8 us
    all_to_all x1, blocking collectives, kernel_body(): got = lax.all_to_all(sent, 'block', 0, 0)  14.3 us
    all_to_all x1, blocking collectives, kernel_body(): first = lax.all_to_all(sent, 'block', 0, 0)  10.5 us
    all_to_all x1, starting transfers between devices, kernel_body(): teacher_own = lax.all_to_all(teacher_sent, CHIPS, 0, 0)  8.32 us
    pallas_call x1, Pallas kernels, kernel_body(): call(directions_kernel, (shape((count, width), bf16), pltpu.HBM((count, w...  4.04 us
    ppermute x1, starting transfers between devices, groups_back(): lax.ppermute(values, 'group', [(at, (at + back) % GROUPS) for at in range...  2.82 us
    ppermute x1, waiting for transfers between devices, groups_back(): lax.ppermute(values, 'group', [(at, (at + back) % GROUPS) for at in range...  2.29 us
    pallas_call x1, Pallas kernels, kernel_body(): call(functools.partial(other_teacher_kernel, prototypes), (shape((count,...  2.2 us
  transfers between devices with their start and end apart: 5, of which 4 were waited for; matrix products, arithmetic and copies ran while one was open for 1% of the time, Pallas kernels for 9%

profile of v7, /device:TPU:0, one launch (start us, length us, event | category | flops | bytes accessed | tf_op | source)
XLA Modules:
  0.0 76.6 jit_solution(10148819143435527710)
XLA Ops:
  0.6 1.6 %shard_map.68 = (bf16[16,32,256]{2,1,0:T(8,128)(2,1)}, bf16[32,256]{1,0:T(8,128)(2,1)S(1)}) custom-call(bf16[32,256]{1,0:T(8,128)(2,1)} %teacher_ref.2, bf16[32,256]{1,0:T(8,128)(2,1)} %student_ref.5), custom_call_target="tpu_custom_call" | custom-call | tf_op jit(solution)/shard_map/pallas_call | solution.py:473
  2.2 8.3 %all-to-all-start = ((bf16[16,32,256]{2,1,0:T(8,128)(2,1)}), bf16[16,32,256]{2,1,0:T(8,128)(2,1)S(1)}, u32[]{:S(2)}, u32[]{:S(2)}) async-start(bf16[16,32,256]{2,1,0:T(8,128)(2,1)} %get-tuple-element.29), calls=%async_computation | async-start | bytes 524288 | tf_op jit(solution)/shard_map/all_to_all | solution.py:479
  10.5 0.7 fusion.1.refs_0_
  11.2 2.8 %collective-permute-start = (bf16[48,256]{1,0:T(8,128)(2,1)S(1)}, bf16[48,256]{1,0:T(8,128)(2,1)S(1)}, u32[]{:S(2)}, u32[]{:S(2)}) collective-permute-start(bf16[48,256]{1,0:T(8,128)(2,1)S(1)} %fusion.1.refs_0_), channel_id=1, source_target_pairs={{0,16},{16,0},{1,17},{17,1},{2,18},{18,2},{3,19},{19,3},{4,20},{20... | collective-permute-start | bytes 73736 | tf_op jit(solution)/shard_map/ppermute | solution.py:482
  14.0 4.0 %shard_map.69 = (bf16[2048,256]{1,0:T(8,128)(2,1)S(1)}, bf16[2048,256]{1,0:T(8,128)(2,1)}, f32[1,2048]{1,0:T(1,128)S(1)}) custom-call(s32[1]{0:T(128)} %bitcast.block_ref, bf16[256,16384]{1,0:T(8,128)(2,1)} %teacher_ref.3, bf16[256,16384]{1,0:T(8,128)(2,1)} %directions_ref.1), custom_call_target="tpu_custom_call" | custom-call | flops 6291456 | bytes 4194304 | tf_op jit(solution)/shard_map/pallas_call | solution.py:493
  18.1 2.3 %collective-permute-done.refs_1_ = bf16[48,256]{1,0:T(8,128)(2,1)S(1)} collective-permute-done((bf16[48,256]{1,0:T(8,128)(2,1)S(1)}, bf16[48,256]{1,0:T(8,128)(2,1)S(1)}, u32[]{:S(2)}, u32[]{:S(2)}) %collective-permute-start) | collective-permute-done | bytes 24608 | tf_op jit(solution)/shard_map/ppermute | solution.py:482
  20.4 1.0 %all-to-all-done.got_ref = bf16[16,32,256]{2,1,0:T(8,128)(2,1)S(1)} async-done(((bf16[16,32,256]{2,1,0:T(8,128)(2,1)}), bf16[16,32,256]{2,1,0:T(8,128)(2,1)S(1)}, u32[]{:S(2)}, u32[]{:S(2)}) %all-to-all-start) | async-done | bytes 262176 | tf_op jit(solution)/shard_map/all_to_all | solution.py:479
  21.4 0.0 collective-permute-start.1
  21.4 0.7 shard_map.70.own_ref
  22.1 0.8 %collective-permute-done.1.got_ref = bf16[16,32,256]{2,1,0:T(8,128)(2,1)S(1)} collective-permute-done((bf16[16,32,256]{2,1,0:T(8,128)(2,1)S(1)}, bf16[16,32,256]{2,1,0:T(8,128)(2,1)S(1)}, u32[]{:S(2)}, u32[]{:S(2)}) %collective-permute-start.1) | collective-permute-done | bytes 262176 | tf_op jit(solution)/shard_map/ppermute | solution.py:466
  22.9 2.2 %shard_map.71 = (f32[2048,512]{1,0:T(8,128)S(1)}, bf16[8,80,256]{2,1,0:T(8,128)(2,1)S(1)}, bf16[2048,256]{1,0:T(8,128)(2,1)S(1)}) custom-call(bf16[2048,256]{1,0:T(8,128)(2,1)S(1)} %get-tuple-element.32.teacher_w_ref, bf16[16,32,256]{2,1,0:T(8,128)(2,1)S(1)} %collective-permute-done.1.got_ref, f32[2048,512]{1,0:T(8,128)S(1)} %shard_map.70.own_ref, ...), custom_call_target="tpu_custom_call" | custom-call | flops 536870912 | tf_op jit(solution)/shard_map/pallas_call | solution.py:521
  25.1 10.5 %all_to_all.25.got_ref = bf16[8,80,256]{2,1,0:T(8,128)(2,1)S(1)} all-to-all(bf16[8,80,256]{2,1,0:T(8,128)(2,1)S(1)} %get-tuple-element.38), channel_id=1, replica_groups=mesh['group'=2,'block'=8,'fsdp'=2] {'block'}, dimensions={0} | all-to-all | bytes 655360 | tf_op jit(solution)/shard_map/all_to_all | solution.py:532
  35.7 0.0 collective-permute-start.2
  35.7 0.8 %shard_map.72 = (f32[2048,512]{1,0:T(8,128)S(1)}, f32[8,512]{1,0:T(8,128)S(1)}, bf16[256,512]{1,0:T(8,128)(2,1)S(1)}) custom-call(bf16[2048,256]{1,0:T(8,128)(2,1)S(1)} %get-tuple-element.39.student_w_ref, bf16[8,80,256]{2,1,0:T(8,128)(2,1)S(1)} %all_to_all.25.got_ref), custom_call_target="tpu_custom_call" | custom-call | flops 536870912 | tf_op jit(solution)/shard_map/pallas_call | solution.py:535
  36.5 0.8 %collective-permute-done.2.got_ref.other_got_ref = bf16[8,80,256]{2,1,0:T(8,128)(2,1)S(1)} collective-permute-done((bf16[8,80,256]{2,1,0:T(8,128)(2,1)S(1)}, bf16[8,80,256]{2,1,0:T(8,128)(2,1)S(1)}, u32[]{:S(2)}, u32[]{:S(2)}) %collective-permute-start.2) | collective-permute-done | bytes 327712 | tf_op jit(solution)/shard_map/ppermute | solution.py:466
  37.3 0.8 %shard_map.73 = (f32[2048,512]{1,0:T(8,128)S(1)}, f32[8,128]{1,0:T(8,128)S(1)}, bf16[256,512]{1,0:T(8,128)(2,1)S(1)}) custom-call(bf16[2048,256]{1,0:T(8,128)(2,1)S(1)} %get-tuple-element.39.student_w_ref, bf16[8,80,256]{2,1,0:T(8,128)(2,1)S(1)} %collective-permute-done.2.got_ref.other_got_ref, f32[8,512]{1,0:T(8,128)S(1)} %get-tuple-element.40.own_part_ref), custom_call_target="tpu_custom_call" | custom-call | flops 536870912 | tf_op jit(solution)/shard_map/pallas_call | solution.py:541
  38.1 1.2 %shard_map.74 = (bf16[16,16,128]{2,1,0:T(8,128)(2,1)S(1)}, f32[8,128]{1,0:T(8,128)S(1)}) custom-call(f32[2048,512]{1,0:T(8,128)S(1)} %shard_map.70.own_ref, f32[2048,512]{1,0:T(8,128)S(1)} %get-tuple-element.37.other_ref, bf16[8,80,256]{2,1,0:T(8,128)(2,1)S(1)} %all_to_all.25.got_ref, bf16[8,80,256]{2,1,0:T(8,128)(2,1)S(1)} %collective-permute-done.2.got_ref.other_got_ref, ...), custom_call_target="tpu_custom_call" | custom-call | flops 8388608 | tf_op jit(solution)/shard_map/pallas_call | solution.py:547
  39.3 8.4 %all_to_all.26.got_ref.second_ref = bf16[16,16,128]{2,1,0:T(8,128)(2,1)S(1)} all-to-all(bf16[16,16,128]{2,1,0:T(8,128)(2,1)S(1)} %get-tuple-element.42), channel_id=1, replica_groups=mesh['group'=2,'block'=8,'fsdp'=2] {'block','fsdp'}, dimensions={0} | all-to-all | bytes 131072 | tf_op jit(solution)/shard_map/all_to_all | solution.py:469
  47.7 1.3 %shard_map.75 = (bf16[16,16,128]{2,1,0:T(8,128)(2,1)S(1)}, f32[2048,512]{1,0:T(8,128)S(1)}, f32[2048,512]{1,0:T(8,128)S(1)}, bf16[4,256,512]{2,1,0:T(8,128)(2,1)S(1)}) custom-call(f32[2048,512]{1,0:T(8,128)S(1)} %shard_map.70.own_ref, f32[2048,512]{1,0:T(8,128)S(1)} %get-tuple-element.37.other_ref, bf16[16,16,128]{2,1,0:T(8,128)(2,1)S(1)} %all_to_all.26.got_ref.second_ref, ...), custom_call_target="tpu_custom_call" | custom-call | flops 8388608 | tf_op jit(solution)/shard_map/pallas_call | solution.py:553
  49.0 8.4 %all_to_all.27.third_ref = bf16[16,16,128]{2,1,0:T(8,128)(2,1)S(1)} all-to-all(bf16[16,16,128]{2,1,0:T(8,128)(2,1)S(1)} %get-tuple-element.48), channel_id=1, replica_groups=mesh['group'=2,'block'=8,'fsdp'=2] {'block','fsdp'}, dimensions={0} | all-to-all | bytes 131072 | tf_op jit(solution)/shard_map/all_to_all | solution.py:469
  57.4 2.0 %shard_map.76 = (bf16[2,2048,512]{2,1,0:T(8,128)(2,1)S(1)}, f32[256,256]{1,0:T(8,128)S(1)}, bf16[256,256]{1,0:T(8,128)(2,1)S(1)}) custom-call(f32[2048,512]{1,0:T(8,128)S(1)} %get-tuple-element.43.own_mass_ref, f32[2048,512]{1,0:T(8,128)S(1)} %get-tuple-element.44.other_mass_ref, f32[2048,512]{1,0:T(8,128)S(1)} %get-tuple-element.45.own_student_ref, ...), custom_call_target="tpu_custom_call" | custom-call | flops 536870912 | tf_op jit(solution)/shard_map/pallas_call | solution.py:567
  59.4 0.1 collective-permute-start.3
  59.5 0.0 copy-start
  59.5 1.6 %shard_map.77._ = bf16[8,16,2560]{2,1,0:T(8,128)(2,1)S(1)} custom-call(bf16[2,2048,512]{2,1,0:T(8,128)(2,1)S(1)} %get-tuple-element.53.gradient_ref, bf16[256,512]{1,0:T(8,128)(2,1)S(1)} %get-tuple-element.54.own_turned_ref, bf16[256,512]{1,0:T(8,128)(2,1)S(1)} %get-tuple-element.55.other_turned_ref, f32[1,2048]{1,0:T(1,128)S(1)} %get-tuple-element.49.inverse_ref, ...), custom_call_target="tpu_custom_call" | custom-call | flops 1073741824 | tf_op jit(solution)/shard_map/pallas_call | solution.py:577
  61.1 0.0 collective-permute-done.3.other_ref
  61.1 0.1 shard_map.78
  61.2 14.3 %all_to_all.28.got_ref = bf16[8,16,2560]{2,1,0:T(8,128)(2,1)S(1)} all-to-all(bf16[8,16,2560]{2,1,0:T(8,128)(2,1)S(1)} %shard_map.78), channel_id=1, replica_groups=mesh['group'=2,'block'=8,'fsdp'=2] {'block'}, dimensions={0} | all-to-all | bytes 1310720 | tf_op jit(solution)/shard_map/all_to_all | solution.py:592
  75.5 0.0 copy-done
  75.5 1.1 %shard_map.79 = (f32[16,16384]{1,0:T(8,128)}, f32[32,256]{1,0:T(8,128)}) custom-call(bf16[8,16,2560]{2,1,0:T(8,128)(2,1)S(1)} %all_to_all.28.got_ref, bf16[32,256]{1,0:T(8,128)(2,1)S(1)} %copy-done), custom_call_target="tpu_custom_call" | custom-call | tf_op jit(solution)/shard_map/pallas_call | solution.py:593
Async XLA Ops:
  2.2 19.2 %all-to-all-start = ((bf16[16,32,256]{2,1,0:T(8,128)(2,1)}), bf16[16,32,256]{2,1,0:T(8,128)(2,1)S(1)}, u32[]{:S(2)}, u32[]{:S(2)}) async-start(bf16[16,32,256]{2,1,0:T(8,128)(2,1)} %get-tuple-element.29), calls=%async_computation | async-start | bytes 524288 | tf_op jit(solution)/shard_map/all_to_all | solution.py:479
  11.2 9.2 %collective-permute-start = (bf16[48,256]{1,0:T(8,128)(2,1)S(1)}, bf16[48,256]{1,0:T(8,128)(2,1)S(1)}, u32[]{:S(2)}, u32[]{:S(2)}) collective-permute-start(bf16[48,256]{1,0:T(8,128)(2,1)S(1)} %fusion.1.refs_0_), channel_id=1, source_target_pairs={{0,16},{16,0},{1,17},{17,1},{2,18},{18,2},{3,19},{19,3},{4,20},{20... | collective-permute-start | bytes 73736 | tf_op jit(solution)/shard_map/ppermute | solution.py:482
  21.4 1.5 %collective-permute-start.1 = (bf16[16,32,256]{2,1,0:T(8,128)(2,1)S(1)}, bf16[16,32,256]{2,1,0:T(8,128)(2,1)S(1)}, u32[]{:S(2)}, u32[]{:S(2)}) collective-permute-start(bf16[16,32,256]{2,1,0:T(8,128)(2,1)S(1)} %all-to-all-done.got_ref), channel_id=1, source_target_pairs={{0,1},{1,0},{2,3},{3,2},{4,5},{5,4},{6,7},{7,6},{8,9},{9,8},{10,11... | collective-permute-start | bytes 786440 | tf_op jit(solution)/shard_map/ppermute | solution.py:466
  35.7 1.6 %collective-permute-start.2 = (bf16[8,80,256]{2,1,0:T(8,128)(2,1)S(1)}, bf16[8,80,256]{2,1,0:T(8,128)(2,1)S(1)}, u32[]{:S(2)}, u32[]{:S(2)}) collective-permute-start(bf16[8,80,256]{2,1,0:T(8,128)(2,1)S(1)} %all_to_all.25.got_ref), channel_id=1, source_target_pairs={{0,1},{1,0},{2,3},{3,2},{4,5},{5,4},{6,7},{7,6},{8,9},{9,8},{10,11... | collective-permute-start | bytes 983048 | tf_op jit(solution)/shard_map/ppermute | solution.py:466
  59.4 1.7 %collective-permute-start.3 = (bf16[256,256]{1,0:T(8,128)(2,1)S(1)}, bf16[256,256]{1,0:T(8,128)(2,1)S(1)}, u32[]{:S(2)}, u32[]{:S(2)}) collective-permute-start(bf16[256,256]{1,0:T(8,128)(2,1)S(1)} %get-tuple-element.52), channel_id=1, source_target_pairs={{0,1},{1,0},{2,3},{3,2},{4,5},{5,4},{6,7},{7,6},{8,9},{9,8},{10,11... | collective-permute-start | bytes 393224 | tf_op jit(solution)/shard_map/ppermute | solution.py:466
  59.5 16.0 %copy-start = (bf16[32,256]{1,0:T(8,128)(2,1)S(1)}, bf16[32,256]{1,0:T(8,128)(2,1)}, u32[]{:S(2)}) copy-start(bf16[32,256]{1,0:T(8,128)(2,1)} %student_ref.5) | copy-start | bytes 49156

commit v8 on v7

--- a/solution.py
+++ b/solution.py
@@ -254,10 +254,8 @@
         mass_ref[here, :] = exponentials(teacher_w_ref[here, :], units, teacher_temp)
 
 
-def other_teacher_kernel(prototypes, teacher_w_ref, got_ref, own_ref, student_hbm, *refs):
-    *student_refs, mass_ref, sent_ref, student_w_ref, sem = refs
-    copy = pltpu.make_async_copy(student_hbm, student_w_ref, sem)
-    copy.start()
+def other_teacher_kernel(prototypes, teacher_w_ref, got_ref, own_ref, *refs):
+    *student_refs, mass_ref, sent_ref = refs
     chips, rows = sent_ref.shape[0], got_ref.shape[1]
     placed = placed_weights(student_refs, 2 * own_ref.shape[1] // LANES, rows, chips)
     units = units_of(got_ref)
@@ -279,7 +277,6 @@
             sent_ref[chip] = values
 
     in_core_order(lax.axis_index("fsdp"), own_total, total, finish)
-    copy.wait()
 
 
 def own_student_kernel(student_w_ref, got_ref, mass_ref, part_ref, turned_ref, units_ref):
@@ -494,7 +491,7 @@
         directions_kernel,
         (
             shape((count, width), bf16),
-            pltpu.HBM((count, width), bf16),
+            shape((count, width), bf16),
             shape((1, count), f32),
         ),
         flops=12 * count * width,
@@ -518,17 +515,14 @@
     pieces = count // (FETCH * TILE)
     quarter = dict(flops=elements * width, exps=elements // 2)
     own_mass = call(own_teacher_kernel, shape((count, half), f32), **quarter)(teacher_w, teacher_own)
-    other_mass, sent, student_w = call(
+    other_mass, sent = call(
         functools.partial(other_teacher_kernel, prototypes),
         (
             shape((count, half), f32),
             shape((blocks, GROUPS * rows + 2 * lines, width), bf16),
-            shape((count, width), bf16),
         ),
-        in_specs=[vmem] * 3 + [anyspace] + [vmem] * GROUPS,
-        scratch_shapes=[dma],
         **quarter,
-    )(teacher_w, teacher_other, own_mass, hbm(student_w), *student_units)
+    )(teacher_w, teacher_other, own_mass, *student_units)
     first = lax.all_to_all(sent, "block", 0, 0)
     first_other = swap(first)
     units = pltpu.VMEM((half, width), bf16)

time: 77.2 us -> 76.5 us (level)
  Pallas kernels: 17.4 us -> 15.6 us
  waiting for transfers between devices: 4.92 us -> 5.99 us
    pallas_call x1, Pallas kernels: 4.04 us -> 2.96 us  [kernel_body(): call(directions_kernel, (shape((count, width), bf16), shape((count, width...]
    ppermute x1, waiting for transfers between devices: 2.29 us -> 3.36 us  [groups_back(): lax.ppermute(values, 'group', [(at, (at + back) % GROUPS) for at in range...]
  transfers between devices with their start and end apart: 5 -> 5, of which waited for: 4 -> 4; matrix products, arithmetic and copies ran while one was open for 1% -> 1% of each run, Pallas kernels for 9% -> 8%
where the time goes in v8:
time: 76.5 us; the launch traced here: 75.9 us
  blocking collectives  41.7 us (55%)
  Pallas kernels  15.6 us (20%)
  starting transfers between devices  11.2 us (15%)
  waiting for transfers between devices  5.99 us (8%)
    all_to_all x2, blocking collectives, share(): return lax.all_to_all(values, GROUP, 0, 0)  16.8 us
    all_to_all x1, blocking collectives, kernel_body(): got = lax.all_to_all(sent, 'block', 0, 0)  14.3 us
    all_to_all x1, blocking collectives, kernel_body(): first = lax.all_to_all(sent, 'block', 0, 0)  10.5 us
    all_to_all x1, starting transfers between devices, kernel_body(): teacher_own = lax.all_to_all(teacher_sent, CHIPS, 0, 0)  8.32 us
    ppermute x1, waiting for transfers between devices, groups_back(): lax.ppermute(values, 'group', [(at, (at + back) % GROUPS) for at in range...  3.36 us
    pallas_call x1, Pallas kernels, kernel_body(): call(directions_kernel, (shape((count, width), bf16), shape((count, width...  2.96 us
    ppermute x1, starting transfers between devices, groups_back(): lax.ppermute(values, 'group', [(at, (at + back) % GROUPS) for at in range...  2.82 us
    pallas_call x1, Pallas kernels, kernel_body(): call(gradient_kernel, (shape((2, count, half), bf16), shape((half // GROU...  1.98 us
  transfers between devices with their start and end apart: 5, of which 4 were waited for; matrix products, arithmetic and copies ran while one was open for 1% of the time, Pallas kernels for 8%

profile of v8, /device:TPU:0, one launch (start us, length us, event | category | flops | bytes accessed | tf_op | source)
XLA Modules:
  0.0 75.9 jit_solution(14166120535624927982)
XLA Ops:
  0.6 1.6 %shard_map.68 = (bf16[16,32,256]{2,1,0:T(8,128)(2,1)}, bf16[32,256]{1,0:T(8,128)(2,1)S(1)}) custom-call(bf16[32,256]{1,0:T(8,128)(2,1)} %teacher_ref.2, bf16[32,256]{1,0:T(8,128)(2,1)} %student_ref.5), custom_call_target="tpu_custom_call" | custom-call | tf_op jit(solution)/shard_map/pallas_call | solution.py:470
  2.2 8.3 %all-to-all-start = ((bf16[16,32,256]{2,1,0:T(8,128)(2,1)}), bf16[16,32,256]{2,1,0:T(8,128)(2,1)S(1)}, u32[]{:S(2)}, u32[]{:S(2)}) async-start(bf16[16,32,256]{2,1,0:T(8,128)(2,1)} %get-tuple-element.28), calls=%async_computation | async-start | bytes 524288 | tf_op jit(solution)/shard_map/all_to_all | solution.py:476
  10.5 0.7 fusion.1.refs_0_
  11.2 2.8 %collective-permute-start = (bf16[48,256]{1,0:T(8,128)(2,1)S(1)}, bf16[48,256]{1,0:T(8,128)(2,1)S(1)}, u32[]{:S(2)}, u32[]{:S(2)}) collective-permute-start(bf16[48,256]{1,0:T(8,128)(2,1)S(1)} %fusion.1.refs_0_), channel_id=1, source_target_pairs={{0,16},{16,0},{1,17},{17,1},{2,18},{18,2},{3,19},{19,3},{4,20},{20... | collective-permute-start | bytes 73736 | tf_op jit(solution)/shard_map/ppermute | solution.py:479
  14.0 3.0 %shard_map.69 = (bf16[2048,256]{1,0:T(8,128)(2,1)S(1)}, bf16[2048,256]{1,0:T(8,128)(2,1)S(1)}, f32[1,2048]{1,0:T(1,128)S(1)}) custom-call(s32[1]{0:T(128)} %bitcast.block_ref, bf16[256,16384]{1,0:T(8,128)(2,1)} %teacher_ref.3, bf16[256,16384]{1,0:T(8,128)(2,1)} %directions_ref.1), custom_call_target="tpu_custom_call" | custom-call | flops 6291456 | bytes 4194304 | tf_op jit(solution)/shard_map/pallas_call | solution.py:490
  17.0 3.4 %collective-permute-done.refs_1_ = bf16[48,256]{1,0:T(8,128)(2,1)S(1)} collective-permute-done((bf16[48,256]{1,0:T(8,128)(2,1)S(1)}, bf16[48,256]{1,0:T(8,128)(2,1)S(1)}, u32[]{:S(2)}, u32[]{:S(2)}) %collective-permute-start) | collective-permute-done | bytes 24608 | tf_op jit(solution)/shard_map/ppermute | solution.py:479
  20.4 1.0 %all-to-all-done.got_ref = bf16[16,32,256]{2,1,0:T(8,128)(2,1)S(1)} async-done(((bf16[16,32,256]{2,1,0:T(8,128)(2,1)}), bf16[16,32,256]{2,1,0:T(8,128)(2,1)S(1)}, u32[]{:S(2)}, u32[]{:S(2)}) %all-to-all-start) | async-done | bytes 262176 | tf_op jit(solution)/shard_map/all_to_all | solution.py:476
  21.4 0.0 collective-permute-start.1
  21.4 0.7 shard_map.70.own_ref
  22.1 0.8 %collective-permute-done.1.got_ref = bf16[16,32,256]{2,1,0:T(8,128)(2,1)S(1)} collective-permute-done((bf16[16,32,256]{2,1,0:T(8,128)(2,1)S(1)}, bf16[16,32,256]{2,1,0:T(8,128)(2,1)S(1)}, u32[]{:S(2)}, u32[]{:S(2)}) %collective-permute-start.1) | collective-permute-done | bytes 262176 | tf_op jit(solution)/shard_map/ppermute | solution.py:463
  22.9 1.5 %shard_map.71 = (f32[2048,512]{1,0:T(8,128)S(1)}, bf16[8,80,256]{2,1,0:T(8,128)(2,1)S(1)}) custom-call(bf16[2048,256]{1,0:T(8,128)(2,1)S(1)} %get-tuple-element.31.teacher_w_ref, bf16[16,32,256]{2,1,0:T(8,128)(2,1)S(1)} %collective-permute-done.1.got_ref, f32[2048,512]{1,0:T(8,128)S(1)} %shard_map.70.own_ref, bf16[48,256]{1,0:T(8,128)(2,1)S(1)} %fusion.1.refs_0_, ...), custom_call_target="tpu_custom_call" | custom-call | flops 536870912 | tf_op jit(solution)/shard_map/pallas_call | solution.py:518
  24.4 10.5 %all_to_all.25.got_ref = bf16[8,80,256]{2,1,0:T(8,128)(2,1)S(1)} all-to-all(bf16[8,80,256]{2,1,0:T(8,128)(2,1)S(1)} %get-tuple-element.36), channel_id=1, replica_groups=mesh['group'=2,'block'=8,'fsdp'=2] {'block'}, dimensions={0} | all-to-all | bytes 655360 | tf_op jit(solution)/shard_map/all_to_all | solution.py:526
  34.9 0.0 collective-permute-start.2
  34.9 0.8 %shard_map.72 = (f32[2048,512]{1,0:T(8,128)S(1)}, f32[8,512]{1,0:T(8,128)S(1)}, bf16[256,512]{1,0:T(8,128)(2,1)S(1)}) custom-call(bf16[2048,256]{1,0:T(8,128)(2,1)S(1)} %get-tuple-element.37.student_w_ref, bf16[8,80,256]{2,1,0:T(8,128)(2,1)S(1)} %all_to_all.25.got_ref), custom_call_target="tpu_custom_call" | custom-call | flops 536870912 | tf_op jit(solution)/shard_map/pallas_call | solution.py:529
  35.7 0.8 %collective-permute-done.2.got_ref.other_got_ref = bf16[8,80,256]{2,1,0:T(8,128)(2,1)S(1)} collective-permute-done((bf16[8,80,256]{2,1,0:T(8,128)(2,1)S(1)}, bf16[8,80,256]{2,1,0:T(8,128)(2,1)S(1)}, u32[]{:S(2)}, u32[]{:S(2)}) %collective-permute-start.2) | collective-permute-done | bytes 327712 | tf_op jit(solution)/shard_map/ppermute | solution.py:463
  36.5 0.8 %shard_map.73 = (f32[2048,512]{1,0:T(8,128)S(1)}, f32[8,128]{1,0:T(8,128)S(1)}, bf16[256,512]{1,0:T(8,128)(2,1)S(1)}) custom-call(bf16[2048,256]{1,0:T(8,128)(2,1)S(1)} %get-tuple-element.37.student_w_ref, bf16[8,80,256]{2,1,0:T(8,128)(2,1)S(1)} %collective-permute-done.2.got_ref.other_got_ref, f32[8,512]{1,0:T(8,128)S(1)} %get-tuple-element.38.own_part_ref), custom_call_target="tpu_custom_call" | custom-call | flops 536870912 | tf_op jit(solution)/shard_map/pallas_call | solution.py:535
  37.4 1.2 %shard_map.74 = (bf16[16,16,128]{2,1,0:T(8,128)(2,1)S(1)}, f32[8,128]{1,0:T(8,128)S(1)}) custom-call(f32[2048,512]{1,0:T(8,128)S(1)} %shard_map.70.own_ref, f32[2048,512]{1,0:T(8,128)S(1)} %get-tuple-element.35.other_ref, bf16[8,80,256]{2,1,0:T(8,128)(2,1)S(1)} %all_to_all.25.got_ref, bf16[8,80,256]{2,1,0:T(8,128)(2,1)S(1)} %collective-permute-done.2.got_ref.other_got_ref, ...), custom_call_target="tpu_custom_call" | custom-call | flops 8388608 | tf_op jit(solution)/shard_map/pallas_call | solution.py:541
  38.5 8.4 %all_to_all.26.got_ref.second_ref = bf16[16,16,128]{2,1,0:T(8,128)(2,1)S(1)} all-to-all(bf16[16,16,128]{2,1,0:T(8,128)(2,1)S(1)} %get-tuple-element.40), channel_id=1, replica_groups=mesh['group'=2,'block'=8,'fsdp'=2] {'block','fsdp'}, dimensions={0} | all-to-all | bytes 131072 | tf_op jit(solution)/shard_map/all_to_all | solution.py:466
  46.9 1.3 %shard_map.75 = (bf16[16,16,128]{2,1,0:T(8,128)(2,1)S(1)}, f32[2048,512]{1,0:T(8,128)S(1)}, f32[2048,512]{1,0:T(8,128)S(1)}, bf16[4,256,512]{2,1,0:T(8,128)(2,1)S(1)}) custom-call(f32[2048,512]{1,0:T(8,128)S(1)} %shard_map.70.own_ref, f32[2048,512]{1,0:T(8,128)S(1)} %get-tuple-element.35.other_ref, bf16[16,16,128]{2,1,0:T(8,128)(2,1)S(1)} %all_to_all.26.got_ref.second_ref, ...), custom_call_target="tpu_custom_call" | custom-call | flops 8388608 | tf_op jit(solution)/shard_map/pallas_call | solution.py:547
  48.2 8.4 %all_to_all.27.third_ref = bf16[16,16,128]{2,1,0:T(8,128)(2,1)S(1)} all-to-all(bf16[16,16,128]{2,1,0:T(8,128)(2,1)S(1)} %get-tuple-element.46), channel_id=1, replica_groups=mesh['group'=2,'block'=8,'fsdp'=2] {'block','fsdp'}, dimensions={0} | all-to-all | bytes 131072 | tf_op jit(solution)/shard_map/all_to_all | solution.py:466
  56.6 2.0 %shard_map.76 = (bf16[2,2048,512]{2,1,0:T(8,128)(2,1)S(1)}, f32[256,256]{1,0:T(8,128)S(1)}, bf16[256,256]{1,0:T(8,128)(2,1)S(1)}) custom-call(f32[2048,512]{1,0:T(8,128)S(1)} %get-tuple-element.41.own_mass_ref, f32[2048,512]{1,0:T(8,128)S(1)} %get-tuple-element.42.other_mass_ref, f32[2048,512]{1,0:T(8,128)S(1)} %get-tuple-element.43.own_student_ref, ...), custom_call_target="tpu_custom_call" | custom-call | flops 536870912 | tf_op jit(solution)/shard_map/pallas_call | solution.py:561
  58.6 0.1 collective-permute-start.3
  58.7 0.0 copy-start
  58.7 1.6 %shard_map.77._ = bf16[8,16,2560]{2,1,0:T(8,128)(2,1)S(1)} custom-call(bf16[2,2048,512]{2,1,0:T(8,128)(2,1)S(1)} %get-tuple-element.51.gradient_ref, bf16[256,512]{1,0:T(8,128)(2,1)S(1)} %get-tuple-element.52.own_turned_ref, bf16[256,512]{1,0:T(8,128)(2,1)S(1)} %get-tuple-element.53.other_turned_ref, f32[1,2048]{1,0:T(1,128)S(1)} %get-tuple-element.47.inverse_ref, ...), custom_call_target="tpu_custom_call" | custom-call | flops 1073741824 | tf_op jit(solution)/shard_map/pallas_call | solution.py:571
  60.3 0.0 collective-permute-done.3.other_ref
  60.3 0.1 shard_map.78
  60.4 14.3 %all_to_all.28.got_ref = bf16[8,16,2560]{2,1,0:T(8,128)(2,1)S(1)} all-to-all(bf16[8,16,2560]{2,1,0:T(8,128)(2,1)S(1)} %shard_map.78), channel_id=1, replica_groups=mesh['group'=2,'block'=8,'fsdp'=2] {'block'}, dimensions={0} | all-to-all | bytes 1310720 | tf_op jit(solution)/shard_map/all_to_all | solution.py:586
  74.7 0.0 copy-done
  74.7 1.1 %shard_map.79 = (f32[16,16384]{1,0:T(8,128)}, f32[32,256]{1,0:T(8,128)}) custom-call(bf16[8,16,2560]{2,1,0:T(8,128)(2,1)S(1)} %all_to_all.28.got_ref, bf16[32,256]{1,0:T(8,128)(2,1)S(1)} %copy-done), custom_call_target="tpu_custom_call" | custom-call | tf_op jit(solution)/shard_map/pallas_call | solution.py:587
Async XLA Ops:
  2.2 19.2 %all-to-all-start = ((bf16[16,32,256]{2,1,0:T(8,128)(2,1)}), bf16[16,32,256]{2,1,0:T(8,128)(2,1)S(1)}, u32[]{:S(2)}, u32[]{:S(2)}) async-start(bf16[16,32,256]{2,1,0:T(8,128)(2,1)} %get-tuple-element.28), calls=%async_computation | async-start | bytes 524288 | tf_op jit(solution)/shard_map/all_to_all | solution.py:476
  11.2 9.2 %collective-permute-start = (bf16[48,256]{1,0:T(8,128)(2,1)S(1)}, bf16[48,256]{1,0:T(8,128)(2,1)S(1)}, u32[]{:S(2)}, u32[]{:S(2)}) collective-permute-start(bf16[48,256]{1,0:T(8,128)(2,1)S(1)} %fusion.1.refs_0_), channel_id=1, source_target_pairs={{0,16},{16,0},{1,17},{17,1},{2,18},{18,2},{3,19},{19,3},{4,20},{20... | collective-permute-start | bytes 73736 | tf_op jit(solution)/shard_map/ppermute | solution.py:479
  21.4 1.5 %collective-permute-start.1 = (bf16[16,32,256]{2,1,0:T(8,128)(2,1)S(1)}, bf16[16,32,256]{2,1,0:T(8,128)(2,1)S(1)}, u32[]{:S(2)}, u32[]{:S(2)}) collective-permute-start(bf16[16,32,256]{2,1,0:T(8,128)(2,1)S(1)} %all-to-all-done.got_ref), channel_id=1, source_target_pairs={{0,1},{1,0},{2,3},{3,2},{4,5},{5,4},{6,7},{7,6},{8,9},{9,8},{10,11... | collective-permute-start | bytes 786440 | tf_op jit(solution)/shard_map/ppermute | solution.py:463
  34.9 1.6 %collective-permute-start.2 = (bf16[8,80,256]{2,1,0:T(8,128)(2,1)S(1)}, bf16[8,80,256]{2,1,0:T(8,128)(2,1)S(1)}, u32[]{:S(2)}, u32[]{:S(2)}) collective-permute-start(bf16[8,80,256]{2,1,0:T(8,128)(2,1)S(1)} %all_to_all.25.got_ref), channel_id=1, source_target_pairs={{0,1},{1,0},{2,3},{3,2},{4,5},{5,4},{6,7},{7,6},{8,9},{9,8},{10,11... | collective-permute-start | bytes 983048 | tf_op jit(solution)/shard_map/ppermute | solution.py:463
  58.6 1.7 %collective-permute-start.3 = (bf16[256,256]{1,0:T(8,128)(2,1)S(1)}, bf16[256,256]{1,0:T(8,128)(2,1)S(1)}, u32[]{:S(2)}, u32[]{:S(2)}) collective-permute-start(bf16[256,256]{1,0:T(8,128)(2,1)S(1)} %get-tuple-element.50), channel_id=1, source_target_pairs={{0,1},{1,0},{2,3},{3,2},{4,5},{5,4},{6,7},{7,6},{8,9},{9,8},{10,11... | collective-permute-start | bytes 393224 | tf_op jit(solution)/shard_map/ppermute | solution.py:463
  58.7 16.0 %copy-start = (bf16[32,256]{1,0:T(8,128)(2,1)S(1)}, bf16[32,256]{1,0:T(8,128)(2,1)}, u32[]{:S(2)}) copy-start(bf16[32,256]{1,0:T(8,128)(2,1)} %student_ref.5) | copy-start | bytes 49156

commit v9 on v5

--- a/solution.py
+++ b/solution.py
@@ -135,7 +135,7 @@
     )
 
 
-def units_kernel(teacher_ref, student_ref, sent_ref, teacher_vmem, student_vmem, sems):
+def units_kernel(teacher_ref, student_ref, units_out, teacher_vmem, student_vmem, sems):
     copies = [
         pltpu.make_async_copy(teacher_ref, teacher_vmem, sems.at[0]),
         pltpu.make_async_copy(student_ref, student_vmem, sems.at[1]),
@@ -145,11 +145,30 @@
     for copy in copies:
         copy.wait()
     width = teacher_vmem.shape[1]
-    teacher = unit_rows(teacher_vmem[...])[0].astype(jnp.bfloat16)
-    student = unit_rows(student_vmem[...])[0].astype(jnp.bfloat16)
+    units_out[:, :width] = unit_rows(teacher_vmem[...])[0].astype(jnp.bfloat16)
+    units_out[:, width:] = unit_rows(student_vmem[...])[0].astype(jnp.bfloat16)
+
+
+def spread_kernel(*refs):
+    *unit_refs, sent_ref = refs
+    values = jnp.concatenate([ref[...] for ref in unit_refs], axis=0)
     for chip in range(sent_ref.shape[0]):
-        sent_ref[chip, :, :width] = teacher
-        sent_ref[chip, :, width:] = student
+        sent_ref[chip] = values
+
+
+def placed_weights(weight_refs, lines, rows, chips):
+    group, block = lax.axis_index("group"), lax.axis_index("block")
+    line = lax.broadcasted_iota(jnp.int32, (lines, LANES), 0)
+    part = lax.broadcasted_iota(jnp.int32, (lines, LANES), 1) // rows
+    each = LANES // rows
+    placed = jnp.zeros((lines, LANES), jnp.float32)
+    for back, ref in enumerate(weight_refs):
+        at = lax.axis_index("fsdp") * chips * GROUPS + ((group + GROUPS - back) % GROUPS) * chips + block
+        weights = ref[:, :rows].astype(jnp.float32)[0:1, :]
+        weights = jnp.concatenate([weights] * each, axis=1)
+        here = (line == at // each) & (part == at % each)
+        placed = placed + jnp.where(here, jnp.broadcast_to(weights, (lines, LANES)), 0.0)
+    return placed
 
 
 def directions_kernel(block_ref, teacher_ref, student_ref, teacher_out, student_out, inverse_out):
@@ -207,75 +226,75 @@
     return line[:, :half], line[:, half:]
 
 
-def received(got_ref):
-    total = got_ref[0].astype(jnp.float32)
+def received(got_ref, at=0):
+    total = got_ref[0, at:, :].astype(jnp.float32)
     for device in range(1, got_ref.shape[0]):
-        total = total + got_ref[device].astype(jnp.float32)
+        total = total + got_ref[device, at:, :].astype(jnp.float32)
     return total
 
 
-def units_of(got_ref, width, side):
-    chips, rows, _ = got_ref.shape
-    return got_ref[:, :, side * width : (side + 1) * width].reshape(chips * rows, width)
+def in_chip_order(got_ref, teacher_ref, student_ref):
+    chips = got_ref.shape[0]
+    width = teacher_ref.shape[1]
+    rows = teacher_ref.shape[0] // (GROUPS * chips)
+    group = lax.axis_index("group")
+    for back in range(GROUPS):
+        for chip in range(chips):
+            at = (((group + GROUPS - back) % GROUPS) * chips + chip) * rows
+            here = pl.ds(pl.multiple_of(at, rows), rows)
+            teacher_ref[here, :] = got_ref[chip, back * rows : (back + 1) * rows, :width]
+            student_ref[here, :] = got_ref[chip, back * rows : (back + 1) * rows, width:]
 
 
 def turn(units):
     return jnp.transpose(units.astype(jnp.float32)).astype(jnp.bfloat16)
 
 
-def own_kernel(teacher_w_ref, student_hbm, got_ref, teacher_ref, student_ref, student_w_ref, part_ref, turned_ref, sems):
-    count, width = teacher_w_ref.shape
-    span = FETCH * TILE
-    copies = []
-    for piece in range(count // span):
-        rows = pl.ds(piece * span, span)
-        copies.append(pltpu.make_async_copy(student_hbm.at[rows], student_w_ref.at[rows], sems.at[piece]))
-        copies[-1].start()
-    teacher, student = units_of(got_ref, width, 0), units_of(got_ref, width, 1)
-    turned_ref[...] = turn(student)
+def own_kernel(
+    teacher_w_ref, student_w_ref, got_ref, teacher_ref, student_ref, part_ref, turned_ref, teacher_units, student_units
+):
+    in_chip_order(got_ref, teacher_units, student_units)
+    turned_ref[...] = turn(student_units[...])
     part = 0.0
-    for start in range(0, count, HALF_TILE):
+    for start in range(0, teacher_ref.shape[0], HALF_TILE):
         here = slice(start, start + HALF_TILE)
-        teacher_ref[here, :] = exponentials(teacher_w_ref[here, :], teacher, teacher_temp)
-        if start % span == 0:
-            copies[start // span].wait()
-        mass = exponentials(student_w_ref[here, :], student, student_temp)
+        teacher_ref[here, :] = exponentials(teacher_w_ref[here, :], teacher_units[...], teacher_temp)
+        mass = exponentials(student_w_ref[here, :], student_units[...], student_temp)
         student_ref[here, :] = mass
         part = part + fold(mass)
     part_ref[...] = part
 
 
-def other_kernel(
-    prototypes, teacher_w_ref, student_w_ref, got_ref, own_ref, own_part_ref, weight_ref,
-    teacher_ref, student_ref, sent_ref, part_ref, turned_ref,
-):
-    count, width = teacher_w_ref.shape
-    core = lax.axis_index("fsdp")
-    teacher, student = units_of(got_ref, width, 0), units_of(got_ref, width, 1)
-    turned_ref[...] = turn(student)
+def other_kernel(prototypes, teacher_w_ref, student_w_ref, got_ref, own_ref, own_part_ref, *refs):
+    weight_refs = refs[:GROUPS]
+    teacher_ref, student_ref, sent_ref, part_ref, turned_ref, teacher_units, student_units = refs[GROUPS:]
+    chips = got_ref.shape[0]
+    in_chip_order(got_ref, teacher_units, student_units)
+    turned_ref[...] = turn(student_units[...])
+    half = own_ref.shape[1]
+    placed = placed_weights(weight_refs, 2 * half // LANES, half // (GROUPS * chips), chips)
     own_total = total = part = 0.0
-    for start in range(0, count, HALF_TILE):
+    for start in range(0, teacher_ref.shape[0], HALF_TILE):
         here = slice(start, start + HALF_TILE)
-        mass = exponentials(teacher_w_ref[here, :], teacher, teacher_temp)
+        mass = exponentials(teacher_w_ref[here, :], teacher_units[...], teacher_temp)
         teacher_ref[here, :] = mass
         own = own_ref[here, :]
-        proto = jnp.sum(own + mass, axis=1, keepdims=True)
-        scale = 1.0 / (prototypes * proto)
+        scale = 1.0 / (prototypes * jnp.sum(own + mass, axis=1, keepdims=True))
         own_total = own_total + fold(own * scale)
         total = total + fold(mass * scale)
-        mass = exponentials(student_w_ref[here, :], student, student_temp)
+        mass = exponentials(student_w_ref[here, :], student_units[...], student_temp)
         student_ref[here, :] = mass
         part = part + fold(mass)
 
     def finish(first, second):
-        send(sent_ref, sums(first[0], second[0]), weight_ref[...])
+        send(sent_ref, sums(first[0], second[0]), placed)
         part_ref[...] = sums(first[1], second[1])
 
-    in_core_order(core, (own_total, own_part_ref[...]), (total, part), finish)
-
-
-def sweep(prototypes, crops, first_ref, second_ref, got_ref, scaled_refs=None):
-    first_crop, second_crop = halves(1.0 / (crops * received(got_ref)[: crops // LANES]))
+    in_core_order(lax.axis_index("fsdp"), (own_total, own_part_ref[...]), (total, part), finish)
+
+
+def sweep(prototypes, crops, first_ref, second_ref, received_sums, scaled_refs=None):
+    first_crop, second_crop = halves(1.0 / (crops * received_sums))
     first_total = second_total = 0.0
     for start in range(0, first_ref.shape[0], TILE):
         here = slice(start, start + TILE)
@@ -290,9 +309,13 @@
     return sums(first_total, second_total)
 
 
-def sweep_kernel(prototypes, crops, own_ref, other_ref, got_ref, part_ref, sent_ref):
+def sweep_kernel(prototypes, crops, own_ref, other_ref, got_ref, part_ref, sent_ref, weight_ref):
+    lines = crops // LANES
+    extra = received(got_ref)
+    weight_ref[...] = extra[lines:]
+
     def body(first_ref, second_ref):
-        send(sent_ref, sweep(prototypes, crops, first_ref, second_ref, got_ref), part_ref[...])
+        send(sent_ref, sweep(prototypes, crops, first_ref, second_ref, extra[:lines]), part_ref[...])
 
     in_core_order(lax.axis_index("fsdp"), own_ref, other_ref, body)
 
@@ -308,9 +331,12 @@
         copies.append(pltpu.make_async_copy(directions_ref.at[:, columns], copy_ref.at[piece], sems.at[piece]))
         copies[-1].start()
 
+    total = received(got_ref)[: crops // LANES]
+
     def body(first_refs, second_refs):
         (first_ref, *scaled_refs), (second_ref, second_scaled_ref) = first_refs, second_refs
-        send(sent_ref, sweep(prototypes, crops, first_ref, second_ref, got_ref, (*scaled_refs, second_scaled_ref)))
+        sent = sweep(prototypes, crops, first_ref, second_ref, total, (*scaled_refs, second_scaled_ref))
+        send(sent_ref, sent)
 
     in_core_order(lax.axis_index("fsdp"), (own_ref, own_scaled_ref), (other_ref, other_scaled_ref), body)
     for copy in copies:
@@ -324,14 +350,14 @@
 
 
 def gradient_kernel(
-    own_mass_ref, other_mass_ref, own_student_ref, other_student_ref, first_ref, second_ref, third_ref,
+    own_mass_ref, other_mass_ref, own_student_ref, other_student_ref, weight_ref, second_ref, third_ref,
     inverse_ref, copy_ref, gradient_ref, keep_ref, give_ref, unit_ref,
 ):
     group, core = lax.axis_index("group"), lax.axis_index("fsdp")
     count, half = own_mass_ref.shape
     lines = 2 * half // LANES
-    weights = received(first_ref)[lines:] / student_temp
-    teacher_scales = halves(weights / received(third_ref))
+    weights = weight_ref[...] / student_temp
+    teacher_scales = halves(weights / received(third_ref)[:lines])
     student_scales = halves(weights / received(second_ref)[lines:])
 
     def body(first_refs, second_refs):
@@ -385,26 +411,19 @@
     copy.wait()
 
 
-def outputs_kernel(got_ref, student_ref, weight_out, feature_out, wide_ref, sems):
+def outputs_kernel(got_ref, student_ref, weight_out, feature_out):
     chips, rows_each, columns = got_ref.shape
     rows, width = student_ref.shape
     pieces = rows // rows_each
     count = columns - pieces * width
-    copies = []
-    for chip in range(chips):
-        here = slice(chip * count, (chip + 1) * count)
-        wide_ref[:, here] = got_ref[chip, :, :count].astype(jnp.float32)
-        here = pl.ds(chip * count, count)
-        copies.append(pltpu.make_async_copy(wide_ref.at[:, here], weight_out.at[:, here], sems.at[chip]))
-        copies[-1].start()
     total = got_ref[0, :, count:].astype(jnp.float32)
     for chip in range(1, chips):
         total = total + got_ref[chip, :, count:].astype(jnp.float32)
     total = jnp.concatenate([total[:, piece * width : (piece + 1) * width] for piece in range(pieces)], axis=0)
     hat, length = unit_rows(student_ref[...])
     feature_out[...] = (total - hat * jnp.sum(hat * total, axis=1, keepdims=True)) / length
-    for copy in copies:
-        copy.wait()
+    for chip in range(chips):
+        weight_out[:, chip * count : (chip + 1) * count] = got_ref[chip, :, :count].astype(jnp.float32)
 
 
 def kernel_body(teacher_feat, student_feat, crop_weight, teacher_v, student_v):
@@ -432,19 +451,20 @@
 
     dma = pltpu.SemaphoreType.DMA
     hbm = functools.partial(pltpu.with_memory_space_constraint, memory_space=pltpu.HBM)
-    sent = call(
+    units = call(
         units_kernel,
-        shape((chips, rows, 2 * width), bf16),
+        shape((rows, 2 * width), bf16),
         in_specs=[pl.BlockSpec(memory_space=pl.ANY)] * 2,
         scratch_shapes=[pltpu.VMEM((rows, width), bf16), pltpu.VMEM((rows, width), bf16), dma((2,))],
     )(hbm(teacher_feat), hbm(student_feat))
-    own = lax.all_to_all(sent, CHIPS, 0, 0)
-
-    device = (core[0] * chips + group[0] * blocks + block[0]) * rows
-    weights = lax.dynamic_update_slice(jnp.zeros((crops,), f32), crop_weight.astype(f32), (device,)).reshape(lines, LANES)
-    placed = weights
-    for move in range(1, GROUPS):
-        placed = placed + lax.ppermute(weights, "group", [(at, (at + move) % GROUPS) for at in range(GROUPS)])
+
+    def of_groups(values):
+        return [values] + [
+            lax.ppermute(values, "group", [(at, (at + back) % GROUPS) for at in range(GROUPS)]) for back in range(1, GROUPS)
+        ]
+
+    units = of_groups(units)
+    weights = of_groups(jnp.pad(crop_weight[None, :], ((0, 15), (0, width - rows))))
 
     span = 2 * TILE
     spans = count // span
@@ -455,7 +475,7 @@
         directions_kernel,
         (
             shape((count, width), bf16),
-            pltpu.HBM((count, width), bf16),
+            shape((count, width), bf16),
             shape((1, count), f32),
         ),
         flops=12 * count * width,
@@ -472,25 +492,26 @@
         hbm(student_v),
     )
 
-    own, teacher_w, placed = lax.optimization_barrier((own, teacher_w, placed))
+    units, weights, teacher_w = lax.optimization_barrier((units, weights, teacher_w))
+    sent = call(spread_kernel, shape((blocks, GROUPS * rows, 2 * width), bf16))(*units)
+    own = lax.all_to_all(sent, "block", 0, 0)
     other = swap(own)
     half = crops // 2
     anyspace = pl.BlockSpec(memory_space=pl.ANY)
     pieces = count // (FETCH * TILE)
     halved = dict(flops=2 * elements * width, exps=elements)
-    own_mass, own_student, student_w, own_part, own_turned = call(
+    units = pltpu.VMEM((half, width), bf16)
+    own_mass, own_student, own_part, own_turned = call(
         own_kernel,
         (
             shape((count, half), f32),
             shape((count, half), f32),
-            shape((count, width), bf16),
             shape((8, half), f32),
             shape((width, half), bf16),
         ),
-        in_specs=[vmem, anyspace, vmem],
-        scratch_shapes=[dma((pieces,))],
+        scratch_shapes=[units, units],
         **halved,
-    )(teacher_w, hbm(student_w), own)
+    )(teacher_w, student_w, own)
     other_mass, other_student, sent, student_part, other_turned = call(
         functools.partial(other_kernel, prototypes),
         (
@@ -500,15 +521,14 @@
             shape((lines, LANES), f32),
             shape((width, half), bf16),
         ),
-        in_specs=[vmem] * 6,
+        scratch_shapes=[units, units],
         **halved,
-    )(teacher_w, student_w, other, own_mass, own_part, placed)
+    )(teacher_w, student_w, other, own_mass, own_part, *weights)
     first = share(sent)
-    sent = call(
+    sent, weights = call(
         functools.partial(sweep_kernel, prototypes, crops),
-        shape((members, 2 * lines, LANES), bf16),
+        (shape((members, 2 * lines, LANES), bf16), shape((lines, LANES), f32)),
         flops=4 * elements,
-        in_specs=[vmem] * 4,
     )(own_mass, other_mass, first, student_part)
     second = share(sent)
     sent, own_scaled, other_scaled, student_copy = call(
@@ -531,7 +551,7 @@
         flops=2 * elements * width // GROUPS,
         in_specs=[vmem] * 9,
         scratch_shapes=[pltpu.VMEM((width, count), bf16)],
-    )(own_scaled, other_scaled, own_student, other_student, first, second, third, inverse, student_copy)
+    )(own_scaled, other_scaled, own_student, other_student, weights, second, third, inverse, student_copy)
     other = swap(give)
     out_rows = width // chips
     per_chip = rows * width // out_rows
@@ -552,10 +572,7 @@
     )(keep, other, sent)
     got = lax.all_to_all(sent, "block", 0, 0)
     return call(
-        outputs_kernel,
-        (shape((out_rows, kept), f32), shape((rows, width), f32)),
-        out_specs=[anyspace, vmem],
-        scratch_shapes=[pltpu.VMEM((out_rows, kept), f32), dma((blocks,))],
+        outputs_kernel, (shape((out_rows, kept), f32), shape((rows, width), f32))
     )(got, student_feat)
 
 

time: 79.4 us -> 74.7 us (0.941)
  blocking collectives: 39.8 us -> 51.9 us
  starting transfers between devices: 11.2 us -> 4.19 us
  waiting for transfers between devices: 7.58 us -> 2.13 us
  Pallas kernels: 18.6 us -> 14.6 us
    all_to_all x0 -> x1, blocking collectives: none -> 12.6 us  [kernel_body(): own = lax.all_to_all(sent, 'block', 0, 0)]
    all_to_all x1 -> x0, starting transfers between devices: 8.32 us -> none  [kernel_body(): own = lax.all_to_all(sent, CHIPS, 0, 0)]
    ppermute x1 -> x2, waiting for transfers between devices: 6.92 us -> 1.56 us  [of_groups(): lax.ppermute(values, 'group', [(at, (at + back) % GROUPS) for at in range...]
    pallas_call x3 -> x4, Pallas kernels: 6.9 us -> 5.02 us  [the longest x1 2.96 us: kernel_body(): call(directions_kernel, (shape((count, width), bf16), shape((count, width...]
    pallas_call x1, Pallas kernels: 2.78 us -> 1.34 us  [kernel_body(): call(own_kernel, (shape((count, half), f32), shape((count, half), f32), s...]
    ppermute x1 -> x2, starting transfers between devices: 2.81 us -> 4.12 us  [of_groups(): lax.ppermute(values, 'group', [(at, (at + back) % GROUPS) for at in range...]
  transfers between devices with their start and end apart: 4 -> 4, of which waited for: 2 -> 2; matrix products, arithmetic and copies ran while one was open for 1% -> 1% of each run, Pallas kernels for 11% -> 8%
where the time goes in v9:
time: 74.7 us; the launch traced here: 74.3 us
  blocking collectives  51.9 us (69%)
  Pallas kernels  14.6 us (20%)
  starting transfers between devices  4.19 us (6%)
  waiting for transfers between devices  2.13 us (3%)
    all_to_all x3, blocking collectives, share(): return lax.all_to_all(values, GROUP, 0, 0)  25 us
    all_to_all x1, blocking collectives, kernel_body(): got = lax.all_to_all(sent, 'block', 0, 0)  14.3 us
    all_to_all x1, blocking collectives, kernel_body(): own = lax.all_to_all(sent, 'block', 0, 0)  12.6 us
    ppermute x2, starting transfers between devices, of_groups(): lax.ppermute(values, 'group', [(at, (at + back) % GROUPS) for at in range...  4.12 us
    pallas_call x1, Pallas kernels, kernel_body(): call(directions_kernel, (shape((count, width), bf16), shape((count, width...  2.96 us
    pallas_call x1, Pallas kernels, kernel_body(): call(functools.partial(other_kernel, prototypes), (shape((count, half), f...  2.21 us
    pallas_call x1, Pallas kernels, kernel_body(): call(gradient_kernel, (shape((2, count, half), bf16), shape((half // GROU...  1.99 us
    pallas_call x1, Pallas kernels, kernel_body(): call(weight_kernel, shape((blocks, out_rows, count + per_chip), bf16), fl...  1.6 us
  transfers between devices with their start and end apart: 4, of which 2 were waited for; matrix products, arithmetic and copies ran while one was open for 1% of the time, Pallas kernels for 8%

profile of v9, /device:TPU:0, one launch (start us, length us, event | category | flops | bytes accessed | tf_op | source)
XLA Modules:
  0.0 74.3 jit_solution(9369681044584859598)
XLA Ops:
  0.6 0.9 %shard_map.68.refs_0_ = bf16[32,512]{1,0:T(8,128)(2,1)S(1)} custom-call(bf16[32,256]{1,0:T(8,128)(2,1)} %teacher_ref.2, bf16[32,256]{1,0:T(8,128)(2,1)} %student_ref.5), custom_call_target="tpu_custom_call" | custom-call | tf_op jit(solution)/shard_map/pallas_call | solution.py:454
  1.5 4.1 %collective-permute-start = (bf16[32,512]{1,0:T(8,128)(2,1)S(1)}, bf16[32,512]{1,0:T(8,128)(2,1)S(1)}, u32[]{:S(2)}, u32[]{:S(2)}) collective-permute-start(bf16[32,512]{1,0:T(8,128)(2,1)S(1)} %shard_map.68.refs_0_), channel_id=1, source_target_pairs={{0,16},{16,0},{1,17},{17,1},{2,18},{18,2},{3,19},{19,3},{4,20},{20... | collective-permute-start | bytes 98312 | tf_op jit(solution)/shard_map/ppermute | solution.py:463
  5.6 0.7 pad.4.refs_0_
  6.3 0.0 collective-permute-start.1
  6.3 3.0 %shard_map.69 = (bf16[2048,256]{1,0:T(8,128)(2,1)S(1)}, bf16[2048,256]{1,0:T(8,128)(2,1)S(1)}, f32[1,2048]{1,0:T(1,128)S(1)}) custom-call(s32[1]{0:T(128)} %bitcast.1.block_ref, bf16[256,16384]{1,0:T(8,128)(2,1)} %teacher_ref.3, bf16[256,16384]{1,0:T(8,128)(2,1)} %directions_ref.1), custom_call_target="tpu_custom_call" | custom-call | flops 6291456 | bytes 4194304 | tf_op jit(solution)/shard_map/pallas_call | solution.py:474
  9.2 1.6 %collective-permute-done.1.refs_1_ = bf16[16,256]{1,0:T(8,128)(2,1)S(1)} collective-permute-done((bf16[16,256]{1,0:T(8,128)(2,1)S(1)}, bf16[16,256]{1,0:T(8,128)(2,1)S(1)}, u32[]{:S(2)}, u32[]{:S(2)}) %collective-permute-start.1) | collective-permute-done | bytes 8224 | tf_op jit(solution)/shard_map/ppermute | solution.py:463
  10.8 0.0 collective-permute-done.refs_1_
  10.8 12.6 %all_to_all.25.got_ref = bf16[8,64,512]{2,1,0:T(8,128)(2,1)S(1)} all-to-all(bf16[8,64,512]{2,1,0:T(8,128)(2,1)S(1)} %shard_map.70), channel_id=1, replica_groups=mesh['group'=2,'block'=8,'fsdp'=2] {'block'}, dimensions={0} | all-to-all | bytes 1048576 | tf_op jit(solution)/shard_map/all_to_all | solution.py:497
  23.4 0.0 collective-permute-start.2
  23.4 1.3 %shard_map.71 = (f32[2048,512]{1,0:T(8,128)S(1)}, f32[2048,512]{1,0:T(8,128)S(1)}, f32[8,512]{1,0:T(8,128)S(1)}, bf16[256,512]{1,0:T(8,128)(2,1)S(1)}) custom-call(bf16[2048,256]{1,0:T(8,128)(2,1)S(1)} %get-tuple-element.29.teacher_w_ref, bf16[2048,256]{1,0:T(8,128)(2,1)S(1)} %get-tuple-element.30.student_w_ref, bf16[8,64,512]{2,1,0:T(8,128)(2,1)S(1)} %all_to_all.25.got_ref), custom_call_target="tpu_custom_call" | custom-call | flops 1073741824 | tf_op jit(solution)/shard_map/pallas_call | solution.py:504
  24.8 0.6 collective-permute-done.2.got_ref
  25.3 2.2 %shard_map.72 = (f32[2048,512]{1,0:T(8,128)S(1)}, f32[2048,512]{1,0:T(8,128)S(1)}, bf16[16,16,128]{2,1,0:T(8,128)(2,1)S(1)}, f32[8,128]{1,0:T(8,128)S(1)}, bf16[256,512]{1,0:T(8,128)(2,1)S(1)}) custom-call(bf16[2048,256]{1,0:T(8,128)(2,1)S(1)} %get-tuple-element.29.teacher_w_ref, bf16[2048,256]{1,0:T(8,128)(2,1)S(1)} %get-tuple-element.30.student_w_ref, ...), custom_call_target="tpu_custom_call" | custom-call | flops 1073741824 | tf_op jit(solution)/shard_map/pallas_call | solution.py:515
  27.5 8.4 %all_to_all.26.got_ref = bf16[16,16,128]{2,1,0:T(8,128)(2,1)S(1)} all-to-all(bf16[16,16,128]{2,1,0:T(8,128)(2,1)S(1)} %get-tuple-element.38), channel_id=1, replica_groups=mesh['group'=2,'block'=8,'fsdp'=2] {'block','fsdp'}, dimensions={0} | all-to-all | bytes 131072 | tf_op jit(solution)/shard_map/all_to_all | solution.py:450
  35.9 1.2 %shard_map.73 = (bf16[16,16,128]{2,1,0:T(8,128)(2,1)S(1)}, f32[8,128]{1,0:T(8,128)S(1)}) custom-call(f32[2048,512]{1,0:T(8,128)S(1)} %get-tuple-element.33.own_ref, f32[2048,512]{1,0:T(8,128)S(1)} %get-tuple-element.37.other_ref, bf16[16,16,128]{2,1,0:T(8,128)(2,1)S(1)} %all_to_all.26.got_ref, f32[8,128]{1,0:T(8,128)S(1)} %get-tuple-element.39.part_ref), custom_call_target="tpu_custom_call" | custom-call | flops 8388608 | tf_op jit(solution)/shard_map/pallas_call | solution.py:528
  37.1 8.4 %all_to_all.27.got_ref.second_ref = bf16[16,16,128]{2,1,0:T(8,128)(2,1)S(1)} all-to-all(bf16[16,16,128]{2,1,0:T(8,128)(2,1)S(1)} %get-tuple-element.40), channel_id=1, replica_groups=mesh['group'=2,'block'=8,'fsdp'=2] {'block','fsdp'}, dimensions={0} | all-to-all | bytes 131072 | tf_op jit(solution)/shard_map/all_to_all | solution.py:450
  45.5 1.3 %shard_map.74 = (bf16[16,8,128]{2,1,0:T(8,128)(2,1)S(1)}, f32[2048,512]{1,0:T(8,128)S(1)}, f32[2048,512]{1,0:T(8,128)S(1)}, bf16[4,256,512]{2,1,0:T(8,128)(2,1)S(1)}) custom-call(f32[2048,512]{1,0:T(8,128)S(1)} %get-tuple-element.33.own_ref, f32[2048,512]{1,0:T(8,128)S(1)} %get-tuple-element.37.other_ref, ...), custom_call_target="tpu_custom_call" | custom-call | flops 8388608 | tf_op jit(solution)/shard_map/pallas_call | solution.py:534
  46.8 8.2 %all_to_all.28.third_ref = bf16[16,8,128]{2,1,0:T(8,128)(2,1)S(1)} all-to-all(bf16[16,8,128]{2,1,0:T(8,128)(2,1)S(1)} %get-tuple-element.46), channel_id=1, replica_groups=mesh['group'=2,'block'=8,'fsdp'=2] {'block','fsdp'}, dimensions={0} | all-to-all | bytes 65536 | tf_op jit(solution)/shard_map/all_to_all | solution.py:450
  55.0 2.0 %shard_map.75 = (bf16[2,2048,512]{2,1,0:T(8,128)(2,1)S(1)}, f32[256,256]{1,0:T(8,128)S(1)}, bf16[256,256]{1,0:T(8,128)(2,1)S(1)}) custom-call(f32[2048,512]{1,0:T(8,128)S(1)} %get-tuple-element.41.own_mass_ref, f32[2048,512]{1,0:T(8,128)S(1)} %get-tuple-element.42.other_mass_ref, f32[2048,512]{1,0:T(8,128)S(1)} %get-tuple-element.43.own_student_ref, ...), custom_call_target="tpu_custom_call" | custom-call | flops 536870912 | tf_op jit(solution)/shard_map/pallas_call | solution.py:548
  57.0 0.1 collective-permute-start.3
  57.1 0.0 copy-start
  57.1 1.6 %shard_map.76._ = bf16[8,16,2560]{2,1,0:T(8,128)(2,1)S(1)} custom-call(bf16[2,2048,512]{2,1,0:T(8,128)(2,1)S(1)} %get-tuple-element.51.gradient_ref, bf16[256,512]{1,0:T(8,128)(2,1)S(1)} %get-tuple-element.52.own_turned_ref, bf16[256,512]{1,0:T(8,128)(2,1)S(1)} %get-tuple-element.53.other_turned_ref, f32[1,2048]{1,0:T(1,128)S(1)} %get-tuple-element.47.inverse_ref, ...), custom_call_target="tpu_custom_call" | custom-call | flops 1073741824 | tf_op jit(solution)/shard_map/pallas_call | solution.py:558
  58.7 0.0 collective-permute-done.3.other_ref
  58.7 0.1 shard_map.77
  58.8 14.3 %all_to_all.29.got_ref = bf16[8,16,2560]{2,1,0:T(8,128)(2,1)S(1)} all-to-all(bf16[8,16,2560]{2,1,0:T(8,128)(2,1)S(1)} %shard_map.77), channel_id=1, replica_groups=mesh['group'=2,'block'=8,'fsdp'=2] {'block'}, dimensions={0} | all-to-all | bytes 1310720 | tf_op jit(solution)/shard_map/all_to_all | solution.py:573
  73.1 0.0 copy-done
  73.1 1.1 %shard_map.78 = (f32[16,16384]{1,0:T(8,128)}, f32[32,256]{1,0:T(8,128)}) custom-call(bf16[8,16,2560]{2,1,0:T(8,128)(2,1)S(1)} %all_to_all.29.got_ref, bf16[32,256]{1,0:T(8,128)(2,1)S(1)} %copy-done), custom_call_target="tpu_custom_call" | custom-call | tf_op jit(solution)/shard_map/pallas_call | solution.py:574
  (1 shorter events, 0.0 us)
Async XLA Ops:
  1.5 9.3 %collective-permute-start = (bf16[32,512]{1,0:T(8,128)(2,1)S(1)}, bf16[32,512]{1,0:T(8,128)(2,1)S(1)}, u32[]{:S(2)}, u32[]{:S(2)}) collective-permute-start(bf16[32,512]{1,0:T(8,128)(2,1)S(1)} %shard_map.68.refs_0_), channel_id=1, source_target_pairs={{0,16},{16,0},{1,17},{17,1},{2,18},{18,2},{3,19},{19,3},{4,20},{20... | collective-permute-start | bytes 98312 | tf_op jit(solution)/shard_map/ppermute | solution.py:463
  6.3 4.5 %collective-permute-start.1 = (bf16[16,256]{1,0:T(8,128)(2,1)S(1)}, bf16[16,256]{1,0:T(8,128)(2,1)S(1)}, u32[]{:S(2)}, u32[]{:S(2)}) collective-permute-start(bf16[16,256]{1,0:T(8,128)(2,1)S(1)} %pad.4.refs_0_), channel_id=1, source_target_pairs={{0,16},{16,0},{1,17},{17,1},{2,18},{18,2},{3,19},{19,3},{4,20},{20... | collective-permute-start | bytes 24584 | tf_op jit(solution)/shard_map/ppermute | solution.py:463
  23.4 1.9 %collective-permute-start.2 = (bf16[8,64,512]{2,1,0:T(8,128)(2,1)S(1)}, bf16[8,64,512]{2,1,0:T(8,128)(2,1)S(1)}, u32[]{:S(2)}, u32[]{:S(2)}) collective-permute-start(bf16[8,64,512]{2,1,0:T(8,128)(2,1)S(1)} %all_to_all.25.got_ref), channel_id=1, source_target_pairs={{0,1},{1,0},{2,3},{3,2},{4,5},{5,4},{6,7},{7,6},{8,9},{9,8},{10,11... | collective-permute-start | bytes 1572872 | tf_op jit(solution)/shard_map/ppermute | solution.py:447
  57.0 1.7 %collective-permute-start.3 = (bf16[256,256]{1,0:T(8,128)(2,1)S(1)}, bf16[256,256]{1,0:T(8,128)(2,1)S(1)}, u32[]{:S(2)}, u32[]{:S(2)}) collective-permute-start(bf16[256,256]{1,0:T(8,128)(2,1)S(1)} %get-tuple-element.50), channel_id=1, source_target_pairs={{0,1},{1,0},{2,3},{3,2},{4,5},{5,4},{6,7},{7,6},{8,9},{9,8},{10,11... | collective-permute-start | bytes 393224 | tf_op jit(solution)/shard_map/ppermute | solution.py:447
  57.1 16.0 %copy-start = (bf16[32,256]{1,0:T(8,128)(2,1)S(1)}, bf16[32,256]{1,0:T(8,128)(2,1)}, u32[]{:S(2)}) copy-start(bf16[32,256]{1,0:T(8,128)(2,1)} %student_ref.5) | copy-start | bytes 49156

commit v10 on v9

--- a/solution.py
+++ b/solution.py
@@ -135,36 +135,41 @@
     )
 
 
-def units_kernel(teacher_ref, student_ref, units_out, teacher_vmem, student_vmem, sems):
+def units_kernel(teacher_ref, student_ref, weight_ref, units_out, teacher_vmem, student_vmem, weight_vmem, sems):
     copies = [
         pltpu.make_async_copy(teacher_ref, teacher_vmem, sems.at[0]),
         pltpu.make_async_copy(student_ref, student_vmem, sems.at[1]),
+        pltpu.make_async_copy(weight_ref, weight_vmem, sems.at[2]),
     ]
     for copy in copies:
         copy.start()
     for copy in copies:
         copy.wait()
-    width = teacher_vmem.shape[1]
-    units_out[:, :width] = unit_rows(teacher_vmem[...])[0].astype(jnp.bfloat16)
-    units_out[:, width:] = unit_rows(student_vmem[...])[0].astype(jnp.bfloat16)
+    rows, width = teacher_vmem.shape
+    units_out[:rows, :width] = unit_rows(teacher_vmem[...])[0].astype(jnp.bfloat16)
+    units_out[:rows, width:] = unit_rows(student_vmem[...])[0].astype(jnp.bfloat16)
+    weights = weight_vmem[...].astype(jnp.float32)
+    weights = jnp.concatenate([weights, jnp.zeros((1, 2 * width - rows), jnp.float32)], axis=1)
+    units_out[rows:, :] = jnp.broadcast_to(weights, (units_out.shape[0] - rows, 2 * width)).astype(jnp.bfloat16)
 
 
 def spread_kernel(*refs):
     *unit_refs, sent_ref = refs
-    values = jnp.concatenate([ref[...] for ref in unit_refs], axis=0)
+    rows = sent_ref.shape[1] // GROUPS
+    values = jnp.concatenate([ref[:rows, :] for ref in unit_refs], axis=0)
     for chip in range(sent_ref.shape[0]):
         sent_ref[chip] = values
 
 
-def placed_weights(weight_refs, lines, rows, chips):
+def placed_weights(unit_refs, lines, rows, chips):
     group, block = lax.axis_index("group"), lax.axis_index("block")
     line = lax.broadcasted_iota(jnp.int32, (lines, LANES), 0)
     part = lax.broadcasted_iota(jnp.int32, (lines, LANES), 1) // rows
     each = LANES // rows
     placed = jnp.zeros((lines, LANES), jnp.float32)
-    for back, ref in enumerate(weight_refs):
+    for back, ref in enumerate(unit_refs):
         at = lax.axis_index("fsdp") * chips * GROUPS + ((group + GROUPS - back) % GROUPS) * chips + block
-        weights = ref[:, :rows].astype(jnp.float32)[0:1, :]
+        weights = ref[rows:, :LANES].astype(jnp.float32)[0:1, :rows]
         weights = jnp.concatenate([weights] * each, axis=1)
         here = (line == at // each) & (part == at % each)
         placed = placed + jnp.where(here, jnp.broadcast_to(weights, (lines, LANES)), 0.0)
@@ -266,13 +271,13 @@
 
 
 def other_kernel(prototypes, teacher_w_ref, student_w_ref, got_ref, own_ref, own_part_ref, *refs):
-    weight_refs = refs[:GROUPS]
+    unit_refs = refs[:GROUPS]
     teacher_ref, student_ref, sent_ref, part_ref, turned_ref, teacher_units, student_units = refs[GROUPS:]
     chips = got_ref.shape[0]
     in_chip_order(got_ref, teacher_units, student_units)
     turned_ref[...] = turn(student_units[...])
     half = own_ref.shape[1]
-    placed = placed_weights(weight_refs, 2 * half // LANES, half // (GROUPS * chips), chips)
+    placed = placed_weights(unit_refs, 2 * half // LANES, half // (GROUPS * chips), chips)
     own_total = total = part = 0.0
     for start in range(0, teacher_ref.shape[0], HALF_TILE):
         here = slice(start, start + HALF_TILE)
@@ -453,10 +458,10 @@
     hbm = functools.partial(pltpu.with_memory_space_constraint, memory_space=pltpu.HBM)
     units = call(
         units_kernel,
-        shape((rows, 2 * width), bf16),
-        in_specs=[pl.BlockSpec(memory_space=pl.ANY)] * 2,
-        scratch_shapes=[pltpu.VMEM((rows, width), bf16), pltpu.VMEM((rows, width), bf16), dma((2,))],
-    )(hbm(teacher_feat), hbm(student_feat))
+        shape((rows + 16, 2 * width), bf16),
+        in_specs=[pl.BlockSpec(memory_space=pl.ANY)] * 3,
+        scratch_shapes=[pltpu.VMEM((rows, width), bf16)] * 2 + [pltpu.VMEM((1, rows), bf16), dma((3,))],
+    )(hbm(teacher_feat), hbm(student_feat), hbm(crop_weight[None, :]))
 
     def of_groups(values):
         return [values] + [
@@ -464,7 +469,6 @@
         ]
 
     units = of_groups(units)
-    weights = of_groups(jnp.pad(crop_weight[None, :], ((0, 15), (0, width - rows))))
 
     span = 2 * TILE
     spans = count // span
@@ -492,7 +496,7 @@
         hbm(student_v),
     )
 
-    units, weights, teacher_w = lax.optimization_barrier((units, weights, teacher_w))
+    units, teacher_w = lax.optimization_barrier((units, teacher_w))
     sent = call(spread_kernel, shape((blocks, GROUPS * rows, 2 * width), bf16))(*units)
     own = lax.all_to_all(sent, "block", 0, 0)
     other = swap(own)
@@ -500,7 +504,7 @@
     anyspace = pl.BlockSpec(memory_space=pl.ANY)
     pieces = count // (FETCH * TILE)
     halved = dict(flops=2 * elements * width, exps=elements)
-    units = pltpu.VMEM((half, width), bf16)
+    scratch = [pltpu.VMEM((half, width), bf16)] * 2
     own_mass, own_student, own_part, own_turned = call(
         own_kernel,
         (
@@ -509,7 +513,7 @@
             shape((8, half), f32),
             shape((width, half), bf16),
         ),
-        scratch_shapes=[units, units],
+        scratch_shapes=scratch,
         **halved,
     )(teacher_w, student_w, own)
     other_mass, other_student, sent, student_part, other_turned = call(
@@ -521,9 +525,9 @@
             shape((lines, LANES), f32),
             shape((width, half), bf16),
         ),
-        scratch_shapes=[units, units],
+        scratch_shapes=scratch,
         **halved,
-    )(teacher_w, student_w, other, own_mass, own_part, *weights)
+    )(teacher_w, student_w, other, own_mass, own_part, *units)
     first = share(sent)
     sent, weights = call(
         functools.partial(sweep_kernel, prototypes, crops),

time: 74.7 us -> 73.6 us (0.985)
  waiting for transfers between devices: 2.13 us -> 0.57 us
  blocking collectives: 51.9 us -> 53 us
    ppermute x2 -> x1, waiting for transfers between devices: 1.56 us -> 0.01 us  [of_groups(): lax.ppermute(values, 'group', [(at, (at + back) % GROUPS) for at in range...]
    all_to_all x1, blocking collectives: 12.6 us -> 13.7 us  [kernel_body(): own = lax.all_to_all(sent, 'block', 0, 0)]
    ppermute x2 -> x1, starting transfers between devices: 4.12 us -> 4.1 us  [of_groups(): lax.ppermute(values, 'group', [(at, (at + back) % GROUPS) for at in range...]
  transfers between devices with their start and end apart: 4 -> 3, of which waited for: 2 -> 1; matrix products, arithmetic and copies ran while one was open for 1% -> 0% of each run, Pallas kernels for 8% -> 8%
where the time goes in v10:
time: 73.6 us; the launch traced here: 73.2 us
  blocking collectives  53 us (72%)
  Pallas kernels  14.7 us (20%)
  starting transfers between devices  4.18 us (6%)
  between operations  0.74 us (1%)
    all_to_all x3, blocking collectives, share(): return lax.all_to_all(values, GROUP, 0, 0)  25 us
    all_to_all x1, blocking collectives, kernel_body(): got = lax.all_to_all(sent, 'block', 0, 0)  14.3 us
    all_to_all x1, blocking collectives, kernel_body(): own = lax.all_to_all(sent, 'block', 0, 0)  13.7 us
    ppermute x1, starting transfers between devices, of_groups(): lax.ppermute(values, 'group', [(at, (at + back) % GROUPS) for at in range...  4.1 us
    pallas_call x1, Pallas kernels, kernel_body(): call(directions_kernel, (shape((count, width), bf16), shape((count, width...  2.96 us
    pallas_call x1, Pallas kernels, kernel_body(): call(functools.partial(other_kernel, prototypes), (shape((count, half), f...  2.22 us
    pallas_call x1, Pallas kernels, kernel_body(): call(gradient_kernel, (shape((2, count, half), bf16), shape((half // GROU...  1.99 us
    pallas_call x1, Pallas kernels, kernel_body(): call(weight_kernel, shape((blocks, out_rows, count + per_chip), bf16), fl...  1.6 us
  transfers between devices with their start and end apart: 3, of which 1 were waited for; matrix products, arithmetic and copies ran while one was open for 0% of the time, Pallas kernels for 8%

profile of v10, /device:TPU:0, one launch (start us, length us, event | category | flops | bytes accessed | tf_op | source)
XLA Modules:
  0.0 73.2 jit_solution(2416545147217189611)
XLA Ops:
  0.6 0.9 %shard_map.68.refs_0_ = bf16[48,512]{1,0:T(8,128)(2,1)S(1)} custom-call(bf16[32,256]{1,0:T(8,128)(2,1)} %teacher_ref.2, bf16[32,256]{1,0:T(8,128)(2,1)} %student_ref.5, bf16[1,32]{1,0:T(2,128)(2,1)} %bitcast.2), custom_call_target="tpu_custom_call" | custom-call | tf_op jit(solution)/shard_map/pallas_call | solution.py:459
  1.5 4.1 %collective-permute-start = (bf16[48,512]{1,0:T(8,128)(2,1)S(1)}, bf16[48,512]{1,0:T(8,128)(2,1)S(1)}, u32[]{:S(2)}, u32[]{:S(2)}) collective-permute-start(bf16[48,512]{1,0:T(8,128)(2,1)S(1)} %shard_map.68.refs_0_), channel_id=1, source_target_pairs={{0,16},{16,0},{1,17},{17,1},{2,18},{18,2},{3,19},{19,3},{4,20},{20... | collective-permute-start | bytes 147464 | tf_op jit(solution)/shard_map/ppermute | solution.py:468
  5.6 3.0 %shard_map.69 = (bf16[2048,256]{1,0:T(8,128)(2,1)S(1)}, bf16[2048,256]{1,0:T(8,128)(2,1)S(1)}, f32[1,2048]{1,0:T(1,128)S(1)}) custom-call(s32[1]{0:T(128)} %bitcast.1.block_ref, bf16[256,16384]{1,0:T(8,128)(2,1)} %teacher_ref.3, bf16[256,16384]{1,0:T(8,128)(2,1)} %directions_ref.1), custom_call_target="tpu_custom_call" | custom-call | flops 6291456 | bytes 4194304 | tf_op jit(solution)/shard_map/pallas_call | solution.py:478
  8.6 0.0 collective-permute-done.refs_1_
  8.6 13.7 %all_to_all.25.got_ref = bf16[8,64,512]{2,1,0:T(8,128)(2,1)S(1)} all-to-all(bf16[8,64,512]{2,1,0:T(8,128)(2,1)S(1)} %shard_map.70), channel_id=1, replica_groups=mesh['group'=2,'block'=8,'fsdp'=2] {'block'}, dimensions={0} | all-to-all | bytes 1048576 | tf_op jit(solution)/shard_map/all_to_all | solution.py:501
  22.3 0.0 collective-permute-start.1
  22.3 1.3 %shard_map.71 = (f32[2048,512]{1,0:T(8,128)S(1)}, f32[2048,512]{1,0:T(8,128)S(1)}, f32[8,512]{1,0:T(8,128)S(1)}, bf16[256,512]{1,0:T(8,128)(2,1)S(1)}) custom-call(bf16[2048,256]{1,0:T(8,128)(2,1)S(1)} %get-tuple-element.27.teacher_w_ref, bf16[2048,256]{1,0:T(8,128)(2,1)S(1)} %get-tuple-element.28.student_w_ref, bf16[8,64,512]{2,1,0:T(8,128)(2,1)S(1)} %all_to_all.25.got_ref), custom_call_target="tpu_custom_call" | custom-call | flops 1073741824 | tf_op jit(solution)/shard_map/pallas_call | solution.py:508
  23.6 0.6 collective-permute-done.1.got_ref
  24.2 2.2 %shard_map.72 = (f32[2048,512]{1,0:T(8,128)S(1)}, f32[2048,512]{1,0:T(8,128)S(1)}, bf16[16,16,128]{2,1,0:T(8,128)(2,1)S(1)}, f32[8,128]{1,0:T(8,128)S(1)}, bf16[256,512]{1,0:T(8,128)(2,1)S(1)}) custom-call(bf16[2048,256]{1,0:T(8,128)(2,1)S(1)} %get-tuple-element.27.teacher_w_ref, bf16[2048,256]{1,0:T(8,128)(2,1)S(1)} %get-tuple-element.28.student_w_ref, ...), custom_call_target="tpu_custom_call" | custom-call | flops 1073741824 | tf_op jit(solution)/shard_map/pallas_call | solution.py:519
  26.4 8.4 %all_to_all.26.got_ref = bf16[16,16,128]{2,1,0:T(8,128)(2,1)S(1)} all-to-all(bf16[16,16,128]{2,1,0:T(8,128)(2,1)S(1)} %get-tuple-element.34), channel_id=1, replica_groups=mesh['group'=2,'block'=8,'fsdp'=2] {'block','fsdp'}, dimensions={0} | all-to-all | bytes 131072 | tf_op jit(solution)/shard_map/all_to_all | solution.py:455
  34.9 1.2 %shard_map.73 = (bf16[16,16,128]{2,1,0:T(8,128)(2,1)S(1)}, f32[8,128]{1,0:T(8,128)S(1)}) custom-call(f32[2048,512]{1,0:T(8,128)S(1)} %get-tuple-element.31.own_ref, f32[2048,512]{1,0:T(8,128)S(1)} %get-tuple-element.33.other_ref, bf16[16,16,128]{2,1,0:T(8,128)(2,1)S(1)} %all_to_all.26.got_ref, f32[8,128]{1,0:T(8,128)S(1)} %get-tuple-element.35.part_ref), custom_call_target="tpu_custom_call" | custom-call | flops 8388608 | tf_op jit(solution)/shard_map/pallas_call | solution.py:532
  36.0 8.4 %all_to_all.27.got_ref.second_ref = bf16[16,16,128]{2,1,0:T(8,128)(2,1)S(1)} all-to-all(bf16[16,16,128]{2,1,0:T(8,128)(2,1)S(1)} %get-tuple-element.36), channel_id=1, replica_groups=mesh['group'=2,'block'=8,'fsdp'=2] {'block','fsdp'}, dimensions={0} | all-to-all | bytes 131072 | tf_op jit(solution)/shard_map/all_to_all | solution.py:455
  44.4 1.3 %shard_map.74 = (bf16[16,8,128]{2,1,0:T(8,128)(2,1)S(1)}, f32[2048,512]{1,0:T(8,128)S(1)}, f32[2048,512]{1,0:T(8,128)S(1)}, bf16[4,256,512]{2,1,0:T(8,128)(2,1)S(1)}) custom-call(f32[2048,512]{1,0:T(8,128)S(1)} %get-tuple-element.31.own_ref, f32[2048,512]{1,0:T(8,128)S(1)} %get-tuple-element.33.other_ref, ...), custom_call_target="tpu_custom_call" | custom-call | flops 8388608 | tf_op jit(solution)/shard_map/pallas_call | solution.py:538
  45.7 8.2 %all_to_all.28.third_ref = bf16[16,8,128]{2,1,0:T(8,128)(2,1)S(1)} all-to-all(bf16[16,8,128]{2,1,0:T(8,128)(2,1)S(1)} %get-tuple-element.42), channel_id=1, replica_groups=mesh['group'=2,'block'=8,'fsdp'=2] {'block','fsdp'}, dimensions={0} | all-to-all | bytes 65536 | tf_op jit(solution)/shard_map/all_to_all | solution.py:455
  53.9 2.0 %shard_map.75 = (bf16[2,2048,512]{2,1,0:T(8,128)(2,1)S(1)}, f32[256,256]{1,0:T(8,128)S(1)}, bf16[256,256]{1,0:T(8,128)(2,1)S(1)}) custom-call(f32[2048,512]{1,0:T(8,128)S(1)} %get-tuple-element.37.own_mass_ref, f32[2048,512]{1,0:T(8,128)S(1)} %get-tuple-element.38.other_mass_ref, f32[2048,512]{1,0:T(8,128)S(1)} %get-tuple-element.39.own_student_ref, ...), custom_call_target="tpu_custom_call" | custom-call | flops 536870912 | tf_op jit(solution)/shard_map/pallas_call | solution.py:552
  55.9 0.1 collective-permute-start.2
  56.0 0.0 copy-start
  56.0 1.6 %shard_map.76._ = bf16[8,16,2560]{2,1,0:T(8,128)(2,1)S(1)} custom-call(bf16[2,2048,512]{2,1,0:T(8,128)(2,1)S(1)} %get-tuple-element.47.gradient_ref, bf16[256,512]{1,0:T(8,128)(2,1)S(1)} %get-tuple-element.48.own_turned_ref, bf16[256,512]{1,0:T(8,128)(2,1)S(1)} %get-tuple-element.49.other_turned_ref, f32[1,2048]{1,0:T(1,128)S(1)} %get-tuple-element.43.inverse_ref, ...), custom_call_target="tpu_custom_call" | custom-call | flops 1073741824 | tf_op jit(solution)/shard_map/pallas_call | solution.py:562
  57.6 0.0 collective-permute-done.2.other_ref
  57.7 0.1 shard_map.77
  57.7 14.3 %all_to_all.29.got_ref = bf16[8,16,2560]{2,1,0:T(8,128)(2,1)S(1)} all-to-all(bf16[8,16,2560]{2,1,0:T(8,128)(2,1)S(1)} %shard_map.77), channel_id=1, replica_groups=mesh['group'=2,'block'=8,'fsdp'=2] {'block'}, dimensions={0} | all-to-all | bytes 1310720 | tf_op jit(solution)/shard_map/all_to_all | solution.py:577
  72.0 0.0 copy-done
  72.0 1.1 %shard_map.78 = (f32[16,16384]{1,0:T(8,128)}, f32[32,256]{1,0:T(8,128)}) custom-call(bf16[8,16,2560]{2,1,0:T(8,128)(2,1)S(1)} %all_to_all.29.got_ref, bf16[32,256]{1,0:T(8,128)(2,1)S(1)} %copy-done), custom_call_target="tpu_custom_call" | custom-call | tf_op jit(solution)/shard_map/pallas_call | solution.py:578
  (1 shorter events, 0.0 us)
Async XLA Ops:
  1.5 7.1 %collective-permute-start = (bf16[48,512]{1,0:T(8,128)(2,1)S(1)}, bf16[48,512]{1,0:T(8,128)(2,1)S(1)}, u32[]{:S(2)}, u32[]{:S(2)}) collective-permute-start(bf16[48,512]{1,0:T(8,128)(2,1)S(1)} %shard_map.68.refs_0_), channel_id=1, source_target_pairs={{0,16},{16,0},{1,17},{17,1},{2,18},{18,2},{3,19},{19,3},{4,20},{20... | collective-permute-start | bytes 147464 | tf_op jit(solution)/shard_map/ppermute | solution.py:468
  22.3 1.9 %collective-permute-start.1 = (bf16[8,64,512]{2,1,0:T(8,128)(2,1)S(1)}, bf16[8,64,512]{2,1,0:T(8,128)(2,1)S(1)}, u32[]{:S(2)}, u32[]{:S(2)}) collective-permute-start(bf16[8,64,512]{2,1,0:T(8,128)(2,1)S(1)} %all_to_all.25.got_ref), channel_id=1, source_target_pairs={{0,1},{1,0},{2,3},{3,2},{4,5},{5,4},{6,7},{7,6},{8,9},{9,8},{10,11... | collective-permute-start | bytes 1572872 | tf_op jit(solution)/shard_map/ppermute | solution.py:452
  55.9 1.7 %collective-permute-start.2 = (bf16[256,256]{1,0:T(8,128)(2,1)S(1)}, bf16[256,256]{1,0:T(8,128)(2,1)S(1)}, u32[]{:S(2)}, u32[]{:S(2)}) collective-permute-start(bf16[256,256]{1,0:T(8,128)(2,1)S(1)} %get-tuple-element.46), channel_id=1, source_target_pairs={{0,1},{1,0},{2,3},{3,2},{4,5},{5,4},{6,7},{7,6},{8,9},{9,8},{10,11... | collective-permute-start | bytes 393224 | tf_op jit(solution)/shard_map/ppermute | solution.py:452
  56.0 16.0 %copy-start = (bf16[32,256]{1,0:T(8,128)(2,1)S(1)}, bf16[32,256]{1,0:T(8,128)(2,1)}, u32[]{:S(2)}) copy-start(bf16[32,256]{1,0:T(8,128)(2,1)} %student_ref.5) | copy-start | bytes 49156

commit v11 on v10

--- a/solution.py
+++ b/solution.py
@@ -18,7 +18,6 @@
 GROUPS = 2
 TILE = 256
 HALF_TILE = 512
-FETCH = 2
 LANES = 128
 VMEM_BYTES = 12 << 20
 KEPT_BYTES = 18 << 20
@@ -176,11 +175,12 @@
     return placed
 
 
-def directions_kernel(block_ref, teacher_ref, student_ref, teacher_out, student_out, inverse_out):
+def directions_kernel(block_ref, teacher_ref, student_ref, teacher_out, student_out, unit_out, inverse_out):
     teacher, _ = unit_columns(teacher_ref[...])
     teacher_out[...] = jnp.transpose(teacher).astype(jnp.bfloat16)
     student, length = unit_columns(student_ref[...])
     student_out[...] = jnp.transpose(student).astype(jnp.bfloat16)
+    unit_out[...] = student
     inverse_out[...] = 1.0 / length
 
 
@@ -325,17 +325,7 @@
     in_core_order(lax.axis_index("fsdp"), own_ref, other_ref, body)
 
 
-def last_sweep_kernel(
-    prototypes, crops, own_ref, other_ref, got_ref, directions_ref,
-    sent_ref, own_scaled_ref, other_scaled_ref, copy_ref, sems,
-):
-    pieces, _, span = copy_ref.shape
-    copies = []
-    for piece in range(pieces):
-        columns = pl.ds(pl.multiple_of((lax.axis_index("block") * pieces + piece) * span, span), span)
-        copies.append(pltpu.make_async_copy(directions_ref.at[:, columns], copy_ref.at[piece], sems.at[piece]))
-        copies[-1].start()
-
+def last_sweep_kernel(prototypes, crops, own_ref, other_ref, got_ref, sent_ref, own_scaled_ref, other_scaled_ref):
     total = received(got_ref)[: crops // LANES]
 
     def body(first_refs, second_refs):
@@ -344,19 +334,11 @@
         send(sent_ref, sent)
 
     in_core_order(lax.axis_index("fsdp"), (own_ref, own_scaled_ref), (other_ref, other_scaled_ref), body)
-    for copy in copies:
-        copy.wait()
-
-
-def units_tile(copy_ref, inverse_ref, start):
-    span = copy_ref.shape[2]
-    at = start % span
-    return copy_ref[start // span, :, at : at + TILE].astype(jnp.float32) * inverse_ref[:, start : start + TILE]
 
 
 def gradient_kernel(
     own_mass_ref, other_mass_ref, own_student_ref, other_student_ref, weight_ref, second_ref, third_ref,
-    inverse_ref, copy_ref, gradient_ref, keep_ref, give_ref, unit_ref,
+    unit_ref, gradient_ref, keep_ref, give_ref,
 ):
     group, core = lax.axis_index("group"), lax.axis_index("fsdp")
     count, half = own_mass_ref.shape
@@ -375,16 +357,15 @@
                 gradient_ref[side, start : start + TILE, :] = gradient.astype(jnp.bfloat16)
 
     in_core_order(core, (0, own_mass_ref, own_student_ref), (1, other_mass_ref, other_student_ref), body)
-    for start in range(0, count, TILE):
-        unit_ref[:, start : start + TILE] = units_tile(copy_ref, inverse_ref, start).astype(jnp.bfloat16)
+    unit = unit_ref[...].astype(jnp.bfloat16)
     kept = half // GROUPS
     lanes = pl.ds(pl.multiple_of(group * kept, kept), kept)
     for side, out_ref in enumerate((keep_ref, give_ref)):
-        feature = jnp.dot(unit_ref[...], gradient_ref[side, :, lanes], preferred_element_type=jnp.float32)
+        feature = jnp.dot(unit, gradient_ref[side, :, lanes], preferred_element_type=jnp.float32)
         out_ref[...] = jnp.transpose(feature).astype(out_ref.dtype)
 
 
-def weight_kernel(gradient_ref, own_turned_ref, other_turned_ref, inverse_ref, copy_ref, sent_ref, grad_ref):
+def weight_kernel(gradient_ref, own_turned_ref, other_turned_ref, inverse_ref, unit_ref, sent_ref, grad_ref):
     chips, rows_each, _ = sent_ref.shape
     count = gradient_ref.shape[1]
     width = own_turned_ref.shape[0]
@@ -397,7 +378,7 @@
             weight_grad = weight_grad + lax.dot_general(
                 turned_ref[...], gradient_ref[side, here, :], (((1,), (1,)), ((), ())), preferred_element_type=jnp.float32
             )
-        unit = units_tile(copy_ref, inverse_ref, start)
+        unit = unit_ref[:, here]
         dot = jnp.sum(unit * weight_grad, axis=0, keepdims=True)
         grad_ref[slot] = (weight_grad - unit * dot) * inverse_ref[:, here]
         own = grad_ref[slot, own_rows, :].astype(jnp.bfloat16)
@@ -474,12 +455,14 @@
     spans = count // span
     column = pl.BlockSpec((width, span), lambda step, at: (0, at[0] * spans + step))
     turned = pl.BlockSpec((span, width), lambda step, at: (step, 0))
+    straight = pl.BlockSpec((width, span), lambda step, at: (0, step))
     line = pl.BlockSpec((1, span), lambda step, at: (0, step))
-    teacher_w, student_w, inverse = call(
+    teacher_w, student_w, student_unit, inverse = call(
         directions_kernel,
         (
             shape((count, width), bf16),
             shape((count, width), bf16),
+            shape((width, count), f32),
             shape((1, count), f32),
         ),
         flops=12 * count * width,
@@ -488,7 +471,7 @@
             num_scalar_prefetch=1,
             grid=(spans,),
             in_specs=[column, column],
-            out_specs=[turned, turned, line],
+            out_specs=[turned, turned, straight, line],
         ),
     )(
         block,
@@ -502,7 +485,6 @@
     other = swap(own)
     half = crops // 2
     anyspace = pl.BlockSpec(memory_space=pl.ANY)
-    pieces = count // (FETCH * TILE)
     halved = dict(flops=2 * elements * width, exps=elements)
     scratch = [pltpu.VMEM((half, width), bf16)] * 2
     own_mass, own_student, own_part, own_turned = call(
@@ -535,27 +517,22 @@
         flops=4 * elements,
     )(own_mass, other_mass, first, student_part)
     second = share(sent)
-    sent, own_scaled, other_scaled, student_copy = call(
+    sent, own_scaled, other_scaled = call(
         functools.partial(last_sweep_kernel, prototypes, crops),
         (
             shape((members, lines, LANES), bf16),
             shape((count, half), f32),
             shape((count, half), f32),
-            shape((pieces, width, count // pieces), bf16),
         ),
         flops=4 * elements,
-        in_specs=[vmem] * 3 + [anyspace],
-        scratch_shapes=[dma((pieces,))],
-    )(own_mass, other_mass, second, hbm(student_v))
+    )(own_mass, other_mass, second)
     third = share(sent)
 
     gradient, keep, give = call(
         gradient_kernel,
         (shape((2, count, half), bf16), shape((half // GROUPS, width), f32), shape((half // GROUPS, width), bf16)),
         flops=2 * elements * width // GROUPS,
-        in_specs=[vmem] * 9,
-        scratch_shapes=[pltpu.VMEM((width, count), bf16)],
-    )(own_scaled, other_scaled, own_student, other_student, weights, second, third, inverse, student_copy)
+    )(own_scaled, other_scaled, own_student, other_student, weights, second, third, student_unit)
     other = swap(give)
     out_rows = width // chips
     per_chip = rows * width // out_rows
@@ -565,7 +542,7 @@
         flops=2 * elements * width,
         in_specs=[vmem] * 5,
         scratch_shapes=[pltpu.VMEM((count // TILE, width, TILE), f32)],
-    )(gradient, own_turned, other_turned, inverse, student_copy)
+    )(gradient, own_turned, other_turned, inverse, student_unit)
     sent = call(
         pack_kernel,
         shape((blocks, out_rows, count + per_chip), bf16),

time: 73.6 us -> 74 us (level)
  no operation moved by 1% of the time
where the time goes in v11:
time: 74 us; the launch traced here: 73.6 us
  blocking collectives  53 us (72%)
  Pallas kernels  15 us (20%)
  starting transfers between devices  4.18 us (6%)
  between operations  0.74 us (1%)
    all_to_all x3, blocking collectives, share(): return lax.all_to_all(values, GROUP, 0, 0)  25 us
    all_to_all x1, blocking collectives, kernel_body(): got = lax.all_to_all(sent, 'block', 0, 0)  14.3 us
    all_to_all x1, blocking collectives, kernel_body(): own = lax.all_to_all(sent, 'block', 0, 0)  13.7 us
    ppermute x1, starting transfers between devices, of_groups(): lax.ppermute(values, 'group', [(at, (at + back) % GROUPS) for at in range...  4.1 us
    pallas_call x1, Pallas kernels, kernel_body(): call(directions_kernel, (shape((count, width), bf16), shape((count, width...  3.11 us
    pallas_call x1, Pallas kernels, kernel_body(): call(gradient_kernel, (shape((2, count, half), bf16), shape((half // GROU...  2.28 us
    pallas_call x1, Pallas kernels, kernel_body(): call(functools.partial(other_kernel, prototypes), (shape((count, half), f...  2.19 us
    pallas_call x1, Pallas kernels, kernel_body(): call(weight_kernel, shape((blocks, out_rows, count + per_chip), bf16), fl...  1.62 us
  transfers between devices with their start and end apart: 3, of which 1 were waited for; matrix products, arithmetic and copies ran while one was open for 0% of the time, Pallas kernels for 8%

profile of v11, /device:TPU:0, one launch (start us, length us, event | category | flops | bytes accessed | tf_op | source)
XLA Modules:
  0.0 73.6 jit_solution(13041922835178596660)
XLA Ops:
  0.6 0.9 %shard_map.68.refs_0_ = bf16[48,512]{1,0:T(8,128)(2,1)S(1)} custom-call(bf16[32,256]{1,0:T(8,128)(2,1)} %teacher_ref.2, bf16[32,256]{1,0:T(8,128)(2,1)} %student_ref.5, bf16[1,32]{1,0:T(2,128)(2,1)} %bitcast.2), custom_call_target="tpu_custom_call" | custom-call | tf_op jit(solution)/shard_map/pallas_call | solution.py:440
  1.5 4.1 %collective-permute-start = (bf16[48,512]{1,0:T(8,128)(2,1)S(1)}, bf16[48,512]{1,0:T(8,128)(2,1)S(1)}, u32[]{:S(2)}, u32[]{:S(2)}) collective-permute-start(bf16[48,512]{1,0:T(8,128)(2,1)S(1)} %shard_map.68.refs_0_), channel_id=1, source_target_pairs={{0,16},{16,0},{1,17},{17,1},{2,18},{18,2},{3,19},{19,3},{4,20},{20... | collective-permute-start | bytes 147464 | tf_op jit(solution)/shard_map/ppermute | solution.py:449
  5.6 3.1 %shard_map.69 = (bf16[2048,256]{1,0:T(8,128)(2,1)S(1)}, bf16[2048,256]{1,0:T(8,128)(2,1)S(1)}, f32[256,2048]{1,0:T(8,128)S(1)}, f32[1,2048]{1,0:T(1,128)S(1)}) custom-call(s32[1]{0:T(128)} %bitcast.1.block_ref, bf16[256,16384]{1,0:T(8,128)(2,1)} %teacher_ref.3, bf16[256,16384]{1,0:T(8,128)(2,1)} %student_ref.4), custom_call_target="tpu_custom_call" | custom-call | flops 6291456 | bytes 4194304 | tf_op jit(solution)/shard_map/pallas_call | solution.py:460
  8.7 0.0 collective-permute-done.refs_1_
  8.8 13.7 %all_to_all.25.got_ref = bf16[8,64,512]{2,1,0:T(8,128)(2,1)S(1)} all-to-all(bf16[8,64,512]{2,1,0:T(8,128)(2,1)S(1)} %shard_map.70), channel_id=1, replica_groups=mesh['group'=2,'block'=8,'fsdp'=2] {'block'}, dimensions={0} | all-to-all | bytes 1048576 | tf_op jit(solution)/shard_map/all_to_all | solution.py:484
  22.5 0.0 collective-permute-start.1
  22.5 1.3 %shard_map.71 = (f32[2048,512]{1,0:T(8,128)S(1)}, f32[2048,512]{1,0:T(8,128)S(1)}, f32[8,512]{1,0:T(8,128)S(1)}, bf16[256,512]{1,0:T(8,128)(2,1)S(1)}) custom-call(bf16[2048,256]{1,0:T(8,128)(2,1)S(1)} %get-tuple-element.27.teacher_w_ref, bf16[2048,256]{1,0:T(8,128)(2,1)S(1)} %get-tuple-element.28.student_w_ref, bf16[8,64,512]{2,1,0:T(8,128)(2,1)S(1)} %all_to_all.25.got_ref), custom_call_target="tpu_custom_call" | custom-call | flops 1073741824 | tf_op jit(solution)/shard_map/pallas_call | solution.py:490
  23.8 0.6 collective-permute-done.1.got_ref
  24.4 2.2 %shard_map.72 = (f32[2048,512]{1,0:T(8,128)S(1)}, f32[2048,512]{1,0:T(8,128)S(1)}, bf16[16,16,128]{2,1,0:T(8,128)(2,1)S(1)}, f32[8,128]{1,0:T(8,128)S(1)}, bf16[256,512]{1,0:T(8,128)(2,1)S(1)}) custom-call(bf16[2048,256]{1,0:T(8,128)(2,1)S(1)} %get-tuple-element.27.teacher_w_ref, bf16[2048,256]{1,0:T(8,128)(2,1)S(1)} %get-tuple-element.28.student_w_ref, ...), custom_call_target="tpu_custom_call" | custom-call | flops 1073741824 | tf_op jit(solution)/shard_map/pallas_call | solution.py:501
  26.6 8.4 %all_to_all.26.got_ref = bf16[16,16,128]{2,1,0:T(8,128)(2,1)S(1)} all-to-all(bf16[16,16,128]{2,1,0:T(8,128)(2,1)S(1)} %get-tuple-element.34), channel_id=1, replica_groups=mesh['group'=2,'block'=8,'fsdp'=2] {'block','fsdp'}, dimensions={0} | all-to-all | bytes 131072 | tf_op jit(solution)/shard_map/all_to_all | solution.py:436
  35.0 1.2 %shard_map.73 = (bf16[16,16,128]{2,1,0:T(8,128)(2,1)S(1)}, f32[8,128]{1,0:T(8,128)S(1)}) custom-call(f32[2048,512]{1,0:T(8,128)S(1)} %get-tuple-element.31.own_ref, f32[2048,512]{1,0:T(8,128)S(1)} %get-tuple-element.33.other_ref, bf16[16,16,128]{2,1,0:T(8,128)(2,1)S(1)} %all_to_all.26.got_ref, f32[8,128]{1,0:T(8,128)S(1)} %get-tuple-element.35.part_ref), custom_call_target="tpu_custom_call" | custom-call | flops 8388608 | tf_op jit(solution)/shard_map/pallas_call | solution.py:514
  36.1 8.4 %all_to_all.27.got_ref.second_ref = bf16[16,16,128]{2,1,0:T(8,128)(2,1)S(1)} all-to-all(bf16[16,16,128]{2,1,0:T(8,128)(2,1)S(1)} %get-tuple-element.36), channel_id=1, replica_groups=mesh['group'=2,'block'=8,'fsdp'=2] {'block','fsdp'}, dimensions={0} | all-to-all | bytes 131072 | tf_op jit(solution)/shard_map/all_to_all | solution.py:436
  44.5 1.3 %shard_map.74 = (bf16[16,8,128]{2,1,0:T(8,128)(2,1)S(1)}, f32[2048,512]{1,0:T(8,128)S(1)}, f32[2048,512]{1,0:T(8,128)S(1)}) custom-call(f32[2048,512]{1,0:T(8,128)S(1)} %get-tuple-element.31.own_ref, f32[2048,512]{1,0:T(8,128)S(1)} %get-tuple-element.33.other_ref, bf16[16,16,128]{2,1,0:T(8,128)(2,1)S(1)} %all_to_all.27.got_ref.second_ref), custom_call_target="tpu_custom_call" | custom-call | flops 8388608 | tf_op jit(solution)/shard_map/pallas_call | solution.py:520
  45.8 8.2 %all_to_all.28.third_ref = bf16[16,8,128]{2,1,0:T(8,128)(2,1)S(1)} all-to-all(bf16[16,8,128]{2,1,0:T(8,128)(2,1)S(1)} %get-tuple-element.42), channel_id=1, replica_groups=mesh['group'=2,'block'=8,'fsdp'=2] {'block','fsdp'}, dimensions={0} | all-to-all | bytes 65536 | tf_op jit(solution)/shard_map/all_to_all | solution.py:436
  54.0 2.3 %shard_map.75 = (bf16[2,2048,512]{2,1,0:T(8,128)(2,1)S(1)}, f32[256,256]{1,0:T(8,128)S(1)}, bf16[256,256]{1,0:T(8,128)(2,1)S(1)}) custom-call(f32[2048,512]{1,0:T(8,128)S(1)} %get-tuple-element.37.own_mass_ref, f32[2048,512]{1,0:T(8,128)S(1)} %get-tuple-element.38.other_mass_ref, f32[2048,512]{1,0:T(8,128)S(1)} %get-tuple-element.39.own_student_ref, ...), custom_call_target="tpu_custom_call" | custom-call | flops 536870912 | tf_op jit(solution)/shard_map/pallas_call | solution.py:531
  56.3 0.1 collective-permute-start.2
  56.4 0.0 copy-start
  56.4 1.6 %shard_map.76._ = bf16[8,16,2560]{2,1,0:T(8,128)(2,1)S(1)} custom-call(bf16[2,2048,512]{2,1,0:T(8,128)(2,1)S(1)} %get-tuple-element.46.gradient_ref, bf16[256,512]{1,0:T(8,128)(2,1)S(1)} %get-tuple-element.47.own_turned_ref, bf16[256,512]{1,0:T(8,128)(2,1)S(1)} %get-tuple-element.48.other_turned_ref, f32[1,2048]{1,0:T(1,128)S(1)} %get-tuple-element.49.inverse_ref, ...), custom_call_target="tpu_custom_call" | custom-call | flops 1073741824 | tf_op jit(solution)/shard_map/pallas_call | solution.py:539
  58.0 0.0 collective-permute-done.2.other_ref
  58.0 0.1 shard_map.77
  58.1 14.3 %all_to_all.29.got_ref = bf16[8,16,2560]{2,1,0:T(8,128)(2,1)S(1)} all-to-all(bf16[8,16,2560]{2,1,0:T(8,128)(2,1)S(1)} %shard_map.77), channel_id=1, replica_groups=mesh['group'=2,'block'=8,'fsdp'=2] {'block'}, dimensions={0} | all-to-all | bytes 1310720 | tf_op jit(solution)/shard_map/all_to_all | solution.py:554
  72.4 0.0 copy-done
  72.4 1.1 %shard_map.78 = (f32[16,16384]{1,0:T(8,128)}, f32[32,256]{1,0:T(8,128)}) custom-call(bf16[8,16,2560]{2,1,0:T(8,128)(2,1)S(1)} %all_to_all.29.got_ref, bf16[32,256]{1,0:T(8,128)(2,1)S(1)} %copy-done), custom_call_target="tpu_custom_call" | custom-call | tf_op jit(solution)/shard_map/pallas_call | solution.py:555
  (1 shorter events, 0.0 us)
Async XLA Ops:
  1.5 7.2 %collective-permute-start = (bf16[48,512]{1,0:T(8,128)(2,1)S(1)}, bf16[48,512]{1,0:T(8,128)(2,1)S(1)}, u32[]{:S(2)}, u32[]{:S(2)}) collective-permute-start(bf16[48,512]{1,0:T(8,128)(2,1)S(1)} %shard_map.68.refs_0_), channel_id=1, source_target_pairs={{0,16},{16,0},{1,17},{17,1},{2,18},{18,2},{3,19},{19,3},{4,20},{20... | collective-permute-start | bytes 147464 | tf_op jit(solution)/shard_map/ppermute | solution.py:449
  22.5 1.9 %collective-permute-start.1 = (bf16[8,64,512]{2,1,0:T(8,128)(2,1)S(1)}, bf16[8,64,512]{2,1,0:T(8,128)(2,1)S(1)}, u32[]{:S(2)}, u32[]{:S(2)}) collective-permute-start(bf16[8,64,512]{2,1,0:T(8,128)(2,1)S(1)} %all_to_all.25.got_ref), channel_id=1, source_target_pairs={{0,1},{1,0},{2,3},{3,2},{4,5},{5,4},{6,7},{7,6},{8,9},{9,8},{10,11... | collective-permute-start | bytes 1572872 | tf_op jit(solution)/shard_map/ppermute | solution.py:433
  56.3 1.7 %collective-permute-start.2 = (bf16[256,256]{1,0:T(8,128)(2,1)S(1)}, bf16[256,256]{1,0:T(8,128)(2,1)S(1)}, u32[]{:S(2)}, u32[]{:S(2)}) collective-permute-start(bf16[256,256]{1,0:T(8,128)(2,1)S(1)} %get-tuple-element.45), channel_id=1, source_target_pairs={{0,1},{1,0},{2,3},{3,2},{4,5},{5,4},{6,7},{7,6},{8,9},{9,8},{10,11... | collective-permute-start | bytes 393224 | tf_op jit(solution)/shard_map/ppermute | solution.py:433
  56.4 16.0 %copy-start = (bf16[32,256]{1,0:T(8,128)(2,1)S(1)}, bf16[32,256]{1,0:T(8,128)(2,1)}, u32[]{:S(2)}) copy-start(bf16[32,256]{1,0:T(8,128)(2,1)} %student_ref.5) | copy-start | bytes 49156

commit v12 on v10

--- a/solution.py
+++ b/solution.py
@@ -17,7 +17,7 @@
 
 GROUPS = 2
 TILE = 256
-HALF_TILE = 512
+HALF_TILE = 256
 FETCH = 2
 LANES = 128
 VMEM_BYTES = 12 << 20
@@ -421,14 +421,19 @@
     rows, width = student_ref.shape
     pieces = rows // rows_each
     count = columns - pieces * width
-    total = got_ref[0, :, count:].astype(jnp.float32)
-    for chip in range(1, chips):
-        total = total + got_ref[chip, :, count:].astype(jnp.float32)
-    total = jnp.concatenate([total[:, piece * width : (piece + 1) * width] for piece in range(pieces)], axis=0)
-    hat, length = unit_rows(student_ref[...])
-    feature_out[...] = (total - hat * jnp.sum(hat * total, axis=1, keepdims=True)) / length
-    for chip in range(chips):
-        weight_out[:, chip * count : (chip + 1) * count] = got_ref[chip, :, :count].astype(jnp.float32)
+    step = pl.program_id(0)
+    each = chips // pl.num_programs(0)
+    for chip in range(each):
+        weight_out[:, chip * count : (chip + 1) * count] = got_ref[step * each + chip, :, :count].astype(jnp.float32)
+
+    @pl.when(step == 0)
+    def _():
+        total = got_ref[0, :, count:].astype(jnp.float32)
+        for chip in range(1, chips):
+            total = total + got_ref[chip, :, count:].astype(jnp.float32)
+        total = jnp.concatenate([total[:, piece * width : (piece + 1) * width] for piece in range(pieces)], axis=0)
+        hat, length = unit_rows(student_ref[...])
+        feature_out[...] = (total - hat * jnp.sum(hat * total, axis=1, keepdims=True)) / length
 
 
 def kernel_body(teacher_feat, student_feat, crop_weight, teacher_v, student_v):
@@ -576,7 +581,14 @@
     )(keep, other, sent)
     got = lax.all_to_all(sent, "block", 0, 0)
     return call(
-        outputs_kernel, (shape((out_rows, kept), f32), shape((rows, width), f32))
+        outputs_kernel,
+        (shape((out_rows, kept), f32), shape((rows, width), f32)),
+        grid=(2,),
+        in_specs=[vmem, vmem],
+        out_specs=[
+            pl.BlockSpec((out_rows, kept // 2), lambda step: (0, step)),
+            pl.BlockSpec((rows, width), lambda step: (0, 0)),
+        ],
     )(got, student_feat)
 
 

time: 73.6 us -> 73.6 us (level)
  no operation moved by 1% of the time
where the time goes in v12:
time: 73.6 us; the launch traced here: 73.2 us
  blocking collectives  53 us (72%)
  Pallas kernels  14.7 us (20%)
  starting transfers between devices  4.18 us (6%)
  between operations  0.74 us (1%)
    all_to_all x3, blocking collectives, share(): return lax.all_to_all(values, GROUP, 0, 0)  25 us
    all_to_all x1, blocking collectives, kernel_body(): got = lax.all_to_all(sent, 'block', 0, 0)  14.3 us
    all_to_all x1, blocking collectives, kernel_body(): own = lax.all_to_all(sent, 'block', 0, 0)  13.7 us
    ppermute x1, starting transfers between devices, of_groups(): lax.ppermute(values, 'group', [(at, (at + back) % GROUPS) for at in range...  4.1 us
    pallas_call x1, Pallas kernels, kernel_body(): call(directions_kernel, (shape((count, width), bf16), shape((count, width...  2.96 us
    pallas_call x1, Pallas kernels, kernel_body(): call(functools.partial(other_kernel, prototypes), (shape((count, half), f...  2.24 us
    pallas_call x1, Pallas kernels, kernel_body(): call(gradient_kernel, (shape((2, count, half), bf16), shape((half // GROU...  1.99 us
    pallas_call x1, Pallas kernels, kernel_body(): call(weight_kernel, shape((blocks, out_rows, count + per_chip), bf16), fl...  1.6 us
  transfers between devices with their start and end apart: 3, of which 1 were waited for; matrix products, arithmetic and copies ran while one was open for 0% of the time, Pallas kernels for 8%

profile of v12, /device:TPU:0, one launch (start us, length us, event | category | flops | bytes accessed | tf_op | source)
XLA Modules:
  0.0 73.2 jit_solution(4149281229557762870)
XLA Ops:
  0.6 0.9 %shard_map.68.refs_0_ = bf16[48,512]{1,0:T(8,128)(2,1)S(1)} custom-call(bf16[32,256]{1,0:T(8,128)(2,1)} %teacher_ref.2, bf16[32,256]{1,0:T(8,128)(2,1)} %student_ref.5, bf16[1,32]{1,0:T(2,128)(2,1)} %bitcast.2), custom_call_target="tpu_custom_call" | custom-call | tf_op jit(solution)/shard_map/pallas_call | solution.py:464
  1.5 4.1 %collective-permute-start = (bf16[48,512]{1,0:T(8,128)(2,1)S(1)}, bf16[48,512]{1,0:T(8,128)(2,1)S(1)}, u32[]{:S(2)}, u32[]{:S(2)}) collective-permute-start(bf16[48,512]{1,0:T(8,128)(2,1)S(1)} %shard_map.68.refs_0_), channel_id=1, source_target_pairs={{0,16},{16,0},{1,17},{17,1},{2,18},{18,2},{3,19},{19,3},{4,20},{20... | collective-permute-start | bytes 147464 | tf_op jit(solution)/shard_map/ppermute | solution.py:473
  5.6 3.0 %shard_map.69 = (bf16[2048,256]{1,0:T(8,128)(2,1)S(1)}, bf16[2048,256]{1,0:T(8,128)(2,1)S(1)}, f32[1,2048]{1,0:T(1,128)S(1)}) custom-call(s32[1]{0:T(128)} %bitcast.1.block_ref, bf16[256,16384]{1,0:T(8,128)(2,1)} %teacher_ref.3, bf16[256,16384]{1,0:T(8,128)(2,1)} %directions_ref.1), custom_call_target="tpu_custom_call" | custom-call | flops 6291456 | bytes 4194304 | tf_op jit(solution)/shard_map/pallas_call | solution.py:483
  8.6 0.0 collective-permute-done.refs_1_
  8.6 13.7 %all_to_all.25.got_ref = bf16[8,64,512]{2,1,0:T(8,128)(2,1)S(1)} all-to-all(bf16[8,64,512]{2,1,0:T(8,128)(2,1)S(1)} %shard_map.70), channel_id=1, replica_groups=mesh['group'=2,'block'=8,'fsdp'=2] {'block'}, dimensions={0} | all-to-all | bytes 1048576 | tf_op jit(solution)/shard_map/all_to_all | solution.py:506
  22.3 0.0 collective-permute-start.1
  22.3 1.3 %shard_map.71 = (f32[2048,512]{1,0:T(8,128)S(1)}, f32[2048,512]{1,0:T(8,128)S(1)}, f32[8,512]{1,0:T(8,128)S(1)}, bf16[256,512]{1,0:T(8,128)(2,1)S(1)}) custom-call(bf16[2048,256]{1,0:T(8,128)(2,1)S(1)} %get-tuple-element.27.teacher_w_ref, bf16[2048,256]{1,0:T(8,128)(2,1)S(1)} %get-tuple-element.28.student_w_ref, bf16[8,64,512]{2,1,0:T(8,128)(2,1)S(1)} %all_to_all.25.got_ref), custom_call_target="tpu_custom_call" | custom-call | flops 1073741824 | tf_op jit(solution)/shard_map/pallas_call | solution.py:513
  23.6 0.6 collective-permute-done.1.got_ref
  24.2 2.2 %shard_map.72 = (f32[2048,512]{1,0:T(8,128)S(1)}, f32[2048,512]{1,0:T(8,128)S(1)}, bf16[16,16,128]{2,1,0:T(8,128)(2,1)S(1)}, f32[8,128]{1,0:T(8,128)S(1)}, bf16[256,512]{1,0:T(8,128)(2,1)S(1)}) custom-call(bf16[2048,256]{1,0:T(8,128)(2,1)S(1)} %get-tuple-element.27.teacher_w_ref, bf16[2048,256]{1,0:T(8,128)(2,1)S(1)} %get-tuple-element.28.student_w_ref, ...), custom_call_target="tpu_custom_call" | custom-call | flops 1073741824 | tf_op jit(solution)/shard_map/pallas_call | solution.py:524
  26.5 8.4 %all_to_all.26.got_ref = bf16[16,16,128]{2,1,0:T(8,128)(2,1)S(1)} all-to-all(bf16[16,16,128]{2,1,0:T(8,128)(2,1)S(1)} %get-tuple-element.34), channel_id=1, replica_groups=mesh['group'=2,'block'=8,'fsdp'=2] {'block','fsdp'}, dimensions={0} | all-to-all | bytes 131072 | tf_op jit(solution)/shard_map/all_to_all | solution.py:460
  34.9 1.2 %shard_map.73 = (bf16[16,16,128]{2,1,0:T(8,128)(2,1)S(1)}, f32[8,128]{1,0:T(8,128)S(1)}) custom-call(f32[2048,512]{1,0:T(8,128)S(1)} %get-tuple-element.31.own_ref, f32[2048,512]{1,0:T(8,128)S(1)} %get-tuple-element.33.other_ref, bf16[16,16,128]{2,1,0:T(8,128)(2,1)S(1)} %all_to_all.26.got_ref, f32[8,128]{1,0:T(8,128)S(1)} %get-tuple-element.35.part_ref), custom_call_target="tpu_custom_call" | custom-call | flops 8388608 | tf_op jit(solution)/shard_map/pallas_call | solution.py:537
  36.0 8.4 %all_to_all.27.got_ref.second_ref = bf16[16,16,128]{2,1,0:T(8,128)(2,1)S(1)} all-to-all(bf16[16,16,128]{2,1,0:T(8,128)(2,1)S(1)} %get-tuple-element.36), channel_id=1, replica_groups=mesh['group'=2,'block'=8,'fsdp'=2] {'block','fsdp'}, dimensions={0} | all-to-all | bytes 131072 | tf_op jit(solution)/shard_map/all_to_all | solution.py:460
  44.4 1.3 %shard_map.74 = (bf16[16,8,128]{2,1,0:T(8,128)(2,1)S(1)}, f32[2048,512]{1,0:T(8,128)S(1)}, f32[2048,512]{1,0:T(8,128)S(1)}, bf16[4,256,512]{2,1,0:T(8,128)(2,1)S(1)}) custom-call(f32[2048,512]{1,0:T(8,128)S(1)} %get-tuple-element.31.own_ref, f32[2048,512]{1,0:T(8,128)S(1)} %get-tuple-element.33.other_ref, ...), custom_call_target="tpu_custom_call" | custom-call | flops 8388608 | tf_op jit(solution)/shard_map/pallas_call | solution.py:543
  45.7 8.2 %all_to_all.28.third_ref = bf16[16,8,128]{2,1,0:T(8,128)(2,1)S(1)} all-to-all(bf16[16,8,128]{2,1,0:T(8,128)(2,1)S(1)} %get-tuple-element.42), channel_id=1, replica_groups=mesh['group'=2,'block'=8,'fsdp'=2] {'block','fsdp'}, dimensions={0} | all-to-all | bytes 65536 | tf_op jit(solution)/shard_map/all_to_all | solution.py:460
  54.0 2.0 %shard_map.75 = (bf16[2,2048,512]{2,1,0:T(8,128)(2,1)S(1)}, f32[256,256]{1,0:T(8,128)S(1)}, bf16[256,256]{1,0:T(8,128)(2,1)S(1)}) custom-call(f32[2048,512]{1,0:T(8,128)S(1)} %get-tuple-element.37.own_mass_ref, f32[2048,512]{1,0:T(8,128)S(1)} %get-tuple-element.38.other_mass_ref, f32[2048,512]{1,0:T(8,128)S(1)} %get-tuple-element.39.own_student_ref, ...), custom_call_target="tpu_custom_call" | custom-call | flops 536870912 | tf_op jit(solution)/shard_map/pallas_call | solution.py:557
  56.0 0.1 collective-permute-start.2
  56.0 0.0 copy-start
  56.0 1.6 %shard_map.76._ = bf16[8,16,2560]{2,1,0:T(8,128)(2,1)S(1)} custom-call(bf16[2,2048,512]{2,1,0:T(8,128)(2,1)S(1)} %get-tuple-element.47.gradient_ref, bf16[256,512]{1,0:T(8,128)(2,1)S(1)} %get-tuple-element.48.own_turned_ref, bf16[256,512]{1,0:T(8,128)(2,1)S(1)} %get-tuple-element.49.other_turned_ref, f32[1,2048]{1,0:T(1,128)S(1)} %get-tuple-element.43.inverse_ref, ...), custom_call_target="tpu_custom_call" | custom-call | flops 1073741824 | tf_op jit(solution)/shard_map/pallas_call | solution.py:567
  57.7 0.0 collective-permute-done.2.other_ref
  57.7 0.1 shard_map.77
  57.7 14.3 %all_to_all.29.got_ref = bf16[8,16,2560]{2,1,0:T(8,128)(2,1)S(1)} all-to-all(bf16[8,16,2560]{2,1,0:T(8,128)(2,1)S(1)} %shard_map.77), channel_id=1, replica_groups=mesh['group'=2,'block'=8,'fsdp'=2] {'block'}, dimensions={0} | all-to-all | bytes 1310720 | tf_op jit(solution)/shard_map/all_to_all | solution.py:582
  72.1 0.0 copy-done
  72.1 1.2 %shard_map.78 = (f32[16,16384]{1,0:T(8,128)}, f32[32,256]{1,0:T(8,128)}) custom-call(bf16[8,16,2560]{2,1,0:T(8,128)(2,1)S(1)} %all_to_all.29.got_ref, bf16[32,256]{1,0:T(8,128)(2,1)S(1)} %copy-done), custom_call_target="tpu_custom_call" | custom-call | tf_op jit(solution)/shard_map/pallas_call | solution.py:583
  (1 shorter events, 0.0 us)
Async XLA Ops:
  1.5 7.1 %collective-permute-start = (bf16[48,512]{1,0:T(8,128)(2,1)S(1)}, bf16[48,512]{1,0:T(8,128)(2,1)S(1)}, u32[]{:S(2)}, u32[]{:S(2)}) collective-permute-start(bf16[48,512]{1,0:T(8,128)(2,1)S(1)} %shard_map.68.refs_0_), channel_id=1, source_target_pairs={{0,16},{16,0},{1,17},{17,1},{2,18},{18,2},{3,19},{19,3},{4,20},{20... | collective-permute-start | bytes 147464 | tf_op jit(solution)/shard_map/ppermute | solution.py:473
  22.3 1.9 %collective-permute-start.1 = (bf16[8,64,512]{2,1,0:T(8,128)(2,1)S(1)}, bf16[8,64,512]{2,1,0:T(8,128)(2,1)S(1)}, u32[]{:S(2)}, u32[]{:S(2)}) collective-permute-start(bf16[8,64,512]{2,1,0:T(8,128)(2,1)S(1)} %all_to_all.25.got_ref), channel_id=1, source_target_pairs={{0,1},{1,0},{2,3},{3,2},{4,5},{5,4},{6,7},{7,6},{8,9},{9,8},{10,11... | collective-permute-start | bytes 1572872 | tf_op jit(solution)/shard_map/ppermute | solution.py:457
  56.0 1.7 %collective-permute-start.2 = (bf16[256,256]{1,0:T(8,128)(2,1)S(1)}, bf16[256,256]{1,0:T(8,128)(2,1)S(1)}, u32[]{:S(2)}, u32[]{:S(2)}) collective-permute-start(bf16[256,256]{1,0:T(8,128)(2,1)S(1)} %get-tuple-element.46), channel_id=1, source_target_pairs={{0,1},{1,0},{2,3},{3,2},{4,5},{5,4},{6,7},{7,6},{8,9},{9,8},{10,11... | collective-permute-start | bytes 393224 | tf_op jit(solution)/shard_map/ppermute | solution.py:457
  56.0 16.0 %copy-start = (bf16[32,256]{1,0:T(8,128)(2,1)S(1)}, bf16[32,256]{1,0:T(8,128)(2,1)}, u32[]{:S(2)}) copy-start(bf16[32,256]{1,0:T(8,128)(2,1)} %student_ref.5) | copy-start | bytes 49156

commit v13 on v12

--- a/solution.py
+++ b/solution.py
@@ -356,7 +356,7 @@
 
 def gradient_kernel(
     own_mass_ref, other_mass_ref, own_student_ref, other_student_ref, weight_ref, second_ref, third_ref,
-    inverse_ref, copy_ref, gradient_ref, keep_ref, give_ref, unit_ref,
+    inverse_ref, copy_ref, turned_ref, gradient_ref, weight_out, keep_ref, give_ref, unit_ref,
 ):
     group, core = lax.axis_index("group"), lax.axis_index("fsdp")
     count, half = own_mass_ref.shape
@@ -373,6 +373,10 @@
             ):
                 gradient = student_ref[here, :] * student_scale - mass_ref[here, :] * teacher_scale
                 gradient_ref[side, start : start + TILE, :] = gradient.astype(jnp.bfloat16)
+                if side == 0:
+                    weight_out[:, here] = lax.dot_general(
+                        turned_ref[...], gradient_ref[0, here, :], (((1,), (1,)), ((), ())), preferred_element_type=jnp.float32
+                    )
 
     in_core_order(core, (0, own_mass_ref, own_student_ref), (1, other_mass_ref, other_student_ref), body)
     for start in range(0, count, TILE):
@@ -384,19 +388,17 @@
         out_ref[...] = jnp.transpose(feature).astype(out_ref.dtype)
 
 
-def weight_kernel(gradient_ref, own_turned_ref, other_turned_ref, inverse_ref, copy_ref, sent_ref, grad_ref):
+def weight_kernel(gradient_ref, own_weight_ref, turned_ref, inverse_ref, copy_ref, sent_ref, grad_ref):
     chips, rows_each, _ = sent_ref.shape
     count = gradient_ref.shape[1]
-    width = own_turned_ref.shape[0]
+    width = turned_ref.shape[0]
     kept = width // GROUPS
     own_rows = pl.ds(pl.multiple_of(lax.axis_index("group") * kept, kept), kept)
     for start in range(0, count, TILE):
         here, slot = slice(start, start + TILE), start // TILE
-        weight_grad = 0.0
-        for side, turned_ref in enumerate((own_turned_ref, other_turned_ref)):
-            weight_grad = weight_grad + lax.dot_general(
-                turned_ref[...], gradient_ref[side, here, :], (((1,), (1,)), ((), ())), preferred_element_type=jnp.float32
-            )
+        weight_grad = own_weight_ref[:, here] + lax.dot_general(
+            turned_ref[...], gradient_ref[1, here, :], (((1,), (1,)), ((), ())), preferred_element_type=jnp.float32
+        )
         unit = units_tile(copy_ref, inverse_ref, start)
         dot = jnp.sum(unit * weight_grad, axis=0, keepdims=True)
         grad_ref[slot] = (weight_grad - unit * dot) * inverse_ref[:, here]
@@ -554,13 +556,13 @@
     )(own_mass, other_mass, second, hbm(student_v))
     third = share(sent)
 
-    gradient, keep, give = call(
+    gradient, own_weight, keep, give = call(
         gradient_kernel,
-        (shape((2, count, half), bf16), shape((half // GROUPS, width), f32), shape((half // GROUPS, width), bf16)),
+        (shape((2, count, half), bf16), shape((width, count), f32), shape((half // GROUPS, width), f32), shape((half // GROUPS, width), bf16)),
         flops=2 * elements * width // GROUPS,
-        in_specs=[vmem] * 9,
+        in_specs=[vmem] * 10,
         scratch_shapes=[pltpu.VMEM((width, count), bf16)],
-    )(own_scaled, other_scaled, own_student, other_student, weights, second, third, inverse, student_copy)
+    )(own_scaled, other_scaled, own_student, other_student, weights, second, third, inverse, student_copy, own_turned)
     other = swap(give)
     out_rows = width // chips
     per_chip = rows * width // out_rows
@@ -570,7 +572,7 @@
         flops=2 * elements * width,
         in_specs=[vmem] * 5,
         scratch_shapes=[pltpu.VMEM((count // TILE, width, TILE), f32)],
-    )(gradient, own_turned, other_turned, inverse, student_copy)
+    )(gradient, own_weight, other_turned, inverse, student_copy)
     sent = call(
         pack_kernel,
         shape((blocks, out_rows, count + per_chip), bf16),

time: 73.6 us -> 74 us (level)
    pallas_call x1, Pallas kernels: 1.99 us -> 2.86 us  [kernel_body(): call(gradient_kernel, (shape((2, count, half), bf16), shape((width, count...]
  transfers between devices with their start and end apart: 3 -> 3, of which waited for: 1 -> 2; matrix products, arithmetic and copies ran while one was open for 0% -> 0% of each run, Pallas kernels for 8% -> 7%
where the time goes in v13:
time: 74 us; the launch traced here: 73.6 us
  blocking collectives  52.9 us (71%)
  Pallas kernels  15.1 us (20%)
  starting transfers between devices  4.18 us (6%)
  waiting for transfers between devices  0.76 us (1%)
  between operations  0.74 us (1%)
    all_to_all x3, blocking collectives, share(): return lax.all_to_all(values, GROUP, 0, 0)  25 us
    all_to_all x1, blocking collectives, kernel_body(): got = lax.all_to_all(sent, 'block', 0, 0)  14.2 us
    all_to_all x1, blocking collectives, kernel_body(): own = lax.all_to_all(sent, 'block', 0, 0)  13.7 us
    ppermute x1, starting transfers between devices, of_groups(): lax.ppermute(values, 'group', [(at, (at + back) % GROUPS) for at in range...  4.1 us
    pallas_call x1, Pallas kernels, kernel_body(): call(directions_kernel, (shape((count, width), bf16), shape((count, width...  2.96 us
    pallas_call x1, Pallas kernels, kernel_body(): call(gradient_kernel, (shape((2, count, half), bf16), shape((width, count...  2.86 us
    pallas_call x1, Pallas kernels, kernel_body(): call(functools.partial(other_kernel, prototypes), (shape((count, half), f...  2.24 us
  transfers between devices with their start and end apart: 3, of which 2 were waited for; matrix products, arithmetic and copies ran while one was open for 0% of the time, Pallas kernels for 7%

profile of v13, /device:TPU:0, one launch (start us, length us, event | category | flops | bytes accessed | tf_op | source)
XLA Modules:
  0.0 73.6 jit_solution(17588750341509495658)
XLA Ops:
  0.6 0.9 %shard_map.68.refs_0_ = bf16[48,512]{1,0:T(8,128)(2,1)S(1)} custom-call(bf16[32,256]{1,0:T(8,128)(2,1)} %teacher_ref.2, bf16[32,256]{1,0:T(8,128)(2,1)} %student_ref.5, bf16[1,32]{1,0:T(2,128)(2,1)} %bitcast.2), custom_call_target="tpu_custom_call" | custom-call | tf_op jit(solution)/shard_map/pallas_call | solution.py:466
  1.5 4.1 %collective-permute-start = (bf16[48,512]{1,0:T(8,128)(2,1)S(1)}, bf16[48,512]{1,0:T(8,128)(2,1)S(1)}, u32[]{:S(2)}, u32[]{:S(2)}) collective-permute-start(bf16[48,512]{1,0:T(8,128)(2,1)S(1)} %shard_map.68.refs_0_), channel_id=1, source_target_pairs={{0,16},{16,0},{1,17},{17,1},{2,18},{18,2},{3,19},{19,3},{4,20},{20... | collective-permute-start | bytes 147464 | tf_op jit(solution)/shard_map/ppermute | solution.py:475
  5.6 3.0 %shard_map.69 = (bf16[2048,256]{1,0:T(8,128)(2,1)S(1)}, bf16[2048,256]{1,0:T(8,128)(2,1)S(1)}, f32[1,2048]{1,0:T(1,128)S(1)}) custom-call(s32[1]{0:T(128)} %bitcast.1.block_ref, bf16[256,16384]{1,0:T(8,128)(2,1)} %teacher_ref.3, bf16[256,16384]{1,0:T(8,128)(2,1)} %directions_ref.1), custom_call_target="tpu_custom_call" | custom-call | flops 6291456 | bytes 4194304 | tf_op jit(solution)/shard_map/pallas_call | solution.py:485
  8.6 0.0 collective-permute-done.refs_1_
  8.6 13.7 %all_to_all.25.got_ref = bf16[8,64,512]{2,1,0:T(8,128)(2,1)S(1)} all-to-all(bf16[8,64,512]{2,1,0:T(8,128)(2,1)S(1)} %shard_map.70), channel_id=1, replica_groups=mesh['group'=2,'block'=8,'fsdp'=2] {'block'}, dimensions={0} | all-to-all | bytes 1048576 | tf_op jit(solution)/shard_map/all_to_all | solution.py:508
  22.3 0.0 collective-permute-start.1
  22.3 1.3 %shard_map.71 = (f32[2048,512]{1,0:T(8,128)S(1)}, f32[2048,512]{1,0:T(8,128)S(1)}, f32[8,512]{1,0:T(8,128)S(1)}, bf16[256,512]{1,0:T(8,128)(2,1)S(1)}) custom-call(bf16[2048,256]{1,0:T(8,128)(2,1)S(1)} %get-tuple-element.28.teacher_w_ref, bf16[2048,256]{1,0:T(8,128)(2,1)S(1)} %get-tuple-element.29.student_w_ref, bf16[8,64,512]{2,1,0:T(8,128)(2,1)S(1)} %all_to_all.25.got_ref), custom_call_target="tpu_custom_call" | custom-call | flops 1073741824 | tf_op jit(solution)/shard_map/pallas_call | solution.py:515
  23.6 0.6 collective-permute-done.1.got_ref
  24.2 2.2 %shard_map.72 = (f32[2048,512]{1,0:T(8,128)S(1)}, f32[2048,512]{1,0:T(8,128)S(1)}, bf16[16,16,128]{2,1,0:T(8,128)(2,1)S(1)}, f32[8,128]{1,0:T(8,128)S(1)}, bf16[256,512]{1,0:T(8,128)(2,1)S(1)}) custom-call(bf16[2048,256]{1,0:T(8,128)(2,1)S(1)} %get-tuple-element.28.teacher_w_ref, bf16[2048,256]{1,0:T(8,128)(2,1)S(1)} %get-tuple-element.29.student_w_ref, ...), custom_call_target="tpu_custom_call" | custom-call | flops 1073741824 | tf_op jit(solution)/shard_map/pallas_call | solution.py:526
  26.5 8.4 %all_to_all.26.got_ref = bf16[16,16,128]{2,1,0:T(8,128)(2,1)S(1)} all-to-all(bf16[16,16,128]{2,1,0:T(8,128)(2,1)S(1)} %get-tuple-element.35), channel_id=1, replica_groups=mesh['group'=2,'block'=8,'fsdp'=2] {'block','fsdp'}, dimensions={0} | all-to-all | bytes 131072 | tf_op jit(solution)/shard_map/all_to_all | solution.py:462
  34.9 1.2 %shard_map.73 = (bf16[16,16,128]{2,1,0:T(8,128)(2,1)S(1)}, f32[8,128]{1,0:T(8,128)S(1)}) custom-call(f32[2048,512]{1,0:T(8,128)S(1)} %get-tuple-element.32.own_ref, f32[2048,512]{1,0:T(8,128)S(1)} %get-tuple-element.34.other_ref, bf16[16,16,128]{2,1,0:T(8,128)(2,1)S(1)} %all_to_all.26.got_ref, f32[8,128]{1,0:T(8,128)S(1)} %get-tuple-element.36.part_ref), custom_call_target="tpu_custom_call" | custom-call | flops 8388608 | tf_op jit(solution)/shard_map/pallas_call | solution.py:539
  36.0 8.4 %all_to_all.27.got_ref.second_ref = bf16[16,16,128]{2,1,0:T(8,128)(2,1)S(1)} all-to-all(bf16[16,16,128]{2,1,0:T(8,128)(2,1)S(1)} %get-tuple-element.37), channel_id=1, replica_groups=mesh['group'=2,'block'=8,'fsdp'=2] {'block','fsdp'}, dimensions={0} | all-to-all | bytes 131072 | tf_op jit(solution)/shard_map/all_to_all | solution.py:462
  44.4 1.3 %shard_map.74 = (bf16[16,8,128]{2,1,0:T(8,128)(2,1)S(1)}, f32[2048,512]{1,0:T(8,128)S(1)}, f32[2048,512]{1,0:T(8,128)S(1)}, bf16[4,256,512]{2,1,0:T(8,128)(2,1)S(1)}) custom-call(f32[2048,512]{1,0:T(8,128)S(1)} %get-tuple-element.32.own_ref, f32[2048,512]{1,0:T(8,128)S(1)} %get-tuple-element.34.other_ref, ...), custom_call_target="tpu_custom_call" | custom-call | flops 8388608 | tf_op jit(solution)/shard_map/pallas_call | solution.py:545
  45.7 8.2 %all_to_all.28.third_ref = bf16[16,8,128]{2,1,0:T(8,128)(2,1)S(1)} all-to-all(bf16[16,8,128]{2,1,0:T(8,128)(2,1)S(1)} %get-tuple-element.43), channel_id=1, replica_groups=mesh['group'=2,'block'=8,'fsdp'=2] {'block','fsdp'}, dimensions={0} | all-to-all | bytes 65536 | tf_op jit(solution)/shard_map/all_to_all | solution.py:462
  54.0 2.9 %shard_map.75 = (bf16[2,2048,512]{2,1,0:T(8,128)(2,1)S(1)}, f32[256,2048]{1,0:T(8,128)S(1)}, f32[256,256]{1,0:T(8,128)S(1)}, bf16[256,256]{1,0:T(8,128)(2,1)S(1)}) custom-call(f32[2048,512]{1,0:T(8,128)S(1)} %get-tuple-element.38.own_mass_ref, f32[2048,512]{1,0:T(8,128)S(1)} %get-tuple-element.39.other_mass_ref, ...), custom_call_target="tpu_custom_call" | custom-call | flops 536870912 | tf_op jit(solution)/shard_map/pallas_call | solution.py:559
  56.8 0.1 collective-permute-start.2
  56.9 0.0 copy-start
  56.9 1.1 %shard_map.76._ = bf16[8,16,2560]{2,1,0:T(8,128)(2,1)S(1)} custom-call(bf16[2,2048,512]{2,1,0:T(8,128)(2,1)S(1)} %get-tuple-element.49.gradient_ref, f32[256,2048]{1,0:T(8,128)S(1)} %get-tuple-element.50.own_weight_ref, bf16[256,512]{1,0:T(8,128)(2,1)S(1)} %get-tuple-element.51.turned_ref, f32[1,2048]{1,0:T(1,128)S(1)} %get-tuple-element.44.inverse_ref, ...), custom_call_target="tpu_custom_call" | custom-call | flops 1073741824 | tf_op jit(solution)/shard_map/pallas_call | solution.py:569
  58.1 0.2 collective-permute-done.2.other_ref
  58.3 14.2 %all_to_all.29.got_ref = bf16[8,16,2560]{2,1,0:T(8,128)(2,1)S(1)} all-to-all(bf16[8,16,2560]{2,1,0:T(8,128)(2,1)S(1)} %shard_map.77), channel_id=1, replica_groups=mesh['group'=2,'block'=8,'fsdp'=2] {'block'}, dimensions={0} | all-to-all | bytes 1310720 | tf_op jit(solution)/shard_map/all_to_all | solution.py:584
  72.5 0.0 copy-done
  72.5 1.2 %shard_map.78 = (f32[16,16384]{1,0:T(8,128)}, f32[32,256]{1,0:T(8,128)}) custom-call(bf16[8,16,2560]{2,1,0:T(8,128)(2,1)S(1)} %all_to_all.29.got_ref, bf16[32,256]{1,0:T(8,128)(2,1)S(1)} %copy-done), custom_call_target="tpu_custom_call" | custom-call | tf_op jit(solution)/shard_map/pallas_call | solution.py:585
  (2 shorter events, 0.1 us)
Async XLA Ops:
  1.5 7.1 %collective-permute-start = (bf16[48,512]{1,0:T(8,128)(2,1)S(1)}, bf16[48,512]{1,0:T(8,128)(2,1)S(1)}, u32[]{:S(2)}, u32[]{:S(2)}) collective-permute-start(bf16[48,512]{1,0:T(8,128)(2,1)S(1)} %shard_map.68.refs_0_), channel_id=1, source_target_pairs={{0,16},{16,0},{1,17},{17,1},{2,18},{18,2},{3,19},{19,3},{4,20},{20... | collective-permute-start | bytes 147464 | tf_op jit(solution)/shard_map/ppermute | solution.py:475
  22.3 1.9 %collective-permute-start.1 = (bf16[8,64,512]{2,1,0:T(8,128)(2,1)S(1)}, bf16[8,64,512]{2,1,0:T(8,128)(2,1)S(1)}, u32[]{:S(2)}, u32[]{:S(2)}) collective-permute-start(bf16[8,64,512]{2,1,0:T(8,128)(2,1)S(1)} %all_to_all.25.got_ref), channel_id=1, source_target_pairs={{0,1},{1,0},{2,3},{3,2},{4,5},{5,4},{6,7},{7,6},{8,9},{9,8},{10,11... | collective-permute-start | bytes 1572872 | tf_op jit(solution)/shard_map/ppermute | solution.py:459
  56.8 1.4 %collective-permute-start.2 = (bf16[256,256]{1,0:T(8,128)(2,1)S(1)}, bf16[256,256]{1,0:T(8,128)(2,1)S(1)}, u32[]{:S(2)}, u32[]{:S(2)}) collective-permute-start(bf16[256,256]{1,0:T(8,128)(2,1)S(1)} %get-tuple-element.48), channel_id=1, source_target_pairs={{0,1},{1,0},{2,3},{3,2},{4,5},{5,4},{6,7},{7,6},{8,9},{9,8},{10,11... | collective-permute-start | bytes 393224 | tf_op jit(solution)/shard_map/ppermute | solution.py:459
  56.9 15.6 %copy-start = (bf16[32,256]{1,0:T(8,128)(2,1)S(1)}, bf16[32,256]{1,0:T(8,128)(2,1)}, u32[]{:S(2)}) copy-start(bf16[32,256]{1,0:T(8,128)(2,1)} %student_ref.5) | copy-start | bytes 49156

commit v14 on v12

--- a/solution.py
+++ b/solution.py
@@ -25,7 +25,7 @@
 
 EVERY = ("dp", "fsdp")
 CHIPS = ("group", "block")
-GROUP = ("block", "fsdp")
+GROUP = ("fsdp", "block")
 
 
 def unit_rows(values):

time: 73.6 us -> 73.3 us (level)
  no operation moved by 1% of the time
where the time goes in v14:
time: 73.3 us; the launch traced here: 72.9 us
  blocking collectives  52.7 us (72%)
  Pallas kernels  14.7 us (20%)
  starting transfers between devices  4.18 us (6%)
  between operations  0.74 us (1%)
    all_to_all x3, blocking collectives, share(): return lax.all_to_all(values, GROUP, 0, 0)  24.7 us
    all_to_all x1, blocking collectives, kernel_body(): got = lax.all_to_all(sent, 'block', 0, 0)  14.3 us
    all_to_all x1, blocking collectives, kernel_body(): own = lax.all_to_all(sent, 'block', 0, 0)  13.7 us
    ppermute x1, starting transfers between devices, of_groups(): lax.ppermute(values, 'group', [(at, (at + back) % GROUPS) for at in range...  4.1 us
    pallas_call x1, Pallas kernels, kernel_body(): call(directions_kernel, (shape((count, width), bf16), shape((count, width...  2.96 us
    pallas_call x1, Pallas kernels, kernel_body(): call(functools.partial(other_kernel, prototypes), (shape((count, half), f...  2.24 us
    pallas_call x1, Pallas kernels, kernel_body(): call(gradient_kernel, (shape((2, count, half), bf16), shape((half // GROU...  1.99 us
    pallas_call x1, Pallas kernels, kernel_body(): call(weight_kernel, shape((blocks, out_rows, count + per_chip), bf16), fl...  1.6 us
  transfers between devices with their start and end apart: 3, of which 1 were waited for; matrix products, arithmetic and copies ran while one was open for 0% of the time, Pallas kernels for 8%

profile of v14, /device:TPU:0, one launch (start us, length us, event | category | flops | bytes accessed | tf_op | source)
XLA Modules:
  0.0 72.9 jit_solution(18119264036305083893)
XLA Ops:
  0.6 0.9 %shard_map.68.refs_0_ = bf16[48,512]{1,0:T(8,128)(2,1)S(1)} custom-call(bf16[32,256]{1,0:T(8,128)(2,1)} %teacher_ref.2, bf16[32,256]{1,0:T(8,128)(2,1)} %student_ref.5, bf16[1,32]{1,0:T(2,128)(2,1)} %bitcast.2), custom_call_target="tpu_custom_call" | custom-call | tf_op jit(solution)/shard_map/pallas_call | solution.py:464
  1.5 4.1 %collective-permute-start = (bf16[48,512]{1,0:T(8,128)(2,1)S(1)}, bf16[48,512]{1,0:T(8,128)(2,1)S(1)}, u32[]{:S(2)}, u32[]{:S(2)}) collective-permute-start(bf16[48,512]{1,0:T(8,128)(2,1)S(1)} %shard_map.68.refs_0_), channel_id=1, source_target_pairs={{0,16},{16,0},{1,17},{17,1},{2,18},{18,2},{3,19},{19,3},{4,20},{20... | collective-permute-start | bytes 147464 | tf_op jit(solution)/shard_map/ppermute | solution.py:473
  5.6 3.0 %shard_map.69 = (bf16[2048,256]{1,0:T(8,128)(2,1)S(1)}, bf16[2048,256]{1,0:T(8,128)(2,1)S(1)}, f32[1,2048]{1,0:T(1,128)S(1)}) custom-call(s32[1]{0:T(128)} %bitcast.1.block_ref, bf16[256,16384]{1,0:T(8,128)(2,1)} %teacher_ref.3, bf16[256,16384]{1,0:T(8,128)(2,1)} %directions_ref.1), custom_call_target="tpu_custom_call" | custom-call | flops 6291456 | bytes 4194304 | tf_op jit(solution)/shard_map/pallas_call | solution.py:483
  8.6 0.0 collective-permute-done.refs_1_
  8.6 13.7 %all_to_all.25.got_ref = bf16[8,64,512]{2,1,0:T(8,128)(2,1)S(1)} all-to-all(bf16[8,64,512]{2,1,0:T(8,128)(2,1)S(1)} %shard_map.70), channel_id=1, replica_groups=mesh['group'=2,'block'=8,'fsdp'=2] {'block'}, dimensions={0} | all-to-all | bytes 1048576 | tf_op jit(solution)/shard_map/all_to_all | solution.py:506
  22.3 0.0 collective-permute-start.1
  22.3 1.3 %shard_map.71 = (f32[2048,512]{1,0:T(8,128)S(1)}, f32[2048,512]{1,0:T(8,128)S(1)}, f32[8,512]{1,0:T(8,128)S(1)}, bf16[256,512]{1,0:T(8,128)(2,1)S(1)}) custom-call(bf16[2048,256]{1,0:T(8,128)(2,1)S(1)} %get-tuple-element.27.teacher_w_ref, bf16[2048,256]{1,0:T(8,128)(2,1)S(1)} %get-tuple-element.28.student_w_ref, bf16[8,64,512]{2,1,0:T(8,128)(2,1)S(1)} %all_to_all.25.got_ref), custom_call_target="tpu_custom_call" | custom-call | flops 1073741824 | tf_op jit(solution)/shard_map/pallas_call | solution.py:513
  23.6 0.6 collective-permute-done.1.got_ref
  24.2 2.2 %shard_map.72 = (f32[2048,512]{1,0:T(8,128)S(1)}, f32[2048,512]{1,0:T(8,128)S(1)}, bf16[16,16,128]{2,1,0:T(8,128)(2,1)S(1)}, f32[8,128]{1,0:T(8,128)S(1)}, bf16[256,512]{1,0:T(8,128)(2,1)S(1)}) custom-call(bf16[2048,256]{1,0:T(8,128)(2,1)S(1)} %get-tuple-element.27.teacher_w_ref, bf16[2048,256]{1,0:T(8,128)(2,1)S(1)} %get-tuple-element.28.student_w_ref, ...), custom_call_target="tpu_custom_call" | custom-call | flops 1073741824 | tf_op jit(solution)/shard_map/pallas_call | solution.py:524
  26.5 8.3 %all_to_all.26.got_ref = bf16[16,16,128]{2,1,0:T(8,128)(2,1)S(1)} all-to-all(bf16[16,16,128]{2,1,0:T(8,128)(2,1)S(1)} %get-tuple-element.34), channel_id=1, replica_groups=mesh['group'=2,'block'=8,'fsdp'=2] {'fsdp','block'}, dimensions={0} | all-to-all | bytes 131072 | tf_op jit(solution)/shard_map/all_to_all | solution.py:460
  34.7 1.2 %shard_map.73 = (bf16[16,16,128]{2,1,0:T(8,128)(2,1)S(1)}, f32[8,128]{1,0:T(8,128)S(1)}) custom-call(f32[2048,512]{1,0:T(8,128)S(1)} %get-tuple-element.31.own_ref, f32[2048,512]{1,0:T(8,128)S(1)} %get-tuple-element.33.other_ref, bf16[16,16,128]{2,1,0:T(8,128)(2,1)S(1)} %all_to_all.26.got_ref, f32[8,128]{1,0:T(8,128)S(1)} %get-tuple-element.35.part_ref), custom_call_target="tpu_custom_call" | custom-call | flops 8388608 | tf_op jit(solution)/shard_map/pallas_call | solution.py:537
  35.9 8.3 %all_to_all.27.got_ref.second_ref = bf16[16,16,128]{2,1,0:T(8,128)(2,1)S(1)} all-to-all(bf16[16,16,128]{2,1,0:T(8,128)(2,1)S(1)} %get-tuple-element.36), channel_id=1, replica_groups=mesh['group'=2,'block'=8,'fsdp'=2] {'fsdp','block'}, dimensions={0} | all-to-all | bytes 131072 | tf_op jit(solution)/shard_map/all_to_all | solution.py:460
  44.2 1.3 %shard_map.74 = (bf16[16,8,128]{2,1,0:T(8,128)(2,1)S(1)}, f32[2048,512]{1,0:T(8,128)S(1)}, f32[2048,512]{1,0:T(8,128)S(1)}, bf16[4,256,512]{2,1,0:T(8,128)(2,1)S(1)}) custom-call(f32[2048,512]{1,0:T(8,128)S(1)} %get-tuple-element.31.own_ref, f32[2048,512]{1,0:T(8,128)S(1)} %get-tuple-element.33.other_ref, ...), custom_call_target="tpu_custom_call" | custom-call | flops 8388608 | tf_op jit(solution)/shard_map/pallas_call | solution.py:543
  45.5 8.1 %all_to_all.28.third_ref = bf16[16,8,128]{2,1,0:T(8,128)(2,1)S(1)} all-to-all(bf16[16,8,128]{2,1,0:T(8,128)(2,1)S(1)} %get-tuple-element.42), channel_id=1, replica_groups=mesh['group'=2,'block'=8,'fsdp'=2] {'fsdp','block'}, dimensions={0} | all-to-all | bytes 65536 | tf_op jit(solution)/shard_map/all_to_all | solution.py:460
  53.6 2.0 %shard_map.75 = (bf16[2,2048,512]{2,1,0:T(8,128)(2,1)S(1)}, f32[256,256]{1,0:T(8,128)S(1)}, bf16[256,256]{1,0:T(8,128)(2,1)S(1)}) custom-call(f32[2048,512]{1,0:T(8,128)S(1)} %get-tuple-element.37.own_mass_ref, f32[2048,512]{1,0:T(8,128)S(1)} %get-tuple-element.38.other_mass_ref, f32[2048,512]{1,0:T(8,128)S(1)} %get-tuple-element.39.own_student_ref, ...), custom_call_target="tpu_custom_call" | custom-call | flops 536870912 | tf_op jit(solution)/shard_map/pallas_call | solution.py:557
  55.6 0.1 collective-permute-start.2
  55.7 0.0 copy-start
  55.7 1.6 %shard_map.76._ = bf16[8,16,2560]{2,1,0:T(8,128)(2,1)S(1)} custom-call(bf16[2,2048,512]{2,1,0:T(8,128)(2,1)S(1)} %get-tuple-element.47.gradient_ref, bf16[256,512]{1,0:T(8,128)(2,1)S(1)} %get-tuple-element.48.own_turned_ref, bf16[256,512]{1,0:T(8,128)(2,1)S(1)} %get-tuple-element.49.other_turned_ref, f32[1,2048]{1,0:T(1,128)S(1)} %get-tuple-element.43.inverse_ref, ...), custom_call_target="tpu_custom_call" | custom-call | flops 1073741824 | tf_op jit(solution)/shard_map/pallas_call | solution.py:567
  57.3 0.0 collective-permute-done.2.other_ref
  57.3 0.1 shard_map.77
  57.4 14.3 %all_to_all.29.got_ref = bf16[8,16,2560]{2,1,0:T(8,128)(2,1)S(1)} all-to-all(bf16[8,16,2560]{2,1,0:T(8,128)(2,1)S(1)} %shard_map.77), channel_id=1, replica_groups=mesh['group'=2,'block'=8,'fsdp'=2] {'block'}, dimensions={0} | all-to-all | bytes 1310720 | tf_op jit(solution)/shard_map/all_to_all | solution.py:582
  71.7 0.0 copy-done
  71.7 1.2 %shard_map.78 = (f32[16,16384]{1,0:T(8,128)}, f32[32,256]{1,0:T(8,128)}) custom-call(bf16[8,16,2560]{2,1,0:T(8,128)(2,1)S(1)} %all_to_all.29.got_ref, bf16[32,256]{1,0:T(8,128)(2,1)S(1)} %copy-done), custom_call_target="tpu_custom_call" | custom-call | tf_op jit(solution)/shard_map/pallas_call | solution.py:583
  (1 shorter events, 0.0 us)
Async XLA Ops:
  1.5 7.1 %collective-permute-start = (bf16[48,512]{1,0:T(8,128)(2,1)S(1)}, bf16[48,512]{1,0:T(8,128)(2,1)S(1)}, u32[]{:S(2)}, u32[]{:S(2)}) collective-permute-start(bf16[48,512]{1,0:T(8,128)(2,1)S(1)} %shard_map.68.refs_0_), channel_id=1, source_target_pairs={{0,16},{16,0},{1,17},{17,1},{2,18},{18,2},{3,19},{19,3},{4,20},{20... | collective-permute-start | bytes 147464 | tf_op jit(solution)/shard_map/ppermute | solution.py:473
  22.3 1.9 %collective-permute-start.1 = (bf16[8,64,512]{2,1,0:T(8,128)(2,1)S(1)}, bf16[8,64,512]{2,1,0:T(8,128)(2,1)S(1)}, u32[]{:S(2)}, u32[]{:S(2)}) collective-permute-start(bf16[8,64,512]{2,1,0:T(8,128)(2,1)S(1)} %all_to_all.25.got_ref), channel_id=1, source_target_pairs={{0,1},{1,0},{2,3},{3,2},{4,5},{5,4},{6,7},{7,6},{8,9},{9,8},{10,11... | collective-permute-start | bytes 1572872 | tf_op jit(solution)/shard_map/ppermute | solution.py:457
  55.6 1.7 %collective-permute-start.2 = (bf16[256,256]{1,0:T(8,128)(2,1)S(1)}, bf16[256,256]{1,0:T(8,128)(2,1)S(1)}, u32[]{:S(2)}, u32[]{:S(2)}) collective-permute-start(bf16[256,256]{1,0:T(8,128)(2,1)S(1)} %get-tuple-element.46), channel_id=1, source_target_pairs={{0,1},{1,0},{2,3},{3,2},{4,5},{5,4},{6,7},{7,6},{8,9},{9,8},{10,11... | collective-permute-start | bytes 393224 | tf_op jit(solution)/shard_map/ppermute | solution.py:457
  55.7 16.0 %copy-start = (bf16[32,256]{1,0:T(8,128)(2,1)S(1)}, bf16[32,256]{1,0:T(8,128)(2,1)}, u32[]{:S(2)}) copy-start(bf16[32,256]{1,0:T(8,128)(2,1)} %student_ref.5) | copy-start | bytes 49156

commit v15 on v14

--- a/solution.py
+++ b/solution.py
@@ -16,7 +16,7 @@
 epsilon = 1e-06
 
 GROUPS = 2
-TILE = 256
+TILE = 512
 HALF_TILE = 256
 FETCH = 2
 LANES = 128

time: 73.3 us -> 72.5 us (0.989)
  Pallas kernels: 14.7 us -> 13.9 us
    pallas_call x1, Pallas kernels: 2.96 us -> 2.14 us  [kernel_body(): call(directions_kernel, (shape((count, width), bf16), shape((count, width...]
  transfers between devices with their start and end apart: 3 -> 3, of which waited for: 1 -> 2; matrix products, arithmetic and copies ran while one was open for 0% -> 0% of each run, Pallas kernels for 8% -> 7%
where the time goes in v15:
time: 72.5 us; the launch traced here: 72.1 us
  blocking collectives  52.2 us (72%)
  Pallas kernels  13.9 us (19%)
  starting transfers between devices  4.18 us (6%)
  waiting for transfers between devices  1.02 us (1%)
  between operations  0.73 us (1%)
    all_to_all x3, blocking collectives, share(): return lax.all_to_all(values, GROUP, 0, 0)  24.7 us
    all_to_all x1, blocking collectives, kernel_body(): got = lax.all_to_all(sent, 'block', 0, 0)  14.3 us
    all_to_all x1, blocking collectives, kernel_body(): own = lax.all_to_all(sent, 'block', 0, 0)  13.2 us
    ppermute x1, starting transfers between devices, of_groups(): lax.ppermute(values, 'group', [(at, (at + back) % GROUPS) for at in range...  4.1 us
    pallas_call x1, Pallas kernels, kernel_body(): call(functools.partial(other_kernel, prototypes), (shape((count, half), f...  2.24 us
    pallas_call x1, Pallas kernels, kernel_body(): call(directions_kernel, (shape((count, width), bf16), shape((count, width...  2.14 us
    pallas_call x1, Pallas kernels, kernel_body(): call(gradient_kernel, (shape((2, count, half), bf16), shape((half // GROU...  1.98 us
    pallas_call x1, Pallas kernels, kernel_body(): call(weight_kernel, shape((blocks, out_rows, count + per_chip), bf16), fl...  1.68 us
  transfers between devices with their start and end apart: 3, of which 2 were waited for; matrix products, arithmetic and copies ran while one was open for 0% of the time, Pallas kernels for 7%

profile of v15, /device:TPU:0, one launch (start us, length us, event | category | flops | bytes accessed | tf_op | source)
XLA Modules:
  0.0 72.1 jit_solution(16431330193895599006)
XLA Ops:
  0.6 0.9 %shard_map.68.refs_0_ = bf16[48,512]{1,0:T(8,128)(2,1)S(1)} custom-call(bf16[32,256]{1,0:T(8,128)(2,1)} %teacher_ref.2, bf16[32,256]{1,0:T(8,128)(2,1)} %student_ref.5, bf16[1,32]{1,0:T(2,128)(2,1)} %bitcast.2), custom_call_target="tpu_custom_call" | custom-call | tf_op jit(solution)/shard_map/pallas_call | solution.py:464
  1.5 4.1 %collective-permute-start = (bf16[48,512]{1,0:T(8,128)(2,1)S(1)}, bf16[48,512]{1,0:T(8,128)(2,1)S(1)}, u32[]{:S(2)}, u32[]{:S(2)}) collective-permute-start(bf16[48,512]{1,0:T(8,128)(2,1)S(1)} %shard_map.68.refs_0_), channel_id=1, source_target_pairs={{0,16},{16,0},{1,17},{17,1},{2,18},{18,2},{3,19},{19,3},{4,20},{20... | collective-permute-start | bytes 147464 | tf_op jit(solution)/shard_map/ppermute | solution.py:473
  5.6 2.1 %shard_map.69 = (bf16[2048,256]{1,0:T(8,128)(2,1)S(1)}, bf16[2048,256]{1,0:T(8,128)(2,1)S(1)}, f32[1,2048]{1,0:T(1,128)S(1)}) custom-call(s32[1]{0:T(128)} %bitcast.1.block_ref, bf16[256,16384]{1,0:T(8,128)(2,1)} %teacher_ref.3, bf16[256,16384]{1,0:T(8,128)(2,1)} %directions_ref.1), custom_call_target="tpu_custom_call" | custom-call | flops 6291456 | bytes 4194304 | tf_op jit(solution)/shard_map/pallas_call | solution.py:483
  7.8 0.4 collective-permute-done.refs_1_
  8.2 13.2 %all_to_all.25.got_ref = bf16[8,64,512]{2,1,0:T(8,128)(2,1)S(1)} all-to-all(bf16[8,64,512]{2,1,0:T(8,128)(2,1)S(1)} %shard_map.70), channel_id=1, replica_groups=mesh['group'=2,'block'=8,'fsdp'=2] {'block'}, dimensions={0} | all-to-all | bytes 1048576 | tf_op jit(solution)/shard_map/all_to_all | solution.py:506
  21.5 0.0 collective-permute-start.1
  21.5 1.3 %shard_map.71 = (f32[2048,512]{1,0:T(8,128)S(1)}, f32[2048,512]{1,0:T(8,128)S(1)}, f32[8,512]{1,0:T(8,128)S(1)}, bf16[256,512]{1,0:T(8,128)(2,1)S(1)}) custom-call(bf16[2048,256]{1,0:T(8,128)(2,1)S(1)} %get-tuple-element.27.teacher_w_ref, bf16[2048,256]{1,0:T(8,128)(2,1)S(1)} %get-tuple-element.28.student_w_ref, bf16[8,64,512]{2,1,0:T(8,128)(2,1)S(1)} %all_to_all.25.got_ref), custom_call_target="tpu_custom_call" | custom-call | flops 1073741824 | tf_op jit(solution)/shard_map/pallas_call | solution.py:513
  22.8 0.6 collective-permute-done.1.got_ref
  23.4 2.2 %shard_map.72 = (f32[2048,512]{1,0:T(8,128)S(1)}, f32[2048,512]{1,0:T(8,128)S(1)}, bf16[16,16,128]{2,1,0:T(8,128)(2,1)S(1)}, f32[8,128]{1,0:T(8,128)S(1)}, bf16[256,512]{1,0:T(8,128)(2,1)S(1)}) custom-call(bf16[2048,256]{1,0:T(8,128)(2,1)S(1)} %get-tuple-element.27.teacher_w_ref, bf16[2048,256]{1,0:T(8,128)(2,1)S(1)} %get-tuple-element.28.student_w_ref, ...), custom_call_target="tpu_custom_call" | custom-call | flops 1073741824 | tf_op jit(solution)/shard_map/pallas_call | solution.py:524
  25.6 8.3 %all_to_all.26.got_ref = bf16[16,16,128]{2,1,0:T(8,128)(2,1)S(1)} all-to-all(bf16[16,16,128]{2,1,0:T(8,128)(2,1)S(1)} %get-tuple-element.34), channel_id=1, replica_groups=mesh['group'=2,'block'=8,'fsdp'=2] {'fsdp','block'}, dimensions={0} | all-to-all | bytes 131072 | tf_op jit(solution)/shard_map/all_to_all | solution.py:460
  33.9 1.2 %shard_map.73 = (bf16[16,16,128]{2,1,0:T(8,128)(2,1)S(1)}, f32[8,128]{1,0:T(8,128)S(1)}) custom-call(f32[2048,512]{1,0:T(8,128)S(1)} %get-tuple-element.31.own_ref, f32[2048,512]{1,0:T(8,128)S(1)} %get-tuple-element.33.other_ref, bf16[16,16,128]{2,1,0:T(8,128)(2,1)S(1)} %all_to_all.26.got_ref, f32[8,128]{1,0:T(8,128)S(1)} %get-tuple-element.35.part_ref), custom_call_target="tpu_custom_call" | custom-call | flops 8388608 | tf_op jit(solution)/shard_map/pallas_call | solution.py:537
  35.1 8.3 %all_to_all.27.got_ref.second_ref = bf16[16,16,128]{2,1,0:T(8,128)(2,1)S(1)} all-to-all(bf16[16,16,128]{2,1,0:T(8,128)(2,1)S(1)} %get-tuple-element.36), channel_id=1, replica_groups=mesh['group'=2,'block'=8,'fsdp'=2] {'fsdp','block'}, dimensions={0} | all-to-all | bytes 131072 | tf_op jit(solution)/shard_map/all_to_all | solution.py:460
  43.3 1.3 %shard_map.74 = (bf16[16,8,128]{2,1,0:T(8,128)(2,1)S(1)}, f32[2048,512]{1,0:T(8,128)S(1)}, f32[2048,512]{1,0:T(8,128)S(1)}, bf16[2,256,1024]{2,1,0:T(8,128)(2,1)S(1)}) custom-call(f32[2048,512]{1,0:T(8,128)S(1)} %get-tuple-element.31.own_ref, f32[2048,512]{1,0:T(8,128)S(1)} %get-tuple-element.33.other_ref, ...), custom_call_target="tpu_custom_call" | custom-call | flops 8388608 | tf_op jit(solution)/shard_map/pallas_call | solution.py:543
  44.6 8.1 %all_to_all.28.third_ref = bf16[16,8,128]{2,1,0:T(8,128)(2,1)S(1)} all-to-all(bf16[16,8,128]{2,1,0:T(8,128)(2,1)S(1)} %get-tuple-element.42), channel_id=1, replica_groups=mesh['group'=2,'block'=8,'fsdp'=2] {'fsdp','block'}, dimensions={0} | all-to-all | bytes 65536 | tf_op jit(solution)/shard_map/all_to_all | solution.py:460
  52.8 2.0 %shard_map.75 = (bf16[2,2048,512]{2,1,0:T(8,128)(2,1)S(1)}, f32[256,256]{1,0:T(8,128)S(1)}, bf16[256,256]{1,0:T(8,128)(2,1)S(1)}) custom-call(f32[2048,512]{1,0:T(8,128)S(1)} %get-tuple-element.37.own_mass_ref, f32[2048,512]{1,0:T(8,128)S(1)} %get-tuple-element.38.other_mass_ref, f32[2048,512]{1,0:T(8,128)S(1)} %get-tuple-element.39.own_student_ref, ...), custom_call_target="tpu_custom_call" | custom-call | flops 536870912 | tf_op jit(solution)/shard_map/pallas_call | solution.py:557
  54.7 0.1 collective-permute-start.2
  54.8 0.0 copy-start
  54.8 1.7 %shard_map.76._ = bf16[8,16,2560]{2,1,0:T(8,128)(2,1)S(1)} custom-call(bf16[2,2048,512]{2,1,0:T(8,128)(2,1)S(1)} %get-tuple-element.47.gradient_ref, bf16[256,512]{1,0:T(8,128)(2,1)S(1)} %get-tuple-element.48.own_turned_ref, bf16[256,512]{1,0:T(8,128)(2,1)S(1)} %get-tuple-element.49.other_turned_ref, f32[1,2048]{1,0:T(1,128)S(1)} %get-tuple-element.43.inverse_ref, ...), custom_call_target="tpu_custom_call" | custom-call | flops 1073741824 | tf_op jit(solution)/shard_map/pallas_call | solution.py:567
  56.5 0.0 collective-permute-done.2.other_ref
  56.5 0.1 shard_map.77
  56.6 14.3 %all_to_all.29.got_ref = bf16[8,16,2560]{2,1,0:T(8,128)(2,1)S(1)} all-to-all(bf16[8,16,2560]{2,1,0:T(8,128)(2,1)S(1)} %shard_map.77), channel_id=1, replica_groups=mesh['group'=2,'block'=8,'fsdp'=2] {'block'}, dimensions={0} | all-to-all | bytes 1310720 | tf_op jit(solution)/shard_map/all_to_all | solution.py:582
  70.9 0.0 copy-done
  70.9 1.2 %shard_map.78 = (f32[16,16384]{1,0:T(8,128)}, f32[32,256]{1,0:T(8,128)}) custom-call(bf16[8,16,2560]{2,1,0:T(8,128)(2,1)S(1)} %all_to_all.29.got_ref, bf16[32,256]{1,0:T(8,128)(2,1)S(1)} %copy-done), custom_call_target="tpu_custom_call" | custom-call | tf_op jit(solution)/shard_map/pallas_call | solution.py:583
  (1 shorter events, 0.0 us)
Async XLA Ops:
  1.5 6.7 %collective-permute-start = (bf16[48,512]{1,0:T(8,128)(2,1)S(1)}, bf16[48,512]{1,0:T(8,128)(2,1)S(1)}, u32[]{:S(2)}, u32[]{:S(2)}) collective-permute-start(bf16[48,512]{1,0:T(8,128)(2,1)S(1)} %shard_map.68.refs_0_), channel_id=1, source_target_pairs={{0,16},{16,0},{1,17},{17,1},{2,18},{18,2},{3,19},{19,3},{4,20},{20... | collective-permute-start | bytes 147464 | tf_op jit(solution)/shard_map/ppermute | solution.py:473
  21.5 1.9 %collective-permute-start.1 = (bf16[8,64,512]{2,1,0:T(8,128)(2,1)S(1)}, bf16[8,64,512]{2,1,0:T(8,128)(2,1)S(1)}, u32[]{:S(2)}, u32[]{:S(2)}) collective-permute-start(bf16[8,64,512]{2,1,0:T(8,128)(2,1)S(1)} %all_to_all.25.got_ref), channel_id=1, source_target_pairs={{0,1},{1,0},{2,3},{3,2},{4,5},{5,4},{6,7},{7,6},{8,9},{9,8},{10,11... | collective-permute-start | bytes 1572872 | tf_op jit(solution)/shard_map/ppermute | solution.py:457
  54.7 1.8 %collective-permute-start.2 = (bf16[256,256]{1,0:T(8,128)(2,1)S(1)}, bf16[256,256]{1,0:T(8,128)(2,1)S(1)}, u32[]{:S(2)}, u32[]{:S(2)}) collective-permute-start(bf16[256,256]{1,0:T(8,128)(2,1)S(1)} %get-tuple-element.46), channel_id=1, source_target_pairs={{0,1},{1,0},{2,3},{3,2},{4,5},{5,4},{6,7},{7,6},{8,9},{9,8},{10,11... | collective-permute-start | bytes 393224 | tf_op jit(solution)/shard_map/ppermute | solution.py:457
  54.8 16.1 %copy-start = (bf16[32,256]{1,0:T(8,128)(2,1)S(1)}, bf16[32,256]{1,0:T(8,128)(2,1)}, u32[]{:S(2)}) copy-start(bf16[32,256]{1,0:T(8,128)(2,1)} %student_ref.5) | copy-start | bytes 49156
